TPU v7x, 32 devices: a whole 2x2x4 slice. The times are simulated.
32 devices in a mesh: graph: 2 (over x), feat: 16 (over z, y, core).
Axes of the slice: x: 2, y: 2, z: 4, core: 2. Of those that a mesh axis runs over, the one named last changes fastest.
Arguments:
- features: bfloat16 [2048, 512], P('graph', 'feat'), may hold values from -6 to 6
- w_first: bfloat16 [2, 512, 256], P(None, 'feat'), may hold values from -0.25 to 0.25
- w_second: bfloat16 [2, 256, 256], replicated, may hold values from -0.375 to 0.375
- cotangent: bfloat16 [1024, 256], P(('graph', 'feat')), may hold values from -6 to 6
- nbr_first: int32 [1024, 15], P('graph'), may hold values from 0 to 1023
- send_rows: int32 [32, 2, 8], P(('graph', 'feat')), may hold values from -1 to 31, as said below
- nbr_second: int32 [1024, 10], P(('graph', 'feat')), may hold values from 0 to 47, as said below
Outputs:
- layer_out: bfloat16 [1024, 256], P(('graph', 'feat'))
- grad_second: float32 [2, 256, 256], replicated
- grad_first: float32 [2, 512, 256], P(None, 'feat')
Inputs may be any that keep to these rules, and one draw needn't show every extreme that they name: `send_rows`: for each device and partition the used slots come first; a device's own partition gets only -1; every used slot of a device to one partition names a different row; for each feat index some partition other than the last receives all 8 slots used from every other partition. `nbr_second`: each entry below 32 names an owned row; every other entry names a used slot received from another partition.
All inputs are finite; a program needn't handle non-finite values.
Results may differ from a plain program's by a relative error of at most 0.0051.
Values may be sent and summed in bfloat16 or wider, within the bound.
No kernel may reach another device: no remote copies, remote signals or barrier semaphores. Data moves between devices by JAX's collectives and lax.ppermute only.
A program may use at most 64 MiB of HBM per device.

v0:
```python
import jax
import jax.numpy as jnp
from jax import lax
from jax.sharding import PartitionSpec as P

HID = 256
FAN1 = 15
FAN2 = 10
OWN = 32


def silu_grad(value):
    sig = jax.nn.sigmoid(value)
    return sig * (1.0 + value * (1.0 - sig))


def body(features, w_first, w_second, cotangent, nbr_first, send_rows, nbr_second):
    high = lax.Precision.HIGHEST
    targets = nbr_first.shape[0]
    gathered = features[nbr_first].astype(jnp.float32)
    mean_all = (jnp.sum(gathered, axis=1) / FAN1).astype(jnp.bfloat16)
    self_all = features[:targets]
    self_part = self_all
    mean_part = mean_all
    term = jnp.dot(self_part, w_first[0], preferred_element_type=jnp.float32)
    pre_one = lax.psum_scatter(
        term + jnp.dot(mean_part, w_first[1], preferred_element_type=jnp.float32),
        "feat",
        scatter_dimension=0,
        tiled=True,
    )
    hidden = jax.nn.silu(pre_one).astype(jnp.bfloat16)
    slot_rows = send_rows[0]
    valid = (slot_rows >= 0)[..., None]
    picked = hidden[jnp.maximum(slot_rows, 0)]
    outgoing_rows = jnp.where(valid, picked, jnp.zeros_like(picked))
    received = lax.all_to_all(outgoing_rows, "graph", split_axis=0, concat_axis=0, tiled=True)
    ext = jnp.concatenate([hidden, received.reshape(-1, HID)], axis=0)
    width = ext.shape[0]
    counts = jnp.zeros((OWN, width), jnp.float32)
    for k in range(FAN2):
        counts = counts + (nbr_second[:, k, None] == jnp.arange(width)[None, :]).astype(jnp.float32)
    mean_two = (
        jnp.dot(counts.astype(jnp.bfloat16), ext, preferred_element_type=jnp.float32) / FAN2
    ).astype(jnp.bfloat16)
    layer_out = jnp.dot(hidden, w_second[0], preferred_element_type=jnp.float32)
    layer_out = (
        layer_out + jnp.dot(mean_two, w_second[1], preferred_element_type=jnp.float32)
    ).astype(jnp.bfloat16)
    grad_terms = jnp.stack(
        [
            jnp.einsum("rh,ro->ho", hidden, cotangent, preferred_element_type=jnp.float32),
            jnp.einsum("rh,ro->ho", mean_two, cotangent, preferred_element_type=jnp.float32),
        ]
    )
    grad_second = lax.psum(grad_terms, ("graph", "feat"))
    d_self = jnp.einsum("ro,ho->rh", cotangent, w_second[0], preferred_element_type=jnp.float32)
    d_mean = (
        jnp.einsum("ro,ho->rh", cotangent, w_second[1], preferred_element_type=jnp.float32) / FAN2
    )
    d_ext = jnp.dot(counts.T, d_mean, precision=high)
    halo_grad = d_ext[OWN:].reshape(-1, slot_rows.shape[1], HID).astype(jnp.bfloat16)
    returned = lax.all_to_all(halo_grad, "graph", split_axis=0, concat_axis=0, tiled=True)
    onehot = (slot_rows.reshape(-1)[:, None] == jnp.arange(OWN)[None, :]).astype(jnp.bfloat16)
    d_back = jnp.einsum(
        "sr,sh->rh", onehot, returned.reshape(-1, HID), preferred_element_type=jnp.float32
    )
    d_hidden = d_self + d_ext[:OWN] + d_back
    d_pre = (d_hidden * silu_grad(pre_one)).astype(jnp.bfloat16)
    piece = lax.all_gather(d_pre, "feat", axis=0, tiled=True)
    self_part = self_all
    mean_part = mean_all
    first_sum = jnp.einsum("rf,rh->fh", self_part, piece, preferred_element_type=jnp.float32)
    second_sum = jnp.einsum("rf,rh->fh", mean_part, piece, preferred_element_type=jnp.float32)
    local_grad = jnp.stack([first_sum, second_sum])
    grad_first = lax.psum(local_grad, "graph")
    return (layer_out, grad_second, grad_first)


def solution(mesh):
    in_specs = (
        P("graph", "feat"),
        P(None, "feat", None),
        P(),
        P(("graph", "feat"), None),
        P("graph", None),
        P(("graph", "feat"), None, None),
        P(("graph", "feat"), None),
    )
    out_specs = (P(("graph", "feat"), None), P(), P(None, "feat", None))
    return jax.shard_map(body, mesh=mesh, in_specs=in_specs, out_specs=out_specs, check_vma=False)
```

profile of v0, /device:TPU:0, one launch (start us, length us, event | category | flops | bytes accessed | tf_op | source)
XLA Modules:
  0.0 289.5 jit_solution(2405819487066639311)
XLA Ops:
  7.2 0.0 copy-start
  7.2 1.0 slice_bitcast_fusion.9
  8.2 1.1 convolution_multiply_fusion
  9.2 0.4 fusion.26
  9.6 0.6 fusion.23
  10.2 4.2 %all-to-all-start.1 = ((bf16[2,8,256]{2,1,0:T(8,128)(2,1)}), bf16[2,8,256]{2,1,0:T(8,128)(2,1)S(1)}, u32[]{:S(2)}, u32[]{:S(2)}) async-start(bf16[2,8,256]{2,1,0:T(8,128)(2,1)} %fusion.23), calls=%async_computation.2 | async-start | bytes 16384 | tf_op jit(solution)/shard_map/all_to_all | solution.py:63
  14.4 0.8 compare_select_fusion
  15.2 0.1 copy.11
  15.3 0.2 reshape.38
  15.6 1.0 copy.12
  16.6 14.4 %gather_fusion = bf16[7680,32]{1,0:T(8,128)(2,1)S(1)} fusion(bf16[1024,32]{1,0:T(8,128)(2,1)S(1)} %copy.12, s32[8192]{0:T(1024)S(1)} %pad_clamp_fusion), kind=kCustom, calls=%fused_computation | custom fusion | bytes 1013760 | tf_op jit(solution)/shard_map/gather | solution.py:20
  31.0 0.0 copy-start.2
  31.0 0.0 copy-start.3
  31.0 2.1 reshape.56
  33.2 0.2 fusion.14
  33.4 0.0 copy-start.4
  33.4 0.0 copy-start.1
  33.4 3.1 %reduce_sum.9 = f32[512,32]{1,0:T(8,128)S(1)} reduce(f32[512,15,32]{2,1,0:T(8,128)} %reshape.56, f32[]{:T(128)} %constant.9.clone.1), dimensions={1}, to_apply=%region_0.0 | reduce | flops 229376 | bytes 1048580 | tf_op jit(solution)/shard_map/reduce_sum | solution.py:21
  36.6 1.0 convolution_add_fusion
  37.6 0.0 reduce-scatter.2.cloned.1.call-update
  37.6 0.1 reshape.46
  37.7 0.1 convolution_add_fusion.2
  37.9 0.1 eq.205
  38.0 57.8 %reduce-scatter.2.cloned.1.call-done = f32[32,256]{1,0:T(8,128)} async-done(((f32[512,256]{1,0:T(8,128)}), f32[32,256]{1,0:T(8,128)}) %reduce-scatter.2.cloned.1.call-update) | async-done | bytes 32784 | tf_op jit(solution)/shard_map/reduce_scatter | solution.py:26
  95.8 1.0 fusion.3
  96.8 20.1 %all_gather.3 = bf16[512,256]{1,0:T(8,128)(2,1)S(1)} all-gather(bf16[32,256]{1,0:T(8,128)(2,1)S(1)} %fusion.3), channel_id=1, replica_groups=mesh['graph'=2,'feat'=16] {'feat'}, dimensions={0}, use_global_device_ids=true | all-gather | bytes 278528 | tf_op jit(solution)/shard_map/all_gather | solution.py:70
  116.9 0.2 convolution_bitcast_fusion.3
  117.1 0.2 convolution_bitcast_fusion.2
  117.3 0.8 multiply_convert_fusion.3
  118.1 0.2 convolution_bitcast_fusion.1
  118.3 0.6 gather_fusion.1
  118.9 0.7 bitcast_select_fusion
  119.6 3.2 %all-to-all-start = ((bf16[2,8,256]{2,1,0:T(8,128)(2,1)}), bf16[2,8,256]{2,1,0:T(8,128)(2,1)S(1)}, u32[]{:S(2)}, u32[]{:S(2)}) async-start(bf16[2,8,256]{2,1,0:T(8,128)(2,1)} %bitcast_select_fusion), calls=%async_computation.1 | async-start | bytes 16384 | tf_op jit(solution)/shard_map/all_to_all | solution.py:37
  122.8 0.0 all-reduce.5.cloned.1.call-start
  122.8 0.6 pad_maximum_fusion.1
  123.5 0.1 all-reduce.5.cloned.1.call-update
  123.5 0.0 all-reduce.3.cloned.1.call-start
  123.6 3.0 %all-to-all-done = bf16[2,8,256]{2,1,0:T(8,128)(2,1)S(1)} async-done(((bf16[2,8,256]{2,1,0:T(8,128)(2,1)}), bf16[2,8,256]{2,1,0:T(8,128)(2,1)S(1)}, u32[]{:S(2)}, u32[]{:S(2)}) %all-to-all-start) | async-done | bytes 8224 | tf_op jit(solution)/shard_map/all_to_all | solution.py:37
  126.6 0.2 fusion.1
  126.8 0.2 convolution_bitcast_fusion
  127.0 0.8 pad_maximum_fusion
  127.9 0.0 all-reduce.3.cloned.1.call-update
  127.9 0.1 fusion.7
  128.0 0.8 fusion.2
  128.8 16.3 %all-reduce.5.cloned.1.call-done = f32[2,32,256]{2,1,0:T(8,128)} async-done(((f32[2,32,256]{2,1,0:T(8,128)}), f32[2,32,256]{2,1,0:T(8,128)}) %all-reduce.5.cloned.1.call-update) | async-done | bytes 65552 | tf_op jit(solution)/shard_map/psum | solution.py:76
  145.1 134.5 %all-reduce.3.cloned.1.call-done = f32[2,256,256]{2,1,0:T(8,128)} async-done(((f32[2,256,256]{2,1,0:T(8,128)}), f32[2,256,256]{2,1,0:T(8,128)}) %all-reduce.3.cloned.1.call-update) | async-done | bytes 524304 | tf_op jit(solution)/shard_map/psum | solution.py:56
  279.6 1.9 copy.15
  281.5 1.5 copy.16
  (11 shorter events, 0.0 us)
Async XLA Ops:
  7.2 1.0 copy-start
  10.2 27.7 %all-to-all-start.1 = ((bf16[2,8,256]{2,1,0:T(8,128)(2,1)}), bf16[2,8,256]{2,1,0:T(8,128)(2,1)S(1)}, u32[]{:S(2)}, u32[]{:S(2)}) async-start(bf16[2,8,256]{2,1,0:T(8,128)(2,1)} %fusion.23), calls=%async_computation.2 | async-start | bytes 16384 | tf_op jit(solution)/shard_map/all_to_all | solution.py:63
  14.4 81.4 %reduce-scatter.2.cloned.1.call-start = ((), (), s32[]{:S(2)}) async-start(), calls=%async_computation.3 | async-start | bytes 557056 | tf_op jit(solution)/shard_map/reduce_scatter | solution.py:26
  31.0 2.2 copy-start.2
  31.0 2.2 copy-start.3
  33.4 4.2 %copy-start.4 = (s32[1,2,8]{2,1,0:T(2,128)S(1)}, s32[1,2,8]{2,1,0:T(2,128)}, u32[]{:S(2)}) copy-start(s32[1,2,8]{2,1,0:T(2,128)} %param.12) | copy-start | bytes 196
  33.4 4.3 %copy-start.1 = (bf16[2,256,256]{2,1,0:T(8,128)(2,1)S(1)}, bf16[2,256,256]{2,1,0:T(8,128)(2,1)}, u32[]{:S(2)}) copy-start(bf16[2,256,256]{2,1,0:T(8,128)(2,1)} %param.9) | copy-start | bytes 786436
  119.6 7.0 %all-to-all-start = ((bf16[2,8,256]{2,1,0:T(8,128)(2,1)}), bf16[2,8,256]{2,1,0:T(8,128)(2,1)S(1)}, u32[]{:S(2)}, u32[]{:S(2)}) async-start(bf16[2,8,256]{2,1,0:T(8,128)(2,1)} %bitcast_select_fusion), calls=%async_computation.1 | async-start | bytes 16384 | tf_op jit(solution)/shard_map/all_to_all | solution.py:37
  122.8 22.3 %all-reduce.5.cloned.1.call-start = ((), (), s32[]{:S(2)}) async-start(), calls=%async_computation.5 | async-start | bytes 131072 | tf_op jit(solution)/shard_map/psum | solution.py:76
  123.5 156.1 %all-reduce.3.cloned.1.call-start = ((), (), s32[]{:S(2)}) async-start(), calls=%async_computation.4 | async-start | bytes 1048576 | tf_op jit(solution)/shard_map/psum | solution.py:56
Sparse Core Ops, SparseCore 0:
  37.7 58.0 reduce-scatter.1
  126.5 18.5 all-reduce.4
  151.8 127.7 all-reduce.2
where the time goes:
time: 290 us; the launch traced here: 289 us
  waiting for transfers between devices  212 us (73%)
  local copies, waits for them, and re-layouts  23.6 us (8%)
  blocking collectives  20.1 us (7%)
  between operations  13.9 us (5%)
  starting transfers between devices  7.52 us (3%)
  other arithmetic  6.84 us (2%)
  matrix products  5.71 us (2%)
    psum x1, waiting for transfers between devices, body(): grad_second = lax.psum(grad_terms, ('graph', 'feat'))  135 us
    reduce_scatter x1, waiting for transfers between devices, body(): lax.psum_scatter(term + jnp.dot(mean_part, w_first[1], preferred_element_...  57.8 us
    all_gather x1, blocking collectives, body(): piece = lax.all_gather(d_pre, 'feat', axis=0, tiled=True)  20.1 us
    psum x1, waiting for transfers between devices, body(): grad_first = lax.psum(local_grad, 'graph')  16.3 us
    gather x1, local copies, waits for them, and re-layouts, body(): gathered = features[nbr_first].astype(jnp.float32)  14.4 us
  transfers between devices with their start and end apart: 5, of which 4 were waited for; matrix products, arithmetic and copies ran while one was open for 9% of the time, Pallas kernels for 0%

commit v1 on v0

v1 whole, which is shorter than its diff:
```python
import functools

import jax
import jax.numpy as jnp
from jax import lax
from jax.experimental import pallas as pl
from jax.experimental.pallas import tpu as pltpu
from jax.sharding import PartitionSpec as P

HID = 256
FAN1 = 15
FAN2 = 10
OWN = 32
HALO = 8
LANES = 128
INTS = 16
F32 = jnp.float32
BF16 = jnp.bfloat16
AXES = ("graph", "feat")
PLANE = ((0, 0), (1, 0), (0, 1), (1, 1))


def silu_grad(value):
    sig = jax.nn.sigmoid(value)
    return sig * (1.0 + value * (1.0 - sig))


def dot(a, b, contract):
    return lax.dot_general(a, b, (contract, ((), ())), preferred_element_type=F32)


def write_pack(sends, cot, near, pack):
    my_z = lax.axis_index("feat") // 4
    for side in range(2):
        pack[side * OWN : (side + 1) * OWN, :] = cot[:, side * LANES : (side + 1) * LANES]
    lane = lax.broadcasted_iota(jnp.int32, (INTS, LANES), 1)
    row = lax.broadcasted_iota(jnp.int32, (INTS, LANES), 0)
    lists = jnp.concatenate([near[...], jnp.zeros((INTS - FAN2, OWN), jnp.int32)], axis=0)
    ints = jnp.where(lane // OWN == my_z, jnp.concatenate([lists] * (LANES // OWN), axis=1), 0)
    for g in range(2):
        for s in range(HALO):
            here = (row == FAN2) & (lane == my_z * OWN + g * HALO + s)
            ints = jnp.where(here, sends[0, g, s], ints)
    pack[2 * OWN : 2 * OWN + INTS, :] = ints.astype(F32).astype(BF16)


def first_kernel(
    feat_hbm, nbr_hbm, w_hbm, cot_hbm, near_hbm, sends_hbm, pack, x_t, kept, sent,
    feat_t, nbr_t, w_first, cot, near, sends, share, sems,
):
    pairs = ((nbr_hbm, nbr_t), (feat_hbm, feat_t), (w_hbm, w_first), (cot_hbm, cot), (near_hbm, near), (sends_hbm, sends))
    copies = [pltpu.make_async_copy(src, dst, sems.at[i]) for i, (src, dst) in enumerate(pairs)]
    for copy in copies:
        copy.start()
    copies[0].wait()
    copies[1].wait()
    sources = feat_t.shape[1]
    row = lax.broadcasted_iota(jnp.int32, (LANES, LANES), 0)
    for t in range(x_t.shape[0]):
        cols = slice(t * LANES, (t + 1) * LANES)
        low = nbr_t[:, cols] & (LANES - 1)
        unit = jnp.left_shift(1, 4 * jnp.right_shift(nbr_t[:, cols], 7))
        packed = jnp.zeros((LANES, LANES), jnp.int32)
        for k in range(FAN1):
            packed = packed + jnp.where(row == low[k : k + 1, :], unit[k : k + 1, :], 0)
        parts = [jnp.right_shift(packed, 4 * b) & 15 for b in range(sources // LANES)]
        counts = jnp.concatenate([part.astype(F32).astype(BF16) for part in parts], axis=0)
        mean = (dot(feat_t[...], counts, ((1,), (0,))) / FAN1).astype(BF16)
        chunk = jnp.concatenate([feat_t[:, cols], mean], axis=0)
        x_t[t] = chunk
        sent[2 * x_t.shape[0] + t] = chunk
        if t == 0:
            copies[2].wait()
        share[cols, :] = dot(chunk, w_first[...], ((0,), (0,)))
    line = x_t.shape[0]
    my_feat = lax.axis_index("feat")
    for c, out in enumerate((kept, sent)):
        for y in range(2):
            for z in range(line):
                owner = z * 4 + ((my_feat % 4) ^ (2 * y + c))
                block = share[pl.ds(pl.multiple_of(owner * OWN, OWN), OWN), :].astype(out.dtype)
                for side in range(2):
                    out[y * line + z, side * OWN : (side + 1) * OWN, :] = block[:, side * LANES : (side + 1) * LANES]
    for copy in copies[3:]:
        copy.wait()
    write_pack(sends, cot, near, pack)


def sum_core_kernel(mine, received, kept, sent):
    line = kept.shape[0]
    kept[...] = mine[0:line] + received[0:line].astype(F32)
    sent[...] = (mine[line : 2 * line] + received[line : 2 * line].astype(F32)).astype(BF16)


def sum_plane_kernel(pack, mine, received, message):
    total = (mine[...] + received[...].astype(F32)).astype(BF16)
    rows = total.shape[0] * total.shape[1]
    message[0:rows, :] = total.reshape(rows, LANES)
    message[rows:, :] = pack[...]


def sum_line_kernel(after, *refs):
    parts, (exact, message) = refs[:-2], refs[-2:]
    my_z = lax.axis_index("feat") // 4
    line, width = exact.shape[0], exact.shape[1]
    rows = line * width
    sums = [part[0:rows, :].astype(F32) for part in parts]
    while len(sums) > 1:
        sums = [a + b for a, b in zip(sums[::2], sums[1::2])]
    total = sums[0].reshape(exact.shape)
    exact[...] = total
    total = total.astype(BF16)
    for z, part in enumerate(parts):
        message[2 * z * width : (2 * z + 1) * width, :] = total[z]
        at = pl.multiple_of((2 * (my_z ^ z) + 1) * width, width)
        message[pl.ds(at, width), :] = part[rows : rows + width, :]
    lists = [part[rows + width :, :].astype(F32) for part in parts]
    message[2 * rows :, :] = functools.reduce(lambda a, b: a + b, lists).astype(BF16)


def back_kernel(n_feat, plane_0, plane_1, plane_2, plane_3, w_second, cot_all, near_cot, d_hidden, own_counts, lists, spread, turn):
    line = n_feat // 4
    width = 2 * OWN
    my_graph = lax.axis_index("graph")
    my_z = lax.axis_index("feat") // 4
    my_y = lax.axis_index("feat") // 2 % 2
    for (x, y), message in zip(PLANE, (plane_0, plane_1, plane_2, plane_3)):
        at = (my_graph ^ x) * 2 + (my_y ^ y)
        lists[at] = message[2 * line * width :, :]
        for z in range(line):
            span = pl.ds(pl.multiple_of(at * LANES + z * OWN, OWN), OWN)
            for side in range(2):
                top = (2 * z + 1) * width + side * OWN
                cot_all[span, side * LANES : (side + 1) * LANES] = message[top : top + OWN, :]

    ints = lists[...].reshape(4 * INTS, LANES)
    source = lax.broadcasted_iota(jnp.int32, (LANES, LANES), 0)
    start = lax.broadcasted_iota(jnp.int32, (LANES, LANES), 1) // OWN * OWN
    pick = jnp.concatenate([jnp.where(source == start + s, 1.0, 0.0).astype(BF16) for s in range(2 * HALO)], axis=1)
    sent = dot(ints, pick, ((1,), (0,)))

    z_of = lax.broadcasted_iota(jnp.int32, (width, LANES), 1) // OWN
    slot_ix = lax.broadcasted_iota(jnp.int32, (width, LANES), 0).astype(F32)
    for y in range(2):
        total = jnp.zeros((line * width, HID), F32)
        for g in range(2):
            at = g * 2 + y
            entries = ints[at * INTS : (at + 1) * INTS, :].astype(F32)
            place_of = entries + float(g * OWN)
            for p in range(2):
                for s in range(HALO):
                    row = (p * 2 + y) * INTS + FAN2
                    there = sent[row : row + 1, (g * HALO + s) * LANES : (g * HALO + s + 1) * LANES] + p * OWN
                    place_of = jnp.where(entries == float(OWN + p * HALO + s), there, place_of)
            counts = jnp.zeros((width, LANES), F32)
            for k in range(FAN2):
                counts = counts + jnp.where(slot_ix == place_of[k : k + 1, :], 1.0, 0.0)
            spread[at] = counts
            block = jnp.concatenate([jnp.where(z_of == z, counts, 0.0) for z in range(line)], axis=0).astype(BF16)
            total = total + dot(block, cot_all[at * LANES : (at + 1) * LANES, :], ((1,), (0,)))
        total = (total / FAN2).astype(BF16)
        for z in range(line):
            for p in range(2):
                at = (p * 2 + y) * LANES + z * OWN
                near_cot[at : at + OWN, :] = total[z * width + p * OWN : z * width + (p + 1) * OWN, :]

    turn[...] = spread[pl.ds(my_graph * 2 + my_y, 1)][0].T
    own_counts[...] = turn[pl.ds(pl.multiple_of(my_z * OWN, OWN), OWN), :]

    part = dot(cot_all[...], w_second[0], ((1,), (1,)))
    d_hidden[...] = part + dot(near_cot[...], w_second[1], ((1,), (1,)))


def last_kernel(
    n_feat, plane_0, plane_1, plane_2, plane_3, exact, cot, near_cot, d_hidden, own_counts, x_mine, x_core, x_peer, x_last, w_second,
    layer_out, swapped, kept, hidden, d_pre, slices, ext,
):
    my_graph = lax.axis_index("graph")
    my_feat = lax.axis_index("feat")
    rows = n_feat * OWN
    half = rows // 2
    line = n_feat // 4
    d_pre[...] = jnp.zeros_like(d_pre)
    my_y = my_feat // 2 % 2
    for (x, y), message in zip(PLANE, (plane_0, plane_1, plane_2, plane_3)):
        graph = my_graph ^ x
        for z in range(line):
            span = pl.ds(pl.multiple_of((graph * 2 + (my_y ^ y)) * LANES + z * OWN, OWN), OWN)
            top = 4 * z * OWN
            value = jnp.concatenate([message[top : top + OWN, :], message[top + OWN : top + 2 * OWN, :]], axis=1).astype(F32)
            sig = 0.5 + 0.5 * jnp.tanh(0.5 * value)
            hidden[span, :] = (value * sig).astype(BF16)
            slope = sig * (1.0 + value * (1.0 - sig))
            target = pl.ds(pl.multiple_of(graph * rows + (z * 4 + (my_feat % 4 ^ 2 * y)) * OWN, OWN), OWN)
            d_pre[target, :] = (d_hidden[span, :] * slope).astype(BF16)

    swapped[0:HID, :] = dot(hidden[...], cot[...], ((0,), (0,))).astype(BF16)
    swapped[HID : 2 * HID, :] = dot(hidden[...], near_cot[...], ((0,), (0,))).astype(BF16)

    for z in range(line):
        cols = slice(z * LANES, (z + 1) * LANES)
        slices[0, 0 : 2 * OWN, cols] = x_mine[z]
        slices[0, 2 * OWN : 4 * OWN, cols] = x_core[2 * line + z]
        slices[1, 0 : 2 * OWN, cols] = x_peer[z]
        slices[1, 2 * OWN : 4 * OWN, cols] = x_last[z]
    mine = d_pre[pl.ds(pl.multiple_of(my_graph * rows, rows), rows), :]
    peer = d_pre[pl.ds(pl.multiple_of((1 - my_graph) * rows, rows), rows), :]
    first = dot(slices[0], mine, ((1,), (0,))) + dot(slices[1], peer, ((1,), (0,)))
    kept[...] = first[0 : 2 * OWN, :]
    swapped[2 * HID : 2 * HID + 2 * OWN, :] = first[2 * OWN : 4 * OWN, :].astype(BF16)

    value = exact[pl.ds(my_feat // 4, 1)][0]
    value = jnp.concatenate([value[0:OWN, :], value[OWN : 2 * OWN, :]], axis=1)
    hidden_own = (value * (0.5 + 0.5 * jnp.tanh(0.5 * value))).astype(BF16)
    for p in range(2):
        at = (p * 2 + my_y) * LANES + (my_feat // 4) * OWN
        ext[p * OWN : (p + 1) * OWN, :] = hidden[pl.ds(pl.multiple_of(at, OWN), OWN), :]
    ext[pl.ds(pl.multiple_of(my_graph * OWN, OWN), OWN), :] = hidden_own
    mean = (dot(own_counts[...].astype(BF16), ext[...], ((1,), (0,))) / FAN2).astype(BF16)
    out = dot(hidden_own, w_second[0], ((1,), (0,))) + dot(mean, w_second[1], ((1,), (0,)))
    layer_out[...] = out.astype(BF16)


def add_kernel(mine, theirs, kept, grad_second, grad_first):
    for w in range(2):
        span = slice(w * HID, (w + 1) * HID)
        grad_second[w] = mine[span, :].astype(F32) + theirs[span, :].astype(F32)
    grad_first[...] = kept[...] + theirs[2 * HID : 2 * HID + 2 * OWN, :].astype(F32)


VMEM = pl.BlockSpec(memory_space=pltpu.VMEM)
ANY = pl.BlockSpec(memory_space=pl.ANY)
SMEM = pl.BlockSpec(memory_space=pltpu.SMEM)
LIMIT = 40 * 1024 * 1024


def call(kernel, outs, ins, scratch=(), name=None, aliases=None):
    return pl.pallas_call(
        kernel,
        out_shape=[jax.ShapeDtypeStruct(shape, dtype) for shape, dtype in outs],
        in_specs=ins,
        out_specs=[VMEM] * len(outs),
        scratch_shapes=list(scratch),
        input_output_aliases=aliases or {},
        compiler_params=pltpu.CompilerParams(vmem_limit_bytes=LIMIT),
        name=name,
    )


def swap(n_feat, value, relative):
    return lax.ppermute(value, AXES, [(d, d ^ relative) for d in range(2 * n_feat)])


def pair_body(n_feat, features, w_first, w_second, cotangent, nbr_first, send_rows, nbr_second):
    devices = 2 * n_feat
    rows = n_feat * OWN
    width = 2 * OWN
    line = n_feat // 4
    from_hbm = [features.T, nbr_first.T, w_first.reshape(width, HID), cotangent, nbr_second.T, send_rows]
    block = (line, width, LANES)
    pack, x_mine, kept, sent = call(
        first_kernel,
        [((width + INTS, LANES), BF16), (block, BF16), ((2 * line, width, LANES), F32), ((3 * line, width, LANES), BF16)],
        [ANY] * 6,
        [pltpu.VMEM(x.shape, x.dtype) for x in from_hbm[:-1]]
        + [pltpu.SMEM(send_rows.shape, jnp.int32), pltpu.VMEM((rows, HID), F32), pltpu.SemaphoreType.DMA((6,))],
        name="first",
    )(*[pltpu.with_memory_space_constraint(x, pltpu.HBM) for x in from_hbm])
    x_core = swap(n_feat, sent, 1)
    kept, sent = call(sum_core_kernel, [(block, F32), (block, BF16)], [VMEM] * 2, name="sum_core")(kept, x_core)
    x_peer = swap(n_feat, x_mine, n_feat)
    (message,) = call(
        sum_plane_kernel,
        [((line * width + width + INTS, LANES), BF16)],
        [VMEM] * 3,
        name="sum_plane",
    )(pack, kept, swap(n_feat, sent, 2))
    x_last = swap(n_feat, x_peer, 1)
    exact, message = call(
        sum_line_kernel,
        [(block, F32), ((2 * line * width + INTS, LANES), BF16)],
        [ANY] + [VMEM] * line,
        name="sum_line",
    )(x_peer, message, *[swap(n_feat, message, 4 * z) for z in range(1, line)])
    plane = [swap(n_feat, message, r) for r in (n_feat + 2, 2, n_feat)]
    plane = [message, *plane[::-1]]

    half = (devices // 2) * OWN
    cot, near_cot, d_hidden, own_counts = call(
        functools.partial(back_kernel, n_feat),
        [((half, HID), BF16), ((half, HID), BF16), ((half, HID), F32), ((OWN, width), F32)],
        [VMEM] * 5,
        [
            pltpu.VMEM((4, INTS, LANES), BF16),
            pltpu.VMEM((4, width, LANES), F32),
            pltpu.VMEM((LANES, width), F32),
        ],
        name="back",
    )(*plane, w_second)

    layer_out, swapped, kept = call(
        functools.partial(last_kernel, n_feat),
        [((OWN, HID), BF16), ((2 * HID + width, HID), BF16), ((width, HID), F32)],
        [VMEM] * 14,
        [
            pltpu.VMEM((half, HID), BF16),
            pltpu.VMEM((2 * half, HID), BF16),
            pltpu.VMEM((2, 2 * width, rows), BF16),
            pltpu.VMEM((width, HID), BF16),
        ],
        name="last",
    )(*plane, exact, cot, near_cot, d_hidden, own_counts, x_mine, x_core, x_peer, x_last, w_second)
    grad_second, grad_first = call(
        add_kernel,
        [((2, HID, HID), F32), ((width, HID), F32)],
        [VMEM] * 3,
        name="add",
    )(swapped, swap(n_feat, swapped, 1), kept)
    return (layer_out, grad_second, grad_first.reshape(2, OWN, HID))


def body(features, w_first, w_second, cotangent, nbr_first, send_rows, nbr_second):
    high = lax.Precision.HIGHEST
    targets = nbr_first.shape[0]
    gathered = features[nbr_first].astype(F32)
    mean_all = (jnp.sum(gathered, axis=1) / FAN1).astype(BF16)
    self_all = features[:targets]
    term = jnp.dot(self_all, w_first[0], preferred_element_type=F32)
    pre_one = lax.psum_scatter(
        term + jnp.dot(mean_all, w_first[1], preferred_element_type=F32),
        "feat",
        scatter_dimension=0,
        tiled=True,
    )
    hidden = jax.nn.silu(pre_one).astype(BF16)
    slot_rows = send_rows[0]
    valid = (slot_rows >= 0)[..., None]
    picked = hidden[jnp.maximum(slot_rows, 0)]
    outgoing_rows = jnp.where(valid, picked, jnp.zeros_like(picked))
    received = lax.all_to_all(outgoing_rows, "graph", split_axis=0, concat_axis=0, tiled=True)
    ext = jnp.concatenate([hidden, received.reshape(-1, HID)], axis=0)
    width = ext.shape[0]
    counts = jnp.zeros((OWN, width), F32)
    for k in range(FAN2):
        counts = counts + (nbr_second[:, k, None] == jnp.arange(width)[None, :]).astype(F32)
    mean_two = (jnp.dot(counts.astype(BF16), ext, preferred_element_type=F32) / FAN2).astype(BF16)
    layer_out = jnp.dot(hidden, w_second[0], preferred_element_type=F32)
    layer_out = (layer_out + jnp.dot(mean_two, w_second[1], preferred_element_type=F32)).astype(BF16)
    grad_terms = jnp.stack(
        [
            jnp.einsum("rh,ro->ho", hidden, cotangent, preferred_element_type=F32),
            jnp.einsum("rh,ro->ho", mean_two, cotangent, preferred_element_type=F32),
        ]
    )
    grad_second = lax.psum(grad_terms, AXES)
    d_self = jnp.einsum("ro,ho->rh", cotangent, w_second[0], preferred_element_type=F32)
    d_mean = jnp.einsum("ro,ho->rh", cotangent, w_second[1], preferred_element_type=F32) / FAN2
    d_ext = jnp.dot(counts.T, d_mean, precision=high)
    halo_grad = d_ext[OWN:].reshape(-1, slot_rows.shape[1], HID).astype(BF16)
    returned = lax.all_to_all(halo_grad, "graph", split_axis=0, concat_axis=0, tiled=True)
    onehot = (slot_rows.reshape(-1)[:, None] == jnp.arange(OWN)[None, :]).astype(BF16)
    d_back = jnp.einsum("sr,sh->rh", onehot, returned.reshape(-1, HID), preferred_element_type=F32)
    d_hidden = d_self + d_ext[:OWN] + d_back
    d_pre = (d_hidden * silu_grad(pre_one)).astype(BF16)
    piece = lax.all_gather(d_pre, "feat", axis=0, tiled=True)
    first_sum = jnp.einsum("rf,rh->fh", self_all, piece, preferred_element_type=F32)
    second_sum = jnp.einsum("rf,rh->fh", mean_all, piece, preferred_element_type=F32)
    grad_first = lax.psum(jnp.stack([first_sum, second_sum]), "graph")
    return (layer_out, grad_second, grad_first)


def solution(mesh):
    n_graph = mesh.shape["graph"]
    n_feat = mesh.shape["feat"]
    in_specs = (
        P("graph", "feat"),
        P(None, "feat", None),
        P(),
        P(AXES, None),
        P("graph", None),
        P(AXES, None, None),
        P(AXES, None),
    )
    out_specs = (P(AXES, None), P(), P(None, "feat", None))
    two = n_graph == 2 and n_feat == 16
    chosen = functools.partial(pair_body, n_feat) if two else body
    return jax.shard_map(chosen, mesh=mesh, in_specs=in_specs, out_specs=out_specs, check_vma=False)
```

time: 290 us -> 34.4 us (0.12)
  waiting for transfers between devices: 212 us -> 14.6 us
  local copies, waits for them, and re-layouts: 23.6 us -> 0.01 us
  blocking collectives: 20.1 us -> 0 us
  between operations: 13.9 us -> 0.68 us
  other arithmetic: 6.84 us -> 0 us
  starting transfers between devices: 7.52 us -> 13.3 us
  matrix products: 5.71 us -> 0 us
  Pallas kernels: 0 us -> 5.62 us
    psum x2 -> x0, waiting for transfers between devices: 151 us -> none  [the longest x1 135 us: body(): grad_second = lax.psum(grad_terms, ('graph', 'feat'))]
    reduce_scatter x1 -> x0, waiting for transfers between devices: 57.8 us -> none  [body(): lax.psum_scatter(term + jnp.dot(mean_part, w_first[1], preferred_element_...]
    all_gather x1 -> x0, blocking collectives: 20.1 us -> none  [body(): piece = lax.all_gather(d_pre, 'feat', axis=0, tiled=True)]
    gather x2 -> x0, local copies, waits for them, and re-layouts: 15 us -> none  [the longest x1 14.4 us: body(): gathered = features[nbr_first].astype(jnp.float32)]
    ppermute x0 -> x11, waiting for transfers between devices: none -> 14.6 us  [swap(): lax.ppermute(value, AXES, [(d, d ^ relative) for d in range(2 * n_feat)])]
    ppermute x0 -> x11, starting transfers between devices: none -> 13.3 us  [swap(): lax.ppermute(value, AXES, [(d, d ^ relative) for d in range(2 * n_feat)])]
    all_to_all x2 -> x0, starting transfers between devices: 7.43 us -> none  [the longest x1 4.21 us: body(): lax.all_to_all(halo_grad, 'graph', split_axis=0, concat_axis=0, tiled=True)]
    dot_general x13 -> x0, matrix products: 5.71 us -> none  [the longest x1 1.06 us: body(): jnp.einsum('ro,ho->rh', cotangent, w_second[1], preferred_element_type=jn...]
  transfers between devices with their start and end apart: 5 -> 11, of which waited for: 4 -> 8; matrix products, arithmetic and copies ran while one was open for 9% -> 0% of each run, Pallas kernels for 0% -> 3%
where the time goes in v1:
time: 34.4 us; the launch traced here: 34.2 us
  waiting for transfers between devices  14.6 us (42%)
  starting transfers between devices  13.3 us (39%)
  Pallas kernels  5.62 us (16%)
  between operations  0.68 us (2%)
    ppermute x11, waiting for transfers between devices, swap(): lax.ppermute(value, AXES, [(d, d ^ relative) for d in range(2 * n_feat)])  14.6 us
    ppermute x11, starting transfers between devices, swap(): lax.ppermute(value, AXES, [(d, d ^ relative) for d in range(2 * n_feat)])  13.3 us
    pallas_call x1, Pallas kernels, pair_body(): call(first_kernel, [((width + INTS, LANES), BF16), (block, BF16), ((2 * l...  2.41 us
    pallas_call x1, Pallas kernels, pair_body(): call(functools.partial(last_kernel, n_feat), [((OWN, HID), BF16), ((2 * H...  1.37 us
    pallas_call x1, Pallas kernels, pair_body(): call(functools.partial(back_kernel, n_feat), [((half, HID), BF16), ((half...  0.89 us
    pallas_call x1, Pallas kernels, pair_body(): call(add_kernel, [((2, HID, HID), F32), ((width, HID), F32)], [VMEM] * 3,...  0.86 us
  transfers between devices with their start and end apart: 11, of which 8 were waited for; matrix products, arithmetic and copies ran while one was open for 0% of the time, Pallas kernels for 3%

profile of v1, /device:TPU:0, one launch (start us, length us, event | category | flops | bytes accessed | tf_op | source)
XLA Modules:
  0.0 34.2 jit_solution(1772166700179368322)
XLA Ops:
  0.6 2.4 %first.1 = (bf16[80,128]{1,0:T(8,128)(2,1)S(1)}, bf16[4,64,128]{2,1,0:T(8,128)(2,1)S(1)}, f32[8,64,128]{2,1,0:T(8,128)S(1)}, bf16[12,64,128]{2,1,0:T(8,128)(2,1)S(1)}) custom-call(bf16[32,1024]{1,0:T(8,128)(2,1)} %bitcast.5, s32[15,512]{1,0:T(8,128)} %bitcast.6, bf16[64,256]{1,0:T(8,128)(2,1)} %bitcast.7, bf16[32,256]{1,0:T(8,128)(2,1)} %cot_hbm.1, ...), custom_call_target="tpu_custom_call" | custom-call | tf_op jit(solution)/shard_map/first/pallas_call | solution.py:261
  3.0 0.5 %collective-permute-start.1 = (bf16[12,64,128]{2,1,0:T(8,128)(2,1)S(1)}, bf16[12,64,128]{2,1,0:T(8,128)(2,1)S(1)}, u32[]{:S(2)}, u32[]{:S(2)}) collective-permute-start(bf16[12,64,128]{2,1,0:T(8,128)(2,1)S(1)} %get-tuple-element.23), channel_id=1, source_target_pairs={{0,1},{1,0},{2,3},{3,2},{4,5},{5,4},{6,7},{7,6},{8,9},{9,8},{10,11... | collective-permute-start | bytes 589832 | tf_op jit(solution)/shard_map/ppermute | solution.py:251
  3.6 1.1 %collective-permute-done.1.received.x_core = bf16[12,64,128]{2,1,0:T(8,128)(2,1)S(1)} collective-permute-done((bf16[12,64,128]{2,1,0:T(8,128)(2,1)S(1)}, bf16[12,64,128]{2,1,0:T(8,128)(2,1)S(1)}, u32[]{:S(2)}, u32[]{:S(2)}) %collective-permute-start.1) | collective-permute-done | bytes 196640 | tf_op jit(solution)/shard_map/ppermute | solution.py:251
  4.7 3.0 %collective-permute-start.2 = (bf16[4,64,128]{2,1,0:T(8,128)(2,1)S(1)}, bf16[4,64,128]{2,1,0:T(8,128)(2,1)S(1)}, u32[]{:S(2)}, u32[]{:S(2)}) collective-permute-start(bf16[4,64,128]{2,1,0:T(8,128)(2,1)S(1)} %get-tuple-element.25), channel_id=1, source_target_pairs={{0,2},{1,3},{2,0},{3,1},{4,6},{5,7},{6,4},{7,5},{8,10},{9,11},{10,... | collective-permute-start | bytes 196616 | tf_op jit(solution)/shard_map/ppermute | solution.py:251
  7.6 2.4 %collective-permute-done.2.received = bf16[4,64,128]{2,1,0:T(8,128)(2,1)S(1)} collective-permute-done((bf16[4,64,128]{2,1,0:T(8,128)(2,1)S(1)}, bf16[4,64,128]{2,1,0:T(8,128)(2,1)S(1)}, u32[]{:S(2)}, u32[]{:S(2)}) %collective-permute-start.2) | collective-permute-done | bytes 65568 | tf_op jit(solution)/shard_map/ppermute | solution.py:251
  10.0 0.0 copy-start
  10.1 4.0 %collective-permute-start.5 = (bf16[336,128]{1,0:T(8,128)(2,1)S(1)}, bf16[336,128]{1,0:T(8,128)(2,1)S(1)}, u32[]{:S(2)}, u32[]{:S(2)}) collective-permute-start(bf16[336,128]{1,0:T(8,128)(2,1)S(1)} %sum_plane.1.refs_0_), channel_id=1, source_target_pairs={{0,12},{1,13},{2,14},{3,15},{4,8},{5,9},{6,10},{7,11},{8,4},{9,5},... | collective-permute-start | bytes 258056 | tf_op jit(solution)/shard_map/ppermute | solution.py:251
  14.1 0.0 collective-permute-start.4
  14.1 0.6 %collective-permute-start.3 = (bf16[336,128]{1,0:T(8,128)(2,1)S(1)}, bf16[336,128]{1,0:T(8,128)(2,1)S(1)}, u32[]{:S(2)}, u32[]{:S(2)}) collective-permute-start(bf16[336,128]{1,0:T(8,128)(2,1)S(1)} %sum_plane.1.refs_0_), channel_id=1, source_target_pairs={{0,4},{1,5},{2,6},{3,7},{4,0},{5,1},{6,2},{7,3},{8,12},{9,13},{10,... | collective-permute-start | bytes 258056 | tf_op jit(solution)/shard_map/ppermute | solution.py:251
  14.7 1.6 %collective-permute-start = (bf16[4,64,128]{2,1,0:T(8,128)(2,1)S(1)}, bf16[4,64,128]{2,1,0:T(8,128)(2,1)S(1)}, u32[]{:S(2)}, u32[]{:S(2)}) collective-permute-start(bf16[4,64,128]{2,1,0:T(8,128)(2,1)S(1)} %get-tuple-element.20.x_mine), channel_id=1, source_target_pairs={{0,16},{1,17},{2,18},{3,19},{4,20},{5,21},{6,22},{7,23},{8,24},{9,... | collective-permute-start | bytes 196616 | tf_op jit(solution)/shard_map/ppermute | solution.py:251
  16.3 2.6 %collective-permute-done.after.x_peer = bf16[4,64,128]{2,1,0:T(8,128)(2,1)S(1)} collective-permute-done((bf16[4,64,128]{2,1,0:T(8,128)(2,1)S(1)}, bf16[4,64,128]{2,1,0:T(8,128)(2,1)S(1)}, u32[]{:S(2)}, u32[]{:S(2)}) %collective-permute-start) | collective-permute-done | bytes 65568 | tf_op jit(solution)/shard_map/ppermute | solution.py:251
  19.0 0.0 collective-permute-done.5.refs_3_
  19.0 1.6 %collective-permute-done.4.refs_2_ = bf16[336,128]{1,0:T(8,128)(2,1)S(1)} collective-permute-done((bf16[336,128]{1,0:T(8,128)(2,1)S(1)}, bf16[336,128]{1,0:T(8,128)(2,1)S(1)}, u32[]{:S(2)}, u32[]{:S(2)}) %collective-permute-start.4) | collective-permute-done | bytes 86048 | tf_op jit(solution)/shard_map/ppermute | solution.py:251
  20.6 0.0 collective-permute-done.3.refs_1_
  20.6 2.5 %collective-permute-start.8 = (bf16[528,128]{1,0:T(8,128)(2,1)S(1)}, bf16[528,128]{1,0:T(8,128)(2,1)S(1)}, u32[]{:S(2)}, u32[]{:S(2)}) collective-permute-start(bf16[528,128]{1,0:T(8,128)(2,1)S(1)} %get-tuple-element.26.plane_0), channel_id=1, source_target_pairs={{0,18},{1,19},{2,16},{3,17},{4,22},{5,23},{6,20},{7,21},{8,26},{9,... | collective-permute-start | bytes 405512 | tf_op jit(solution)/shard_map/ppermute | solution.py:251
  23.1 0.5 %collective-permute-start.7 = (bf16[528,128]{1,0:T(8,128)(2,1)S(1)}, bf16[528,128]{1,0:T(8,128)(2,1)S(1)}, u32[]{:S(2)}, u32[]{:S(2)}) collective-permute-start(bf16[528,128]{1,0:T(8,128)(2,1)S(1)} %get-tuple-element.26.plane_0), channel_id=1, source_target_pairs={{0,2},{1,3},{2,0},{3,1},{4,6},{5,7},{6,4},{7,5},{8,10},{9,11},{10,... | collective-permute-start | bytes 405512 | tf_op jit(solution)/shard_map/ppermute | solution.py:251
  23.6 0.5 %collective-permute-start.6 = (bf16[528,128]{1,0:T(8,128)(2,1)S(1)}, bf16[528,128]{1,0:T(8,128)(2,1)S(1)}, u32[]{:S(2)}, u32[]{:S(2)}) collective-permute-start(bf16[528,128]{1,0:T(8,128)(2,1)S(1)} %get-tuple-element.26.plane_0), channel_id=1, source_target_pairs={{0,16},{1,17},{2,18},{3,19},{4,20},{5,21},{6,22},{7,23},{8,24},{9,... | collective-permute-start | bytes 405512 | tf_op jit(solution)/shard_map/ppermute | solution.py:251
  24.2 0.0 collective-permute-start.9
  24.2 3.0 %collective-permute-done.8.plane_3 = bf16[528,128]{1,0:T(8,128)(2,1)S(1)} collective-permute-done((bf16[528,128]{1,0:T(8,128)(2,1)S(1)}, bf16[528,128]{1,0:T(8,128)(2,1)S(1)}, u32[]{:S(2)}, u32[]{:S(2)}) %collective-permute-start.8) | collective-permute-done | bytes 135200 | tf_op jit(solution)/shard_map/ppermute | solution.py:251
  27.1 2.3 %collective-permute-done.7.plane_2 = bf16[528,128]{1,0:T(8,128)(2,1)S(1)} collective-permute-done((bf16[528,128]{1,0:T(8,128)(2,1)S(1)}, bf16[528,128]{1,0:T(8,128)(2,1)S(1)}, u32[]{:S(2)}, u32[]{:S(2)}) %collective-permute-start.7) | collective-permute-done | bytes 135200 | tf_op jit(solution)/shard_map/ppermute | solution.py:251
  29.4 0.1 collective-permute-done.6.plane_1
  29.5 0.0 copy-done
  29.5 0.9 %back.1 = (bf16[512,256]{1,0:T(8,128)(2,1)S(1)}, bf16[512,256]{1,0:T(8,128)(2,1)S(1)}, f32[512,256]{1,0:T(8,128)S(1)}, f32[32,64]{1,0:T(8,128)S(1)}) custom-call(bf16[528,128]{1,0:T(8,128)(2,1)S(1)} %get-tuple-element.26.plane_0, bf16[528,128]{1,0:T(8,128)(2,1)S(1)} %collective-permute-done.6.plane_1, bf16[528,128]{1,0:T(8,128)(2,1)S(1)} %collective-permute-done.7.plane_2, ...), custom_call_target="tpu_custom_call" | custom-call | tf_op jit(solution)/shard_map/back/pallas_call | solution.py:289
  30.4 0.0 collective-permute-done.9.x_last
  30.4 1.4 %last.1 = (bf16[32,256]{1,0:T(8,128)(2,1)}, bf16[576,256]{1,0:T(8,128)(2,1)S(1)}, f32[64,256]{1,0:T(8,128)S(1)}) custom-call(bf16[528,128]{1,0:T(8,128)(2,1)S(1)} %get-tuple-element.26.plane_0, bf16[528,128]{1,0:T(8,128)(2,1)S(1)} %collective-permute-done.6.plane_1, bf16[528,128]{1,0:T(8,128)(2,1)S(1)} %collective-permute-done.7.plane_2, ...), custom_call_target="tpu_custom_call" | custom-call | tf_op jit(solution)/shard_map/last/pallas_call | solution.py:301
  31.8 0.0 collective-permute-start.10
  31.8 1.6 %collective-permute-done.10.theirs = bf16[576,256]{1,0:T(8,128)(2,1)S(1)} collective-permute-done((bf16[576,256]{1,0:T(8,128)(2,1)S(1)}, bf16[576,256]{1,0:T(8,128)(2,1)S(1)}, u32[]{:S(2)}, u32[]{:S(2)}) %collective-permute-start.10) | collective-permute-done | bytes 294944 | tf_op jit(solution)/shard_map/ppermute | solution.py:251
  33.4 0.9 %add.1 = (f32[2,256,256]{2,1,0:T(8,128)}, f32[64,256]{1,0:T(8,128)}) custom-call(bf16[576,256]{1,0:T(8,128)(2,1)S(1)} %get-tuple-element.33.mine, bf16[576,256]{1,0:T(8,128)(2,1)S(1)} %collective-permute-done.10.theirs, f32[64,256]{1,0:T(8,128)S(1)} %get-tuple-element.34.kept), custom_call_target="tpu_custom_call" | custom-call | tf_op jit(solution)/shard_map/add/pallas_call | solution.py:313
  (3 shorter events, 0.1 us)
Async XLA Ops:
  3.0 1.6 %collective-permute-start.1 = (bf16[12,64,128]{2,1,0:T(8,128)(2,1)S(1)}, bf16[12,64,128]{2,1,0:T(8,128)(2,1)S(1)}, u32[]{:S(2)}, u32[]{:S(2)}) collective-permute-start(bf16[12,64,128]{2,1,0:T(8,128)(2,1)S(1)} %get-tuple-element.23), channel_id=1, source_target_pairs={{0,1},{1,0},{2,3},{3,2},{4,5},{5,4},{6,7},{7,6},{8,9},{9,8},{10,11... | collective-permute-start | bytes 589832 | tf_op jit(solution)/shard_map/ppermute | solution.py:251
  4.7 5.3 %collective-permute-start.2 = (bf16[4,64,128]{2,1,0:T(8,128)(2,1)S(1)}, bf16[4,64,128]{2,1,0:T(8,128)(2,1)S(1)}, u32[]{:S(2)}, u32[]{:S(2)}) collective-permute-start(bf16[4,64,128]{2,1,0:T(8,128)(2,1)S(1)} %get-tuple-element.25), channel_id=1, source_target_pairs={{0,2},{1,3},{2,0},{3,1},{4,6},{5,7},{6,4},{7,5},{8,10},{9,11},{10,... | collective-permute-start | bytes 196616 | tf_op jit(solution)/shard_map/ppermute | solution.py:251
  10.0 19.5 %copy-start = (bf16[2,256,256]{2,1,0:T(8,128)(2,1)S(1)}, bf16[2,256,256]{2,1,0:T(8,128)(2,1)}, u32[]{:S(2)}) copy-start(bf16[2,256,256]{2,1,0:T(8,128)(2,1)} %w_second.3) | copy-start | bytes 786436
  10.1 8.9 %collective-permute-start.5 = (bf16[336,128]{1,0:T(8,128)(2,1)S(1)}, bf16[336,128]{1,0:T(8,128)(2,1)S(1)}, u32[]{:S(2)}, u32[]{:S(2)}) collective-permute-start(bf16[336,128]{1,0:T(8,128)(2,1)S(1)} %sum_plane.1.refs_0_), channel_id=1, source_target_pairs={{0,12},{1,13},{2,14},{3,15},{4,8},{5,9},{6,10},{7,11},{8,4},{9,5},... | collective-permute-start | bytes 258056 | tf_op jit(solution)/shard_map/ppermute | solution.py:251
  14.1 6.5 %collective-permute-start.4 = (bf16[336,128]{1,0:T(8,128)(2,1)S(1)}, bf16[336,128]{1,0:T(8,128)(2,1)S(1)}, u32[]{:S(2)}, u32[]{:S(2)}) collective-permute-start(bf16[336,128]{1,0:T(8,128)(2,1)S(1)} %sum_plane.1.refs_0_), channel_id=1, source_target_pairs={{0,8},{1,9},{2,10},{3,11},{4,12},{5,13},{6,14},{7,15},{8,0},{9,1},... | collective-permute-start | bytes 258056 | tf_op jit(solution)/shard_map/ppermute | solution.py:251
  14.1 6.5 %collective-permute-start.3 = (bf16[336,128]{1,0:T(8,128)(2,1)S(1)}, bf16[336,128]{1,0:T(8,128)(2,1)S(1)}, u32[]{:S(2)}, u32[]{:S(2)}) collective-permute-start(bf16[336,128]{1,0:T(8,128)(2,1)S(1)} %sum_plane.1.refs_0_), channel_id=1, source_target_pairs={{0,4},{1,5},{2,6},{3,7},{4,0},{5,1},{6,2},{7,3},{8,12},{9,13},{10,... | collective-permute-start | bytes 258056 | tf_op jit(solution)/shard_map/ppermute | solution.py:251
  14.7 4.3 %collective-permute-start = (bf16[4,64,128]{2,1,0:T(8,128)(2,1)S(1)}, bf16[4,64,128]{2,1,0:T(8,128)(2,1)S(1)}, u32[]{:S(2)}, u32[]{:S(2)}) collective-permute-start(bf16[4,64,128]{2,1,0:T(8,128)(2,1)S(1)} %get-tuple-element.20.x_mine), channel_id=1, source_target_pairs={{0,16},{1,17},{2,18},{3,19},{4,20},{5,21},{6,22},{7,23},{8,24},{9,... | collective-permute-start | bytes 196616 | tf_op jit(solution)/shard_map/ppermute | solution.py:251
  20.6 6.5 %collective-permute-start.8 = (bf16[528,128]{1,0:T(8,128)(2,1)S(1)}, bf16[528,128]{1,0:T(8,128)(2,1)S(1)}, u32[]{:S(2)}, u32[]{:S(2)}) collective-permute-start(bf16[528,128]{1,0:T(8,128)(2,1)S(1)} %get-tuple-element.26.plane_0), channel_id=1, source_target_pairs={{0,18},{1,19},{2,16},{3,17},{4,22},{5,23},{6,20},{7,21},{8,26},{9,... | collective-permute-start | bytes 405512 | tf_op jit(solution)/shard_map/ppermute | solution.py:251
  23.1 6.3 %collective-permute-start.7 = (bf16[528,128]{1,0:T(8,128)(2,1)S(1)}, bf16[528,128]{1,0:T(8,128)(2,1)S(1)}, u32[]{:S(2)}, u32[]{:S(2)}) collective-permute-start(bf16[528,128]{1,0:T(8,128)(2,1)S(1)} %get-tuple-element.26.plane_0), channel_id=1, source_target_pairs={{0,2},{1,3},{2,0},{3,1},{4,6},{5,7},{6,4},{7,5},{8,10},{9,11},{10,... | collective-permute-start | bytes 405512 | tf_op jit(solution)/shard_map/ppermute | solution.py:251
  23.6 5.8 %collective-permute-start.6 = (bf16[528,128]{1,0:T(8,128)(2,1)S(1)}, bf16[528,128]{1,0:T(8,128)(2,1)S(1)}, u32[]{:S(2)}, u32[]{:S(2)}) collective-permute-start(bf16[528,128]{1,0:T(8,128)(2,1)S(1)} %get-tuple-element.26.plane_0), channel_id=1, source_target_pairs={{0,16},{1,17},{2,18},{3,19},{4,20},{5,21},{6,22},{7,23},{8,24},{9,... | collective-permute-start | bytes 405512 | tf_op jit(solution)/shard_map/ppermute | solution.py:251
  24.2 6.2 %collective-permute-start.9 = (bf16[4,64,128]{2,1,0:T(8,128)(2,1)S(1)}, bf16[4,64,128]{2,1,0:T(8,128)(2,1)S(1)}, u32[]{:S(2)}, u32[]{:S(2)}) collective-permute-start(bf16[4,64,128]{2,1,0:T(8,128)(2,1)S(1)} %collective-permute-done.after.x_peer), channel_id=1, source_target_pairs={{0,1},{1,0},{2,3},{3,2},{4,5},{5,4},{6,7},{7,6},{8,9},{9,8},{10,11... | collective-permute-start | bytes 196616 | tf_op jit(solution)/shard_map/ppermute | solution.py:251
  31.8 1.6 %collective-permute-start.10 = (bf16[576,256]{1,0:T(8,128)(2,1)S(1)}, bf16[576,256]{1,0:T(8,128)(2,1)S(1)}, u32[]{:S(2)}, u32[]{:S(2)}) collective-permute-start(bf16[576,256]{1,0:T(8,128)(2,1)S(1)} %get-tuple-element.33.mine), channel_id=1, source_target_pairs={{0,1},{1,0},{2,3},{3,2},{4,5},{5,4},{6,7},{7,6},{8,9},{9,8},{10,11... | collective-permute-start | bytes 884744 | tf_op jit(solution)/shard_map/ppermute | solution.py:251

commit v2 on v1

--- a/solution.py
+++ b/solution.py
@@ -17,7 +17,7 @@
 F32 = jnp.float32
 BF16 = jnp.bfloat16
 AXES = ("graph", "feat")
-PLANE = ((0, 0), (1, 0), (0, 1), (1, 1))
+PLANE = ((0, 0), (1, 1), (0, 1), (1, 0))
 
 
 def silu_grad(value):
@@ -53,7 +53,6 @@
     for copy in copies:
         copy.start()
     copies[0].wait()
-    copies[1].wait()
     sources = feat_t.shape[1]
     row = lax.broadcasted_iota(jnp.int32, (LANES, LANES), 0)
     for t in range(x_t.shape[0]):
@@ -65,10 +64,11 @@
             packed = packed + jnp.where(row == low[k : k + 1, :], unit[k : k + 1, :], 0)
         parts = [jnp.right_shift(packed, 4 * b) & 15 for b in range(sources // LANES)]
         counts = jnp.concatenate([part.astype(F32).astype(BF16) for part in parts], axis=0)
+        if t == 0:
+            copies[1].wait()
         mean = (dot(feat_t[...], counts, ((1,), (0,))) / FAN1).astype(BF16)
         chunk = jnp.concatenate([feat_t[:, cols], mean], axis=0)
         x_t[t] = chunk
-        sent[2 * x_t.shape[0] + t] = chunk
         if t == 0:
             copies[2].wait()
         share[cols, :] = dot(chunk, w_first[...], ((0,), (0,)))
@@ -99,8 +99,8 @@
     message[rows:, :] = pack[...]
 
 
-def sum_line_kernel(after, *refs):
-    parts, (exact, message) = refs[:-2], refs[-2:]
+def sum_line_kernel(x_mine, x_peer, *refs):
+    parts, (exact, message, slices) = refs[:-3], refs[-3:]
     my_z = lax.axis_index("feat") // 4
     line, width = exact.shape[0], exact.shape[1]
     rows = line * width
@@ -116,6 +116,8 @@
         message[pl.ds(at, width), :] = part[rows : rows + width, :]
     lists = [part[rows + width :, :].astype(F32) for part in parts]
     message[2 * rows :, :] = functools.reduce(lambda a, b: a + b, lists).astype(BF16)
+    slices[0:line] = x_mine[...]
+    slices[line : 2 * line] = x_peer[...]
 
 
 def back_kernel(n_feat, plane_0, plane_1, plane_2, plane_3, w_second, cot_all, near_cot, d_hidden, own_counts, lists, spread, turn):
@@ -171,9 +173,25 @@
     d_hidden[...] = part + dot(near_cot[...], w_second[1], ((1,), (1,)))
 
 
+def out_kernel(n_feat, mine, peer, exact, own_counts, w_second, layer_out, ext):
+    my_graph = lax.axis_index("graph")
+    my_z = lax.axis_index("feat") // 4
+    own = exact[pl.ds(my_z, 1)][0]
+    other = peer[pl.ds(pl.multiple_of(my_z * 4 * OWN, 4 * OWN), 2 * OWN), :].astype(F32)
+    hiddens = []
+    for value in (own, other):
+        value = jnp.concatenate([value[0:OWN, :], value[OWN : 2 * OWN, :]], axis=1)
+        hiddens.append((value * (0.5 + 0.5 * jnp.tanh(0.5 * value))).astype(BF16))
+    ext[pl.ds(pl.multiple_of(my_graph * OWN, OWN), OWN), :] = hiddens[0]
+    ext[pl.ds(pl.multiple_of((1 - my_graph) * OWN, OWN), OWN), :] = hiddens[1]
+    mean = (dot(own_counts[...].astype(BF16), ext[...], ((1,), (0,))) / FAN2).astype(BF16)
+    out = dot(hiddens[0], w_second[0], ((1,), (0,))) + dot(mean, w_second[1], ((1,), (0,)))
+    layer_out[...] = out.astype(BF16)
+
+
 def last_kernel(
-    n_feat, plane_0, plane_1, plane_2, plane_3, exact, cot, near_cot, d_hidden, own_counts, x_mine, x_core, x_peer, x_last, w_second,
-    layer_out, swapped, kept, hidden, d_pre, slices, ext,
+    n_feat, plane_0, plane_1, plane_2, plane_3, cot, near_cot, d_hidden, x_mine, x_core,
+    swapped, kept, hidden, d_pre, slices,
 ):
     my_graph = lax.axis_index("graph")
     my_feat = lax.axis_index("feat")
@@ -199,33 +217,30 @@
 
     for z in range(line):
         cols = slice(z * LANES, (z + 1) * LANES)
-        slices[0, 0 : 2 * OWN, cols] = x_mine[z]
-        slices[0, 2 * OWN : 4 * OWN, cols] = x_core[2 * line + z]
-        slices[1, 0 : 2 * OWN, cols] = x_peer[z]
-        slices[1, 2 * OWN : 4 * OWN, cols] = x_last[z]
+        for g in range(2):
+            slices[g, 0 : 2 * OWN, cols] = x_mine[g * line + z]
+            slices[g, 2 * OWN : 4 * OWN, cols] = x_core[g * line + z]
     mine = d_pre[pl.ds(pl.multiple_of(my_graph * rows, rows), rows), :]
     peer = d_pre[pl.ds(pl.multiple_of((1 - my_graph) * rows, rows), rows), :]
     first = dot(slices[0], mine, ((1,), (0,))) + dot(slices[1], peer, ((1,), (0,)))
     kept[...] = first[0 : 2 * OWN, :]
     swapped[2 * HID : 2 * HID + 2 * OWN, :] = first[2 * OWN : 4 * OWN, :].astype(BF16)
 
-    value = exact[pl.ds(my_feat // 4, 1)][0]
-    value = jnp.concatenate([value[0:OWN, :], value[OWN : 2 * OWN, :]], axis=1)
-    hidden_own = (value * (0.5 + 0.5 * jnp.tanh(0.5 * value))).astype(BF16)
-    for p in range(2):
-        at = (p * 2 + my_y) * LANES + (my_feat // 4) * OWN
-        ext[p * OWN : (p + 1) * OWN, :] = hidden[pl.ds(pl.multiple_of(at, OWN), OWN), :]
-    ext[pl.ds(pl.multiple_of(my_graph * OWN, OWN), OWN), :] = hidden_own
-    mean = (dot(own_counts[...].astype(BF16), ext[...], ((1,), (0,))) / FAN2).astype(BF16)
-    out = dot(hidden_own, w_second[0], ((1,), (0,))) + dot(mean, w_second[1], ((1,), (0,)))
-    layer_out[...] = out.astype(BF16)
-
-
-def add_kernel(mine, theirs, kept, grad_second, grad_first):
-    for w in range(2):
-        span = slice(w * HID, (w + 1) * HID)
-        grad_second[w] = mine[span, :].astype(F32) + theirs[span, :].astype(F32)
-    grad_first[...] = kept[...] + theirs[2 * HID : 2 * HID + 2 * OWN, :].astype(F32)
+
+def add_kernel(mine, theirs, kept, grad_second, grad_first, second, first, sems):
+    step = HID // 2
+    copies = []
+    for i in range(4):
+        span = slice(i * step, (i + 1) * step)
+        w, rows = i // 2, slice(i % 2 * step, (i % 2 + 1) * step)
+        second[w, rows, :] = mine[span, :].astype(F32) + theirs[span, :].astype(F32)
+        copies.append(pltpu.make_async_copy(second.at[w, rows, :], grad_second.at[w, rows, :], sems.at[i]))
+        copies[-1].start()
+    first[...] = kept[...] + theirs[2 * HID : 2 * HID + 2 * OWN, :].astype(F32)
+    copies.append(pltpu.make_async_copy(first, grad_first, sems.at[4]))
+    copies[-1].start()
+    for copy in copies:
+        copy.wait()
 
 
 VMEM = pl.BlockSpec(memory_space=pltpu.VMEM)
@@ -234,14 +249,13 @@
 LIMIT = 40 * 1024 * 1024
 
 
-def call(kernel, outs, ins, scratch=(), name=None, aliases=None):
+def call(kernel, outs, ins, scratch=(), name=None, place=VMEM):
     return pl.pallas_call(
         kernel,
         out_shape=[jax.ShapeDtypeStruct(shape, dtype) for shape, dtype in outs],
         in_specs=ins,
-        out_specs=[VMEM] * len(outs),
+        out_specs=[place] * len(outs),
         scratch_shapes=list(scratch),
-        input_output_aliases=aliases or {},
         compiler_params=pltpu.CompilerParams(vmem_limit_bytes=LIMIT),
         name=name,
     )
@@ -260,14 +274,13 @@
     block = (line, width, LANES)
     pack, x_mine, kept, sent = call(
         first_kernel,
-        [((width + INTS, LANES), BF16), (block, BF16), ((2 * line, width, LANES), F32), ((3 * line, width, LANES), BF16)],
+        [((width + INTS, LANES), BF16), (block, BF16), ((2 * line, width, LANES), F32), ((2 * line, width, LANES), BF16)],
         [ANY] * 6,
         [pltpu.VMEM(x.shape, x.dtype) for x in from_hbm[:-1]]
         + [pltpu.SMEM(send_rows.shape, jnp.int32), pltpu.VMEM((rows, HID), F32), pltpu.SemaphoreType.DMA((6,))],
         name="first",
     )(*[pltpu.with_memory_space_constraint(x, pltpu.HBM) for x in from_hbm])
-    x_core = swap(n_feat, sent, 1)
-    kept, sent = call(sum_core_kernel, [(block, F32), (block, BF16)], [VMEM] * 2, name="sum_core")(kept, x_core)
+    kept, sent = call(sum_core_kernel, [(block, F32), (block, BF16)], [VMEM] * 2, name="sum_core")(kept, swap(n_feat, sent, 1))
     x_peer = swap(n_feat, x_mine, n_feat)
     (message,) = call(
         sum_plane_kernel,
@@ -275,15 +288,13 @@
         [VMEM] * 3,
         name="sum_plane",
     )(pack, kept, swap(n_feat, sent, 2))
-    x_last = swap(n_feat, x_peer, 1)
-    exact, message = call(
+    exact, message, slices = call(
         sum_line_kernel,
-        [(block, F32), ((2 * line * width + INTS, LANES), BF16)],
-        [ANY] + [VMEM] * line,
+        [(block, F32), ((2 * line * width + INTS, LANES), BF16), ((2 * line, width, LANES), BF16)],
+        [VMEM] * (line + 2),
         name="sum_line",
-    )(x_peer, message, *[swap(n_feat, message, 4 * z) for z in range(1, line)])
-    plane = [swap(n_feat, message, r) for r in (n_feat + 2, 2, n_feat)]
-    plane = [message, *plane[::-1]]
+    )(x_mine, x_peer, message, *[swap(n_feat, message, 4 * z) for z in range(1, line)])
+    plane = [message] + [swap(n_feat, message, r) for r in (n_feat + 2, 2, n_feat)]
 
     half = (devices // 2) * OWN
     cot, near_cot, d_hidden, own_counts = call(
@@ -298,23 +309,31 @@
         name="back",
     )(*plane, w_second)
 
-    layer_out, swapped, kept = call(
+    swapped, kept = call(
         functools.partial(last_kernel, n_feat),
-        [((OWN, HID), BF16), ((2 * HID + width, HID), BF16), ((width, HID), F32)],
-        [VMEM] * 14,
+        [((2 * HID + width, HID), BF16), ((width, HID), F32)],
+        [VMEM] * 9,
         [
             pltpu.VMEM((half, HID), BF16),
             pltpu.VMEM((2 * half, HID), BF16),
             pltpu.VMEM((2, 2 * width, rows), BF16),
-            pltpu.VMEM((width, HID), BF16),
         ],
         name="last",
-    )(*plane, exact, cot, near_cot, d_hidden, own_counts, x_mine, x_core, x_peer, x_last, w_second)
+    )(*plane, cot, near_cot, d_hidden, slices, swap(n_feat, slices, 1))
+    (layer_out,) = call(
+        functools.partial(out_kernel, n_feat),
+        [((OWN, HID), BF16)],
+        [VMEM] * 5,
+        [pltpu.VMEM((width, HID), BF16)],
+        name="out",
+    )(message, plane[3], exact, own_counts, w_second)
     grad_second, grad_first = call(
         add_kernel,
         [((2, HID, HID), F32), ((width, HID), F32)],
         [VMEM] * 3,
+        [pltpu.VMEM((2, HID, HID), F32), pltpu.VMEM((width, HID), F32), pltpu.SemaphoreType.DMA((5,))],
         name="add",
+        place=ANY,
     )(swapped, swap(n_feat, swapped, 1), kept)
     return (layer_out, grad_second, grad_first.reshape(2, OWN, HID))
 

time: 34.4 us -> 34.1 us (level)
  waiting for transfers between devices: 14.6 us -> 14.1 us
    ppermute x11, waiting for transfers between devices: 14.6 us -> 14.1 us  [swap(): lax.ppermute(value, AXES, [(d, d ^ relative) for d in range(2 * n_feat)])]
    pallas_call x1 -> x2, Pallas kernels: 1.37 us -> 1.58 us  [the longest x1 0.9 us: pair_body(): call(functools.partial(out_kernel, n_feat), [((OWN, HID), BF16)], [VMEM]...]
  transfers between devices with their start and end apart: 11 -> 11, of which waited for: 8 -> 9; matrix products, arithmetic and copies ran while one was open for 0% -> 0% of each run, Pallas kernels for 3% -> 5%
where the time goes in v2:
time: 34.1 us; the launch traced here: 33.9 us
  waiting for transfers between devices  14.1 us (41%)
  starting transfers between devices  13.4 us (39%)
  Pallas kernels  5.76 us (17%)
  between operations  0.7 us (2%)
    ppermute x11, waiting for transfers between devices, swap(): lax.ppermute(value, AXES, [(d, d ^ relative) for d in range(2 * n_feat)])  14.1 us
    ppermute x11, starting transfers between devices, swap(): lax.ppermute(value, AXES, [(d, d ^ relative) for d in range(2 * n_feat)])  13.4 us
    pallas_call x1, Pallas kernels, pair_body(): call(first_kernel, [((width + INTS, LANES), BF16), (block, BF16), ((2 * l...  2.34 us
    pallas_call x1, Pallas kernels, pair_body(): call(functools.partial(out_kernel, n_feat), [((OWN, HID), BF16)], [VMEM]...  0.9 us
    pallas_call x1, Pallas kernels, pair_body(): call(functools.partial(back_kernel, n_feat), [((half, HID), BF16), ((half...  0.9 us
    pallas_call x1, Pallas kernels, pair_body(): call(add_kernel, [((2, HID, HID), F32), ((width, HID), F32)], [VMEM] * 3,...  0.86 us
  transfers between devices with their start and end apart: 11, of which 9 were waited for; matrix products, arithmetic and copies ran while one was open for 0% of the time, Pallas kernels for 5%

profile of v2, /device:TPU:0, one launch (start us, length us, event | category | flops | bytes accessed | tf_op | source)
XLA Modules:
  0.0 33.9 jit_solution(17850065945932276261)
XLA Ops:
  0.6 2.3 %first.1 = (bf16[80,128]{1,0:T(8,128)(2,1)S(1)}, bf16[4,64,128]{2,1,0:T(8,128)(2,1)S(1)}, f32[8,64,128]{2,1,0:T(8,128)S(1)}, bf16[8,64,128]{2,1,0:T(8,128)(2,1)S(1)}) custom-call(bf16[32,1024]{1,0:T(8,128)(2,1)} %bitcast.5, s32[15,512]{1,0:T(8,128)} %bitcast.6, bf16[64,256]{1,0:T(8,128)(2,1)} %bitcast.7, bf16[32,256]{1,0:T(8,128)(2,1)} %cot_hbm.1, ...), custom_call_target="tpu_custom_call" | custom-call | tf_op jit(solution)/shard_map/first/pallas_call | solution.py:275
  3.0 0.5 %collective-permute-start.1 = (bf16[8,64,128]{2,1,0:T(8,128)(2,1)S(1)}, bf16[8,64,128]{2,1,0:T(8,128)(2,1)S(1)}, u32[]{:S(2)}, u32[]{:S(2)}) collective-permute-start(bf16[8,64,128]{2,1,0:T(8,128)(2,1)S(1)} %get-tuple-element.23), channel_id=1, source_target_pairs={{0,1},{1,0},{2,3},{3,2},{4,5},{5,4},{6,7},{7,6},{8,9},{9,8},{10,11... | collective-permute-start | bytes 393224 | tf_op jit(solution)/shard_map/ppermute | solution.py:265
  3.5 1.0 %collective-permute-done.1.received = bf16[8,64,128]{2,1,0:T(8,128)(2,1)S(1)} collective-permute-done((bf16[8,64,128]{2,1,0:T(8,128)(2,1)S(1)}, bf16[8,64,128]{2,1,0:T(8,128)(2,1)S(1)}, u32[]{:S(2)}, u32[]{:S(2)}) %collective-permute-start.1) | collective-permute-done | bytes 131104 | tf_op jit(solution)/shard_map/ppermute | solution.py:265
  4.5 2.9 %collective-permute-start.2 = (bf16[4,64,128]{2,1,0:T(8,128)(2,1)S(1)}, bf16[4,64,128]{2,1,0:T(8,128)(2,1)S(1)}, u32[]{:S(2)}, u32[]{:S(2)}) collective-permute-start(bf16[4,64,128]{2,1,0:T(8,128)(2,1)S(1)} %get-tuple-element.25), channel_id=1, source_target_pairs={{0,2},{1,3},{2,0},{3,1},{4,6},{5,7},{6,4},{7,5},{8,10},{9,11},{10,... | collective-permute-start | bytes 196616 | tf_op jit(solution)/shard_map/ppermute | solution.py:265
  7.5 2.4 %collective-permute-done.2.received = bf16[4,64,128]{2,1,0:T(8,128)(2,1)S(1)} collective-permute-done((bf16[4,64,128]{2,1,0:T(8,128)(2,1)S(1)}, bf16[4,64,128]{2,1,0:T(8,128)(2,1)S(1)}, u32[]{:S(2)}, u32[]{:S(2)}) %collective-permute-start.2) | collective-permute-done | bytes 65568 | tf_op jit(solution)/shard_map/ppermute | solution.py:265
  9.9 0.0 copy-start
  9.9 2.0 %collective-permute-start.3 = (bf16[336,128]{1,0:T(8,128)(2,1)S(1)}, bf16[336,128]{1,0:T(8,128)(2,1)S(1)}, u32[]{:S(2)}, u32[]{:S(2)}) collective-permute-start(bf16[336,128]{1,0:T(8,128)(2,1)S(1)} %sum_plane.1.refs_0_), channel_id=1, source_target_pairs={{0,4},{1,5},{2,6},{3,7},{4,0},{5,1},{6,2},{7,3},{8,12},{9,13},{10,... | collective-permute-start | bytes 258056 | tf_op jit(solution)/shard_map/ppermute | solution.py:265
  11.9 2.6 %collective-permute-start.4 = (bf16[336,128]{1,0:T(8,128)(2,1)S(1)}, bf16[336,128]{1,0:T(8,128)(2,1)S(1)}, u32[]{:S(2)}, u32[]{:S(2)}) collective-permute-start(bf16[336,128]{1,0:T(8,128)(2,1)S(1)} %sum_plane.1.refs_0_), channel_id=1, source_target_pairs={{0,8},{1,9},{2,10},{3,11},{4,12},{5,13},{6,14},{7,15},{8,0},{9,1},... | collective-permute-start | bytes 258056 | tf_op jit(solution)/shard_map/ppermute | solution.py:265
  14.5 0.0 collective-permute-start.5
  14.5 1.7 %collective-permute-start = (bf16[4,64,128]{2,1,0:T(8,128)(2,1)S(1)}, bf16[4,64,128]{2,1,0:T(8,128)(2,1)S(1)}, u32[]{:S(2)}, u32[]{:S(2)}) collective-permute-start(bf16[4,64,128]{2,1,0:T(8,128)(2,1)S(1)} %get-tuple-element.20.x_mine), channel_id=1, source_target_pairs={{0,16},{1,17},{2,18},{3,19},{4,20},{5,21},{6,22},{7,23},{8,24},{9,... | collective-permute-start | bytes 196616 | tf_op jit(solution)/shard_map/ppermute | solution.py:265
  16.2 2.6 %collective-permute-done.x_peer = bf16[4,64,128]{2,1,0:T(8,128)(2,1)S(1)} collective-permute-done((bf16[4,64,128]{2,1,0:T(8,128)(2,1)S(1)}, bf16[4,64,128]{2,1,0:T(8,128)(2,1)S(1)}, u32[]{:S(2)}, u32[]{:S(2)}) %collective-permute-start) | collective-permute-done | bytes 65568 | tf_op jit(solution)/shard_map/ppermute | solution.py:265
  18.7 0.0 collective-permute-done.3.refs_1_
  18.7 0.9 %collective-permute-done.4.refs_2_ = bf16[336,128]{1,0:T(8,128)(2,1)S(1)} collective-permute-done((bf16[336,128]{1,0:T(8,128)(2,1)S(1)}, bf16[336,128]{1,0:T(8,128)(2,1)S(1)}, u32[]{:S(2)}, u32[]{:S(2)}) %collective-permute-start.4) | collective-permute-done | bytes 86048 | tf_op jit(solution)/shard_map/ppermute | solution.py:265
  19.6 1.2 %collective-permute-done.5.refs_3_ = bf16[336,128]{1,0:T(8,128)(2,1)S(1)} collective-permute-done((bf16[336,128]{1,0:T(8,128)(2,1)S(1)}, bf16[336,128]{1,0:T(8,128)(2,1)S(1)}, u32[]{:S(2)}, u32[]{:S(2)}) %collective-permute-start.5) | collective-permute-done | bytes 86048 | tf_op jit(solution)/shard_map/ppermute | solution.py:265
  20.9 1.6 %collective-permute-start.6 = (bf16[528,128]{1,0:T(8,128)(2,1)S(1)}, bf16[528,128]{1,0:T(8,128)(2,1)S(1)}, u32[]{:S(2)}, u32[]{:S(2)}) collective-permute-start(bf16[528,128]{1,0:T(8,128)(2,1)S(1)} %get-tuple-element.26.plane_0.mine), channel_id=1, source_target_pairs={{0,16},{1,17},{2,18},{3,19},{4,20},{5,21},{6,22},{7,23},{8,24},{9,... | collective-permute-start | bytes 405512 | tf_op jit(solution)/shard_map/ppermute | solution.py:265
  22.5 1.5 %collective-permute-start.7 = (bf16[528,128]{1,0:T(8,128)(2,1)S(1)}, bf16[528,128]{1,0:T(8,128)(2,1)S(1)}, u32[]{:S(2)}, u32[]{:S(2)}) collective-permute-start(bf16[528,128]{1,0:T(8,128)(2,1)S(1)} %get-tuple-element.26.plane_0.mine), channel_id=1, source_target_pairs={{0,18},{1,19},{2,16},{3,17},{4,22},{5,23},{6,20},{7,21},{8,26},{9,... | collective-permute-start | bytes 405512 | tf_op jit(solution)/shard_map/ppermute | solution.py:265
  23.9 0.5 %collective-permute-start.8 = (bf16[528,128]{1,0:T(8,128)(2,1)S(1)}, bf16[528,128]{1,0:T(8,128)(2,1)S(1)}, u32[]{:S(2)}, u32[]{:S(2)}) collective-permute-start(bf16[528,128]{1,0:T(8,128)(2,1)S(1)} %get-tuple-element.26.plane_0.mine), channel_id=1, source_target_pairs={{0,2},{1,3},{2,0},{3,1},{4,6},{5,7},{6,4},{7,5},{8,10},{9,11},{10,... | collective-permute-start | bytes 405512 | tf_op jit(solution)/shard_map/ppermute | solution.py:265
  24.5 0.0 collective-permute-start.9
  24.5 1.9 %collective-permute-done.6.plane_3.peer = bf16[528,128]{1,0:T(8,128)(2,1)S(1)} collective-permute-done((bf16[528,128]{1,0:T(8,128)(2,1)S(1)}, bf16[528,128]{1,0:T(8,128)(2,1)S(1)}, u32[]{:S(2)}, u32[]{:S(2)}) %collective-permute-start.6) | collective-permute-done | bytes 135200 | tf_op jit(solution)/shard_map/ppermute | solution.py:265
  26.4 2.1 %collective-permute-done.7.plane_1 = bf16[528,128]{1,0:T(8,128)(2,1)S(1)} collective-permute-done((bf16[528,128]{1,0:T(8,128)(2,1)S(1)}, bf16[528,128]{1,0:T(8,128)(2,1)S(1)}, u32[]{:S(2)}, u32[]{:S(2)}) %collective-permute-start.7) | collective-permute-done | bytes 135200 | tf_op jit(solution)/shard_map/ppermute | solution.py:265
  28.5 1.4 %collective-permute-done.8.plane_2 = bf16[528,128]{1,0:T(8,128)(2,1)S(1)} collective-permute-done((bf16[528,128]{1,0:T(8,128)(2,1)S(1)}, bf16[528,128]{1,0:T(8,128)(2,1)S(1)}, u32[]{:S(2)}, u32[]{:S(2)}) %collective-permute-start.8) | collective-permute-done | bytes 135200 | tf_op jit(solution)/shard_map/ppermute | solution.py:265
  29.8 0.0 copy-done
  29.8 0.9 %back.1 = (bf16[512,256]{1,0:T(8,128)(2,1)S(1)}, bf16[512,256]{1,0:T(8,128)(2,1)S(1)}, f32[512,256]{1,0:T(8,128)S(1)}, f32[32,64]{1,0:T(8,128)S(1)}) custom-call(bf16[528,128]{1,0:T(8,128)(2,1)S(1)} %get-tuple-element.26.plane_0.mine, bf16[528,128]{1,0:T(8,128)(2,1)S(1)} %collective-permute-done.7.plane_1, ...), custom_call_target="tpu_custom_call" | custom-call | tf_op jit(solution)/shard_map/back/pallas_call | solution.py:300
  30.7 0.0 collective-permute-done.9.x_core
  30.7 0.7 %last.1 = (bf16[576,256]{1,0:T(8,128)(2,1)S(1)}, f32[64,256]{1,0:T(8,128)S(1)}) custom-call(bf16[528,128]{1,0:T(8,128)(2,1)S(1)} %get-tuple-element.26.plane_0.mine, bf16[528,128]{1,0:T(8,128)(2,1)S(1)} %collective-permute-done.7.plane_1, bf16[528,128]{1,0:T(8,128)(2,1)S(1)} %collective-permute-done.8.plane_2, ...), custom_call_target="tpu_custom_call" | custom-call | tf_op jit(solution)/shard_map/last/pallas_call | solution.py:312
  31.4 0.1 collective-permute-start.10
  31.5 0.9 %out.1 = bf16[32,256]{1,0:T(8,128)(2,1)} custom-call(bf16[528,128]{1,0:T(8,128)(2,1)S(1)} %get-tuple-element.26.plane_0.mine, bf16[528,128]{1,0:T(8,128)(2,1)S(1)} %collective-permute-done.6.plane_3.peer, f32[4,64,128]{2,1,0:T(8,128)S(1)} %get-tuple-element.27.exact, f32[32,64]{1,0:T(8,128)S(1)} %get-tuple-element.28.own_counts, bf16[2,256,256]{2,1,0:T(8,128)(2,1)S(1)} %copy-done), custom_call_target="tpu_custom_call" | custom-call | tf_op jit(solution)/shard_map/out/pallas_call | solution.py:323
  32.4 0.7 %collective-permute-done.10.theirs = bf16[576,256]{1,0:T(8,128)(2,1)S(1)} collective-permute-done((bf16[576,256]{1,0:T(8,128)(2,1)S(1)}, bf16[576,256]{1,0:T(8,128)(2,1)S(1)}, u32[]{:S(2)}, u32[]{:S(2)}) %collective-permute-start.10) | collective-permute-done | bytes 294944 | tf_op jit(solution)/shard_map/ppermute | solution.py:265
  33.1 0.9 %add.1 = (f32[2,256,256]{2,1,0:T(8,128)}, f32[64,256]{1,0:T(8,128)}) custom-call(bf16[576,256]{1,0:T(8,128)(2,1)S(1)} %get-tuple-element.33.mine, bf16[576,256]{1,0:T(8,128)(2,1)S(1)} %collective-permute-done.10.theirs, f32[64,256]{1,0:T(8,128)S(1)} %get-tuple-element.34.kept), custom_call_target="tpu_custom_call" | custom-call | tf_op jit(solution)/shard_map/add/pallas_call | solution.py:330
  (3 shorter events, 0.1 us)
Async XLA Ops:
  3.0 1.5 %collective-permute-start.1 = (bf16[8,64,128]{2,1,0:T(8,128)(2,1)S(1)}, bf16[8,64,128]{2,1,0:T(8,128)(2,1)S(1)}, u32[]{:S(2)}, u32[]{:S(2)}) collective-permute-start(bf16[8,64,128]{2,1,0:T(8,128)(2,1)S(1)} %get-tuple-element.23), channel_id=1, source_target_pairs={{0,1},{1,0},{2,3},{3,2},{4,5},{5,4},{6,7},{7,6},{8,9},{9,8},{10,11... | collective-permute-start | bytes 393224 | tf_op jit(solution)/shard_map/ppermute | solution.py:265
  4.5 5.3 %collective-permute-start.2 = (bf16[4,64,128]{2,1,0:T(8,128)(2,1)S(1)}, bf16[4,64,128]{2,1,0:T(8,128)(2,1)S(1)}, u32[]{:S(2)}, u32[]{:S(2)}) collective-permute-start(bf16[4,64,128]{2,1,0:T(8,128)(2,1)S(1)} %get-tuple-element.25), channel_id=1, source_target_pairs={{0,2},{1,3},{2,0},{3,1},{4,6},{5,7},{6,4},{7,5},{8,10},{9,11},{10,... | collective-permute-start | bytes 196616 | tf_op jit(solution)/shard_map/ppermute | solution.py:265
  9.9 20.0 %copy-start = (bf16[2,256,256]{2,1,0:T(8,128)(2,1)S(1)}, bf16[2,256,256]{2,1,0:T(8,128)(2,1)}, u32[]{:S(2)}) copy-start(bf16[2,256,256]{2,1,0:T(8,128)(2,1)} %w_second.3) | copy-start | bytes 786436
  9.9 8.8 %collective-permute-start.3 = (bf16[336,128]{1,0:T(8,128)(2,1)S(1)}, bf16[336,128]{1,0:T(8,128)(2,1)S(1)}, u32[]{:S(2)}, u32[]{:S(2)}) collective-permute-start(bf16[336,128]{1,0:T(8,128)(2,1)S(1)} %sum_plane.1.refs_0_), channel_id=1, source_target_pairs={{0,4},{1,5},{2,6},{3,7},{4,0},{5,1},{6,2},{7,3},{8,12},{9,13},{10,... | collective-permute-start | bytes 258056 | tf_op jit(solution)/shard_map/ppermute | solution.py:265
  11.9 7.7 %collective-permute-start.4 = (bf16[336,128]{1,0:T(8,128)(2,1)S(1)}, bf16[336,128]{1,0:T(8,128)(2,1)S(1)}, u32[]{:S(2)}, u32[]{:S(2)}) collective-permute-start(bf16[336,128]{1,0:T(8,128)(2,1)S(1)} %sum_plane.1.refs_0_), channel_id=1, source_target_pairs={{0,8},{1,9},{2,10},{3,11},{4,12},{5,13},{6,14},{7,15},{8,0},{9,1},... | collective-permute-start | bytes 258056 | tf_op jit(solution)/shard_map/ppermute | solution.py:265
  14.5 6.4 %collective-permute-start.5 = (bf16[336,128]{1,0:T(8,128)(2,1)S(1)}, bf16[336,128]{1,0:T(8,128)(2,1)S(1)}, u32[]{:S(2)}, u32[]{:S(2)}) collective-permute-start(bf16[336,128]{1,0:T(8,128)(2,1)S(1)} %sum_plane.1.refs_0_), channel_id=1, source_target_pairs={{0,12},{1,13},{2,14},{3,15},{4,8},{5,9},{6,10},{7,11},{8,4},{9,5},... | collective-permute-start | bytes 258056 | tf_op jit(solution)/shard_map/ppermute | solution.py:265
  14.5 4.3 %collective-permute-start = (bf16[4,64,128]{2,1,0:T(8,128)(2,1)S(1)}, bf16[4,64,128]{2,1,0:T(8,128)(2,1)S(1)}, u32[]{:S(2)}, u32[]{:S(2)}) collective-permute-start(bf16[4,64,128]{2,1,0:T(8,128)(2,1)S(1)} %get-tuple-element.20.x_mine), channel_id=1, source_target_pairs={{0,16},{1,17},{2,18},{3,19},{4,20},{5,21},{6,22},{7,23},{8,24},{9,... | collective-permute-start | bytes 196616 | tf_op jit(solution)/shard_map/ppermute | solution.py:265
  20.9 5.5 %collective-permute-start.6 = (bf16[528,128]{1,0:T(8,128)(2,1)S(1)}, bf16[528,128]{1,0:T(8,128)(2,1)S(1)}, u32[]{:S(2)}, u32[]{:S(2)}) collective-permute-start(bf16[528,128]{1,0:T(8,128)(2,1)S(1)} %get-tuple-element.26.plane_0.mine), channel_id=1, source_target_pairs={{0,16},{1,17},{2,18},{3,19},{4,20},{5,21},{6,22},{7,23},{8,24},{9,... | collective-permute-start | bytes 405512 | tf_op jit(solution)/shard_map/ppermute | solution.py:265
  22.5 6.0 %collective-permute-start.7 = (bf16[528,128]{1,0:T(8,128)(2,1)S(1)}, bf16[528,128]{1,0:T(8,128)(2,1)S(1)}, u32[]{:S(2)}, u32[]{:S(2)}) collective-permute-start(bf16[528,128]{1,0:T(8,128)(2,1)S(1)} %get-tuple-element.26.plane_0.mine), channel_id=1, source_target_pairs={{0,18},{1,19},{2,16},{3,17},{4,22},{5,23},{6,20},{7,21},{8,26},{9,... | collective-permute-start | bytes 405512 | tf_op jit(solution)/shard_map/ppermute | solution.py:265
  23.9 5.9 %collective-permute-start.8 = (bf16[528,128]{1,0:T(8,128)(2,1)S(1)}, bf16[528,128]{1,0:T(8,128)(2,1)S(1)}, u32[]{:S(2)}, u32[]{:S(2)}) collective-permute-start(bf16[528,128]{1,0:T(8,128)(2,1)S(1)} %get-tuple-element.26.plane_0.mine), channel_id=1, source_target_pairs={{0,2},{1,3},{2,0},{3,1},{4,6},{5,7},{6,4},{7,5},{8,10},{9,11},{10,... | collective-permute-start | bytes 405512 | tf_op jit(solution)/shard_map/ppermute | solution.py:265
  24.5 6.3 %collective-permute-start.9 = (bf16[8,64,128]{2,1,0:T(8,128)(2,1)S(1)}, bf16[8,64,128]{2,1,0:T(8,128)(2,1)S(1)}, u32[]{:S(2)}, u32[]{:S(2)}) collective-permute-start(bf16[8,64,128]{2,1,0:T(8,128)(2,1)S(1)} %get-tuple-element.32.x_mine), channel_id=1, source_target_pairs={{0,1},{1,0},{2,3},{3,2},{4,5},{5,4},{6,7},{7,6},{8,9},{9,8},{10,11... | collective-permute-start | bytes 393224 | tf_op jit(solution)/shard_map/ppermute | solution.py:265
  31.4 1.6 %collective-permute-start.10 = (bf16[576,256]{1,0:T(8,128)(2,1)S(1)}, bf16[576,256]{1,0:T(8,128)(2,1)S(1)}, u32[]{:S(2)}, u32[]{:S(2)}) collective-permute-start(bf16[576,256]{1,0:T(8,128)(2,1)S(1)} %get-tuple-element.33.mine), channel_id=1, source_target_pairs={{0,1},{1,0},{2,3},{3,2},{4,5},{5,4},{6,7},{7,6},{8,9},{9,8},{10,11... | collective-permute-start | bytes 884744 | tf_op jit(solution)/shard_map/ppermute | solution.py:265

commit v3 on v1

--- a/solution.py
+++ b/solution.py
@@ -53,7 +53,6 @@
     for copy in copies:
         copy.start()
     copies[0].wait()
-    copies[1].wait()
     sources = feat_t.shape[1]
     row = lax.broadcasted_iota(jnp.int32, (LANES, LANES), 0)
     for t in range(x_t.shape[0]):
@@ -65,6 +64,8 @@
             packed = packed + jnp.where(row == low[k : k + 1, :], unit[k : k + 1, :], 0)
         parts = [jnp.right_shift(packed, 4 * b) & 15 for b in range(sources // LANES)]
         counts = jnp.concatenate([part.astype(F32).astype(BF16) for part in parts], axis=0)
+        if t == 0:
+            copies[1].wait()
         mean = (dot(feat_t[...], counts, ((1,), (0,))) / FAN1).astype(BF16)
         chunk = jnp.concatenate([feat_t[:, cols], mean], axis=0)
         x_t[t] = chunk
@@ -171,9 +172,25 @@
     d_hidden[...] = part + dot(near_cot[...], w_second[1], ((1,), (1,)))
 
 
+def out_kernel(n_feat, mine, peer, exact, own_counts, w_second, layer_out, ext):
+    my_graph = lax.axis_index("graph")
+    my_z = lax.axis_index("feat") // 4
+    own = exact[pl.ds(my_z, 1)][0]
+    other = peer[pl.ds(pl.multiple_of(my_z * 4 * OWN, 4 * OWN), 2 * OWN), :].astype(F32)
+    hiddens = []
+    for value in (own, other):
+        value = jnp.concatenate([value[0:OWN, :], value[OWN : 2 * OWN, :]], axis=1)
+        hiddens.append((value * (0.5 + 0.5 * jnp.tanh(0.5 * value))).astype(BF16))
+    ext[pl.ds(pl.multiple_of(my_graph * OWN, OWN), OWN), :] = hiddens[0]
+    ext[pl.ds(pl.multiple_of((1 - my_graph) * OWN, OWN), OWN), :] = hiddens[1]
+    mean = (dot(own_counts[...].astype(BF16), ext[...], ((1,), (0,))) / FAN2).astype(BF16)
+    out = dot(hiddens[0], w_second[0], ((1,), (0,))) + dot(mean, w_second[1], ((1,), (0,)))
+    layer_out[...] = out.astype(BF16)
+
+
 def last_kernel(
-    n_feat, plane_0, plane_1, plane_2, plane_3, exact, cot, near_cot, d_hidden, own_counts, x_mine, x_core, x_peer, x_last, w_second,
-    layer_out, swapped, kept, hidden, d_pre, slices, ext,
+    n_feat, plane_0, plane_1, plane_2, plane_3, cot, near_cot, d_hidden, x_mine, x_core, x_peer, x_last,
+    swapped, kept, hidden, d_pre, slices,
 ):
     my_graph = lax.axis_index("graph")
     my_feat = lax.axis_index("feat")
@@ -208,17 +225,6 @@
     first = dot(slices[0], mine, ((1,), (0,))) + dot(slices[1], peer, ((1,), (0,)))
     kept[...] = first[0 : 2 * OWN, :]
     swapped[2 * HID : 2 * HID + 2 * OWN, :] = first[2 * OWN : 4 * OWN, :].astype(BF16)
-
-    value = exact[pl.ds(my_feat // 4, 1)][0]
-    value = jnp.concatenate([value[0:OWN, :], value[OWN : 2 * OWN, :]], axis=1)
-    hidden_own = (value * (0.5 + 0.5 * jnp.tanh(0.5 * value))).astype(BF16)
-    for p in range(2):
-        at = (p * 2 + my_y) * LANES + (my_feat // 4) * OWN
-        ext[p * OWN : (p + 1) * OWN, :] = hidden[pl.ds(pl.multiple_of(at, OWN), OWN), :]
-    ext[pl.ds(pl.multiple_of(my_graph * OWN, OWN), OWN), :] = hidden_own
-    mean = (dot(own_counts[...].astype(BF16), ext[...], ((1,), (0,))) / FAN2).astype(BF16)
-    out = dot(hidden_own, w_second[0], ((1,), (0,))) + dot(mean, w_second[1], ((1,), (0,)))
-    layer_out[...] = out.astype(BF16)
 
 
 def add_kernel(mine, theirs, kept, grad_second, grad_first):
@@ -298,18 +304,24 @@
         name="back",
     )(*plane, w_second)
 
-    layer_out, swapped, kept = call(
+    swapped, kept = call(
         functools.partial(last_kernel, n_feat),
-        [((OWN, HID), BF16), ((2 * HID + width, HID), BF16), ((width, HID), F32)],
-        [VMEM] * 14,
+        [((2 * HID + width, HID), BF16), ((width, HID), F32)],
+        [VMEM] * 11,
         [
             pltpu.VMEM((half, HID), BF16),
             pltpu.VMEM((2 * half, HID), BF16),
             pltpu.VMEM((2, 2 * width, rows), BF16),
-            pltpu.VMEM((width, HID), BF16),
         ],
         name="last",
-    )(*plane, exact, cot, near_cot, d_hidden, own_counts, x_mine, x_core, x_peer, x_last, w_second)
+    )(*plane, cot, near_cot, d_hidden, x_mine, x_core, x_peer, x_last)
+    (layer_out,) = call(
+        functools.partial(out_kernel, n_feat),
+        [((OWN, HID), BF16)],
+        [VMEM] * 5,
+        [pltpu.VMEM((width, HID), BF16)],
+        name="out",
+    )(message, plane[1], exact, own_counts, w_second)
     grad_second, grad_first = call(
         add_kernel,
         [((2, HID, HID), F32), ((width, HID), F32)],

time: 34.4 us -> 34.3 us (level)
  waiting for transfers between devices: 14.6 us -> 14.2 us
    pallas_call x1 -> x2, Pallas kernels: 1.37 us -> 1.58 us  [the longest x1 0.9 us: pair_body(): call(functools.partial(out_kernel, n_feat), [((OWN, HID), BF16)], [VMEM]...]
  transfers between devices with their start and end apart: 11 -> 11, of which waited for: 8 -> 9; matrix products, arithmetic and copies ran while one was open for 0% -> 0% of each run, Pallas kernels for 3% -> 5%
where the time goes in v3:
time: 34.3 us; the launch traced here: 34.1 us
  waiting for transfers between devices  14.2 us (41%)
  starting transfers between devices  13.4 us (39%)
  Pallas kernels  5.76 us (17%)
  between operations  0.7 us (2%)
    ppermute x11, waiting for transfers between devices, swap(): lax.ppermute(value, AXES, [(d, d ^ relative) for d in range(2 * n_feat)])  14.2 us
    ppermute x11, starting transfers between devices, swap(): lax.ppermute(value, AXES, [(d, d ^ relative) for d in range(2 * n_feat)])  13.4 us
    pallas_call x1, Pallas kernels, pair_body(): call(first_kernel, [((width + INTS, LANES), BF16), (block, BF16), ((2 * l...  2.34 us
    pallas_call x1, Pallas kernels, pair_body(): call(functools.partial(out_kernel, n_feat), [((OWN, HID), BF16)], [VMEM]...  0.9 us
    pallas_call x1, Pallas kernels, pair_body(): call(functools.partial(back_kernel, n_feat), [((half, HID), BF16), ((half...  0.9 us
    pallas_call x1, Pallas kernels, pair_body(): call(add_kernel, [((2, HID, HID), F32), ((width, HID), F32)], [VMEM] * 3,...  0.86 us
  transfers between devices with their start and end apart: 11, of which 9 were waited for; matrix products, arithmetic and copies ran while one was open for 0% of the time, Pallas kernels for 5%

profile of v3, /device:TPU:0, one launch (start us, length us, event | category | flops | bytes accessed | tf_op | source)
XLA Modules:
  0.0 34.1 jit_solution(18082103288122828297)
XLA Ops:
  0.6 2.3 %first.1 = (bf16[80,128]{1,0:T(8,128)(2,1)S(1)}, bf16[4,64,128]{2,1,0:T(8,128)(2,1)S(1)}, f32[8,64,128]{2,1,0:T(8,128)S(1)}, bf16[12,64,128]{2,1,0:T(8,128)(2,1)S(1)}) custom-call(bf16[32,1024]{1,0:T(8,128)(2,1)} %bitcast.5, s32[15,512]{1,0:T(8,128)} %bitcast.6, bf16[64,256]{1,0:T(8,128)(2,1)} %bitcast.7, bf16[32,256]{1,0:T(8,128)(2,1)} %cot_hbm.1, ...), custom_call_target="tpu_custom_call" | custom-call | tf_op jit(solution)/shard_map/first/pallas_call | solution.py:267
  3.0 0.5 %collective-permute-start.1 = (bf16[12,64,128]{2,1,0:T(8,128)(2,1)S(1)}, bf16[12,64,128]{2,1,0:T(8,128)(2,1)S(1)}, u32[]{:S(2)}, u32[]{:S(2)}) collective-permute-start(bf16[12,64,128]{2,1,0:T(8,128)(2,1)S(1)} %get-tuple-element.22), channel_id=1, source_target_pairs={{0,1},{1,0},{2,3},{3,2},{4,5},{5,4},{6,7},{7,6},{8,9},{9,8},{10,11... | collective-permute-start | bytes 589832 | tf_op jit(solution)/shard_map/ppermute | solution.py:257
  3.5 1.1 %collective-permute-done.1.received.x_core = bf16[12,64,128]{2,1,0:T(8,128)(2,1)S(1)} collective-permute-done((bf16[12,64,128]{2,1,0:T(8,128)(2,1)S(1)}, bf16[12,64,128]{2,1,0:T(8,128)(2,1)S(1)}, u32[]{:S(2)}, u32[]{:S(2)}) %collective-permute-start.1) | collective-permute-done | bytes 196640 | tf_op jit(solution)/shard_map/ppermute | solution.py:257
  4.6 3.0 %collective-permute-start.2 = (bf16[4,64,128]{2,1,0:T(8,128)(2,1)S(1)}, bf16[4,64,128]{2,1,0:T(8,128)(2,1)S(1)}, u32[]{:S(2)}, u32[]{:S(2)}) collective-permute-start(bf16[4,64,128]{2,1,0:T(8,128)(2,1)S(1)} %get-tuple-element.24), channel_id=1, source_target_pairs={{0,2},{1,3},{2,0},{3,1},{4,6},{5,7},{6,4},{7,5},{8,10},{9,11},{10,... | collective-permute-start | bytes 196616 | tf_op jit(solution)/shard_map/ppermute | solution.py:257
  7.6 2.4 %collective-permute-done.2.received = bf16[4,64,128]{2,1,0:T(8,128)(2,1)S(1)} collective-permute-done((bf16[4,64,128]{2,1,0:T(8,128)(2,1)S(1)}, bf16[4,64,128]{2,1,0:T(8,128)(2,1)S(1)}, u32[]{:S(2)}, u32[]{:S(2)}) %collective-permute-start.2) | collective-permute-done | bytes 65568 | tf_op jit(solution)/shard_map/ppermute | solution.py:257
  10.0 0.0 copy-start
  10.0 2.0 %collective-permute-start.3 = (bf16[336,128]{1,0:T(8,128)(2,1)S(1)}, bf16[336,128]{1,0:T(8,128)(2,1)S(1)}, u32[]{:S(2)}, u32[]{:S(2)}) collective-permute-start(bf16[336,128]{1,0:T(8,128)(2,1)S(1)} %sum_plane.1.refs_0_), channel_id=1, source_target_pairs={{0,4},{1,5},{2,6},{3,7},{4,0},{5,1},{6,2},{7,3},{8,12},{9,13},{10,... | collective-permute-start | bytes 258056 | tf_op jit(solution)/shard_map/ppermute | solution.py:257
  12.0 2.6 %collective-permute-start.4 = (bf16[336,128]{1,0:T(8,128)(2,1)S(1)}, bf16[336,128]{1,0:T(8,128)(2,1)S(1)}, u32[]{:S(2)}, u32[]{:S(2)}) collective-permute-start(bf16[336,128]{1,0:T(8,128)(2,1)S(1)} %sum_plane.1.refs_0_), channel_id=1, source_target_pairs={{0,8},{1,9},{2,10},{3,11},{4,12},{5,13},{6,14},{7,15},{8,0},{9,1},... | collective-permute-start | bytes 258056 | tf_op jit(solution)/shard_map/ppermute | solution.py:257
  14.6 0.0 collective-permute-start.5
  14.6 1.7 %collective-permute-start = (bf16[4,64,128]{2,1,0:T(8,128)(2,1)S(1)}, bf16[4,64,128]{2,1,0:T(8,128)(2,1)S(1)}, u32[]{:S(2)}, u32[]{:S(2)}) collective-permute-start(bf16[4,64,128]{2,1,0:T(8,128)(2,1)S(1)} %get-tuple-element.19.x_mine), channel_id=1, source_target_pairs={{0,16},{1,17},{2,18},{3,19},{4,20},{5,21},{6,22},{7,23},{8,24},{9,... | collective-permute-start | bytes 196616 | tf_op jit(solution)/shard_map/ppermute | solution.py:257
  16.3 2.6 %collective-permute-done.after.x_peer = bf16[4,64,128]{2,1,0:T(8,128)(2,1)S(1)} collective-permute-done((bf16[4,64,128]{2,1,0:T(8,128)(2,1)S(1)}, bf16[4,64,128]{2,1,0:T(8,128)(2,1)S(1)}, u32[]{:S(2)}, u32[]{:S(2)}) %collective-permute-start) | collective-permute-done | bytes 65568 | tf_op jit(solution)/shard_map/ppermute | solution.py:257
  18.8 0.0 collective-permute-done.3.refs_1_
  18.8 0.9 %collective-permute-done.4.refs_2_ = bf16[336,128]{1,0:T(8,128)(2,1)S(1)} collective-permute-done((bf16[336,128]{1,0:T(8,128)(2,1)S(1)}, bf16[336,128]{1,0:T(8,128)(2,1)S(1)}, u32[]{:S(2)}, u32[]{:S(2)}) %collective-permute-start.4) | collective-permute-done | bytes 86048 | tf_op jit(solution)/shard_map/ppermute | solution.py:257
  19.7 1.3 %collective-permute-done.5.refs_3_ = bf16[336,128]{1,0:T(8,128)(2,1)S(1)} collective-permute-done((bf16[336,128]{1,0:T(8,128)(2,1)S(1)}, bf16[336,128]{1,0:T(8,128)(2,1)S(1)}, u32[]{:S(2)}, u32[]{:S(2)}) %collective-permute-start.5) | collective-permute-done | bytes 86048 | tf_op jit(solution)/shard_map/ppermute | solution.py:257
  21.0 1.6 %collective-permute-start.6 = (bf16[528,128]{1,0:T(8,128)(2,1)S(1)}, bf16[528,128]{1,0:T(8,128)(2,1)S(1)}, u32[]{:S(2)}, u32[]{:S(2)}) collective-permute-start(bf16[528,128]{1,0:T(8,128)(2,1)S(1)} %get-tuple-element.25.plane_0.mine), channel_id=1, source_target_pairs={{0,16},{1,17},{2,18},{3,19},{4,20},{5,21},{6,22},{7,23},{8,24},{9,... | collective-permute-start | bytes 405512 | tf_op jit(solution)/shard_map/ppermute | solution.py:257
  22.6 1.5 %collective-permute-start.7 = (bf16[528,128]{1,0:T(8,128)(2,1)S(1)}, bf16[528,128]{1,0:T(8,128)(2,1)S(1)}, u32[]{:S(2)}, u32[]{:S(2)}) collective-permute-start(bf16[528,128]{1,0:T(8,128)(2,1)S(1)} %get-tuple-element.25.plane_0.mine), channel_id=1, source_target_pairs={{0,2},{1,3},{2,0},{3,1},{4,6},{5,7},{6,4},{7,5},{8,10},{9,11},{10,... | collective-permute-start | bytes 405512 | tf_op jit(solution)/shard_map/ppermute | solution.py:257
  24.1 0.5 %collective-permute-start.8 = (bf16[528,128]{1,0:T(8,128)(2,1)S(1)}, bf16[528,128]{1,0:T(8,128)(2,1)S(1)}, u32[]{:S(2)}, u32[]{:S(2)}) collective-permute-start(bf16[528,128]{1,0:T(8,128)(2,1)S(1)} %get-tuple-element.25.plane_0.mine), channel_id=1, source_target_pairs={{0,18},{1,19},{2,16},{3,17},{4,22},{5,23},{6,20},{7,21},{8,26},{9,... | collective-permute-start | bytes 405512 | tf_op jit(solution)/shard_map/ppermute | solution.py:257
  24.6 0.0 collective-permute-start.9
  24.6 2.1 %collective-permute-done.6.plane_1.peer = bf16[528,128]{1,0:T(8,128)(2,1)S(1)} collective-permute-done((bf16[528,128]{1,0:T(8,128)(2,1)S(1)}, bf16[528,128]{1,0:T(8,128)(2,1)S(1)}, u32[]{:S(2)}, u32[]{:S(2)}) %collective-permute-start.6) | collective-permute-done | bytes 135200 | tf_op jit(solution)/shard_map/ppermute | solution.py:257
  26.7 1.2 %collective-permute-done.7.plane_2 = bf16[528,128]{1,0:T(8,128)(2,1)S(1)} collective-permute-done((bf16[528,128]{1,0:T(8,128)(2,1)S(1)}, bf16[528,128]{1,0:T(8,128)(2,1)S(1)}, u32[]{:S(2)}, u32[]{:S(2)}) %collective-permute-start.7) | collective-permute-done | bytes 135200 | tf_op jit(solution)/shard_map/ppermute | solution.py:257
  27.9 2.1 %collective-permute-done.8.plane_3 = bf16[528,128]{1,0:T(8,128)(2,1)S(1)} collective-permute-done((bf16[528,128]{1,0:T(8,128)(2,1)S(1)}, bf16[528,128]{1,0:T(8,128)(2,1)S(1)}, u32[]{:S(2)}, u32[]{:S(2)}) %collective-permute-start.8) | collective-permute-done | bytes 135200 | tf_op jit(solution)/shard_map/ppermute | solution.py:257
  30.0 0.0 copy-done
  30.0 0.9 %back.1 = (bf16[512,256]{1,0:T(8,128)(2,1)S(1)}, bf16[512,256]{1,0:T(8,128)(2,1)S(1)}, f32[512,256]{1,0:T(8,128)S(1)}, f32[32,64]{1,0:T(8,128)S(1)}) custom-call(bf16[528,128]{1,0:T(8,128)(2,1)S(1)} %get-tuple-element.25.plane_0.mine, bf16[528,128]{1,0:T(8,128)(2,1)S(1)} %collective-permute-done.6.plane_1.peer, ...), custom_call_target="tpu_custom_call" | custom-call | tf_op jit(solution)/shard_map/back/pallas_call | solution.py:295
  30.9 0.0 collective-permute-done.9.x_last
  30.9 0.7 %last.1 = (bf16[576,256]{1,0:T(8,128)(2,1)S(1)}, f32[64,256]{1,0:T(8,128)S(1)}) custom-call(bf16[528,128]{1,0:T(8,128)(2,1)S(1)} %get-tuple-element.25.plane_0.mine, bf16[528,128]{1,0:T(8,128)(2,1)S(1)} %collective-permute-done.6.plane_1.peer, bf16[528,128]{1,0:T(8,128)(2,1)S(1)} %collective-permute-done.7.plane_2, ...), custom_call_target="tpu_custom_call" | custom-call | tf_op jit(solution)/shard_map/last/pallas_call | solution.py:307
  31.6 0.1 collective-permute-start.10
  31.7 0.9 %out.1 = bf16[32,256]{1,0:T(8,128)(2,1)} custom-call(bf16[528,128]{1,0:T(8,128)(2,1)S(1)} %get-tuple-element.25.plane_0.mine, bf16[528,128]{1,0:T(8,128)(2,1)S(1)} %collective-permute-done.6.plane_1.peer, f32[4,64,128]{2,1,0:T(8,128)S(1)} %get-tuple-element.26.exact, f32[32,64]{1,0:T(8,128)S(1)} %get-tuple-element.27.own_counts, bf16[2,256,256]{2,1,0:T(8,128)(2,1)S(1)} %copy-done), custom_call_target="tpu_custom_call" | custom-call | tf_op jit(solution)/shard_map/out/pallas_call | solution.py:318
  32.6 0.7 %collective-permute-done.10.theirs = bf16[576,256]{1,0:T(8,128)(2,1)S(1)} collective-permute-done((bf16[576,256]{1,0:T(8,128)(2,1)S(1)}, bf16[576,256]{1,0:T(8,128)(2,1)S(1)}, u32[]{:S(2)}, u32[]{:S(2)}) %collective-permute-start.10) | collective-permute-done | bytes 294944 | tf_op jit(solution)/shard_map/ppermute | solution.py:257
  33.2 0.9 %add.1 = (f32[2,256,256]{2,1,0:T(8,128)}, f32[64,256]{1,0:T(8,128)}) custom-call(bf16[576,256]{1,0:T(8,128)(2,1)S(1)} %get-tuple-element.31.mine, bf16[576,256]{1,0:T(8,128)(2,1)S(1)} %collective-permute-done.10.theirs, f32[64,256]{1,0:T(8,128)S(1)} %get-tuple-element.32.kept), custom_call_target="tpu_custom_call" | custom-call | tf_op jit(solution)/shard_map/add/pallas_call | solution.py:325
  (3 shorter events, 0.1 us)
Async XLA Ops:
  3.0 1.6 %collective-permute-start.1 = (bf16[12,64,128]{2,1,0:T(8,128)(2,1)S(1)}, bf16[12,64,128]{2,1,0:T(8,128)(2,1)S(1)}, u32[]{:S(2)}, u32[]{:S(2)}) collective-permute-start(bf16[12,64,128]{2,1,0:T(8,128)(2,1)S(1)} %get-tuple-element.22), channel_id=1, source_target_pairs={{0,1},{1,0},{2,3},{3,2},{4,5},{5,4},{6,7},{7,6},{8,9},{9,8},{10,11... | collective-permute-start | bytes 589832 | tf_op jit(solution)/shard_map/ppermute | solution.py:257
  4.6 5.3 %collective-permute-start.2 = (bf16[4,64,128]{2,1,0:T(8,128)(2,1)S(1)}, bf16[4,64,128]{2,1,0:T(8,128)(2,1)S(1)}, u32[]{:S(2)}, u32[]{:S(2)}) collective-permute-start(bf16[4,64,128]{2,1,0:T(8,128)(2,1)S(1)} %get-tuple-element.24), channel_id=1, source_target_pairs={{0,2},{1,3},{2,0},{3,1},{4,6},{5,7},{6,4},{7,5},{8,10},{9,11},{10,... | collective-permute-start | bytes 196616 | tf_op jit(solution)/shard_map/ppermute | solution.py:257
  10.0 20.0 %copy-start = (bf16[2,256,256]{2,1,0:T(8,128)(2,1)S(1)}, bf16[2,256,256]{2,1,0:T(8,128)(2,1)}, u32[]{:S(2)}) copy-start(bf16[2,256,256]{2,1,0:T(8,128)(2,1)} %w_second.3) | copy-start | bytes 786436
  10.0 8.9 %collective-permute-start.3 = (bf16[336,128]{1,0:T(8,128)(2,1)S(1)}, bf16[336,128]{1,0:T(8,128)(2,1)S(1)}, u32[]{:S(2)}, u32[]{:S(2)}) collective-permute-start(bf16[336,128]{1,0:T(8,128)(2,1)S(1)} %sum_plane.1.refs_0_), channel_id=1, source_target_pairs={{0,4},{1,5},{2,6},{3,7},{4,0},{5,1},{6,2},{7,3},{8,12},{9,13},{10,... | collective-permute-start | bytes 258056 | tf_op jit(solution)/shard_map/ppermute | solution.py:257
  12.0 7.7 %collective-permute-start.4 = (bf16[336,128]{1,0:T(8,128)(2,1)S(1)}, bf16[336,128]{1,0:T(8,128)(2,1)S(1)}, u32[]{:S(2)}, u32[]{:S(2)}) collective-permute-start(bf16[336,128]{1,0:T(8,128)(2,1)S(1)} %sum_plane.1.refs_0_), channel_id=1, source_target_pairs={{0,8},{1,9},{2,10},{3,11},{4,12},{5,13},{6,14},{7,15},{8,0},{9,1},... | collective-permute-start | bytes 258056 | tf_op jit(solution)/shard_map/ppermute | solution.py:257
  14.6 6.4 %collective-permute-start.5 = (bf16[336,128]{1,0:T(8,128)(2,1)S(1)}, bf16[336,128]{1,0:T(8,128)(2,1)S(1)}, u32[]{:S(2)}, u32[]{:S(2)}) collective-permute-start(bf16[336,128]{1,0:T(8,128)(2,1)S(1)} %sum_plane.1.refs_0_), channel_id=1, source_target_pairs={{0,12},{1,13},{2,14},{3,15},{4,8},{5,9},{6,10},{7,11},{8,4},{9,5},... | collective-permute-start | bytes 258056 | tf_op jit(solution)/shard_map/ppermute | solution.py:257
  14.6 4.3 %collective-permute-start = (bf16[4,64,128]{2,1,0:T(8,128)(2,1)S(1)}, bf16[4,64,128]{2,1,0:T(8,128)(2,1)S(1)}, u32[]{:S(2)}, u32[]{:S(2)}) collective-permute-start(bf16[4,64,128]{2,1,0:T(8,128)(2,1)S(1)} %get-tuple-element.19.x_mine), channel_id=1, source_target_pairs={{0,16},{1,17},{2,18},{3,19},{4,20},{5,21},{6,22},{7,23},{8,24},{9,... | collective-permute-start | bytes 196616 | tf_op jit(solution)/shard_map/ppermute | solution.py:257
  21.0 5.7 %collective-permute-start.6 = (bf16[528,128]{1,0:T(8,128)(2,1)S(1)}, bf16[528,128]{1,0:T(8,128)(2,1)S(1)}, u32[]{:S(2)}, u32[]{:S(2)}) collective-permute-start(bf16[528,128]{1,0:T(8,128)(2,1)S(1)} %get-tuple-element.25.plane_0.mine), channel_id=1, source_target_pairs={{0,16},{1,17},{2,18},{3,19},{4,20},{5,21},{6,22},{7,23},{8,24},{9,... | collective-permute-start | bytes 405512 | tf_op jit(solution)/shard_map/ppermute | solution.py:257
  22.6 5.4 %collective-permute-start.7 = (bf16[528,128]{1,0:T(8,128)(2,1)S(1)}, bf16[528,128]{1,0:T(8,128)(2,1)S(1)}, u32[]{:S(2)}, u32[]{:S(2)}) collective-permute-start(bf16[528,128]{1,0:T(8,128)(2,1)S(1)} %get-tuple-element.25.plane_0.mine), channel_id=1, source_target_pairs={{0,2},{1,3},{2,0},{3,1},{4,6},{5,7},{6,4},{7,5},{8,10},{9,11},{10,... | collective-permute-start | bytes 405512 | tf_op jit(solution)/shard_map/ppermute | solution.py:257
  24.1 5.9 %collective-permute-start.8 = (bf16[528,128]{1,0:T(8,128)(2,1)S(1)}, bf16[528,128]{1,0:T(8,128)(2,1)S(1)}, u32[]{:S(2)}, u32[]{:S(2)}) collective-permute-start(bf16[528,128]{1,0:T(8,128)(2,1)S(1)} %get-tuple-element.25.plane_0.mine), channel_id=1, source_target_pairs={{0,18},{1,19},{2,16},{3,17},{4,22},{5,23},{6,20},{7,21},{8,26},{9,... | collective-permute-start | bytes 405512 | tf_op jit(solution)/shard_map/ppermute | solution.py:257
  24.6 6.3 %collective-permute-start.9 = (bf16[4,64,128]{2,1,0:T(8,128)(2,1)S(1)}, bf16[4,64,128]{2,1,0:T(8,128)(2,1)S(1)}, u32[]{:S(2)}, u32[]{:S(2)}) collective-permute-start(bf16[4,64,128]{2,1,0:T(8,128)(2,1)S(1)} %collective-permute-done.after.x_peer), channel_id=1, source_target_pairs={{0,1},{1,0},{2,3},{3,2},{4,5},{5,4},{6,7},{7,6},{8,9},{9,8},{10,11... | collective-permute-start | bytes 196616 | tf_op jit(solution)/shard_map/ppermute | solution.py:257
  31.6 1.6 %collective-permute-start.10 = (bf16[576,256]{1,0:T(8,128)(2,1)S(1)}, bf16[576,256]{1,0:T(8,128)(2,1)S(1)}, u32[]{:S(2)}, u32[]{:S(2)}) collective-permute-start(bf16[576,256]{1,0:T(8,128)(2,1)S(1)} %get-tuple-element.31.mine), channel_id=1, source_target_pairs={{0,1},{1,0},{2,3},{3,2},{4,5},{5,4},{6,7},{7,6},{8,9},{9,8},{10,11... | collective-permute-start | bytes 884744 | tf_op jit(solution)/shard_map/ppermute | solution.py:257

commit v4 on v3

--- a/solution.py
+++ b/solution.py
@@ -105,6 +105,7 @@
     my_z = lax.axis_index("feat") // 4
     line, width = exact.shape[0], exact.shape[1]
     rows = line * width
+    parts = parts[:1] + parts[:0:-1]
     sums = [part[0:rows, :].astype(F32) for part in parts]
     while len(sums) > 1:
         sums = [a + b for a, b in zip(sums[::2], sums[1::2])]
@@ -287,7 +288,7 @@
         [(block, F32), ((2 * line * width + INTS, LANES), BF16)],
         [ANY] + [VMEM] * line,
         name="sum_line",
-    )(x_peer, message, *[swap(n_feat, message, 4 * z) for z in range(1, line)])
+    )(x_peer, message, *[swap(n_feat, message, 4 * z) for z in range(line - 1, 0, -1)])
     plane = [swap(n_feat, message, r) for r in (n_feat + 2, 2, n_feat)]
     plane = [message, *plane[::-1]]
 

time: 34.3 us -> 34.3 us (level)
  transfers between devices with their start and end apart: 11 -> 11, of which waited for: 9 -> 7; matrix products, arithmetic and copies ran while one was open for 0% -> 0% of each run, Pallas kernels for 5% -> 5%
where the time goes in v4:
time: 34.3 us; the launch traced here: 34.1 us
  waiting for transfers between devices  14.3 us (42%)
  starting transfers between devices  13.4 us (39%)
  Pallas kernels  5.76 us (17%)
  between operations  0.7 us (2%)
    ppermute x11, waiting for transfers between devices, swap(): lax.ppermute(value, AXES, [(d, d ^ relative) for d in range(2 * n_feat)])  14.3 us
    ppermute x11, starting transfers between devices, swap(): lax.ppermute(value, AXES, [(d, d ^ relative) for d in range(2 * n_feat)])  13.4 us
    pallas_call x1, Pallas kernels, pair_body(): call(first_kernel, [((width + INTS, LANES), BF16), (block, BF16), ((2 * l...  2.34 us
    pallas_call x1, Pallas kernels, pair_body(): call(functools.partial(out_kernel, n_feat), [((OWN, HID), BF16)], [VMEM]...  0.9 us
    pallas_call x1, Pallas kernels, pair_body(): call(functools.partial(back_kernel, n_feat), [((half, HID), BF16), ((half...  0.9 us
    pallas_call x1, Pallas kernels, pair_body(): call(add_kernel, [((2, HID, HID), F32), ((width, HID), F32)], [VMEM] * 3,...  0.86 us
  transfers between devices with their start and end apart: 11, of which 7 were waited for; matrix products, arithmetic and copies ran while one was open for 0% of the time, Pallas kernels for 5%

profile of v4, /device:TPU:0, one launch (start us, length us, event | category | flops | bytes accessed | tf_op | source)
XLA Modules:
  0.0 34.1 jit_solution(1972228909296579018)
XLA Ops:
  0.6 2.3 %first.1 = (bf16[80,128]{1,0:T(8,128)(2,1)S(1)}, bf16[4,64,128]{2,1,0:T(8,128)(2,1)S(1)}, f32[8,64,128]{2,1,0:T(8,128)S(1)}, bf16[12,64,128]{2,1,0:T(8,128)(2,1)S(1)}) custom-call(bf16[32,1024]{1,0:T(8,128)(2,1)} %bitcast.5, s32[15,512]{1,0:T(8,128)} %bitcast.6, bf16[64,256]{1,0:T(8,128)(2,1)} %bitcast.7, bf16[32,256]{1,0:T(8,128)(2,1)} %cot_hbm.1, ...), custom_call_target="tpu_custom_call" | custom-call | tf_op jit(solution)/shard_map/first/pallas_call | solution.py:268
  3.0 0.5 %collective-permute-start.1 = (bf16[12,64,128]{2,1,0:T(8,128)(2,1)S(1)}, bf16[12,64,128]{2,1,0:T(8,128)(2,1)S(1)}, u32[]{:S(2)}, u32[]{:S(2)}) collective-permute-start(bf16[12,64,128]{2,1,0:T(8,128)(2,1)S(1)} %get-tuple-element.22), channel_id=1, source_target_pairs={{0,1},{1,0},{2,3},{3,2},{4,5},{5,4},{6,7},{7,6},{8,9},{9,8},{10,11... | collective-permute-start | bytes 589832 | tf_op jit(solution)/shard_map/ppermute | solution.py:258
  3.5 1.1 %collective-permute-done.1.received.x_core = bf16[12,64,128]{2,1,0:T(8,128)(2,1)S(1)} collective-permute-done((bf16[12,64,128]{2,1,0:T(8,128)(2,1)S(1)}, bf16[12,64,128]{2,1,0:T(8,128)(2,1)S(1)}, u32[]{:S(2)}, u32[]{:S(2)}) %collective-permute-start.1) | collective-permute-done | bytes 196640 | tf_op jit(solution)/shard_map/ppermute | solution.py:258
  4.6 3.0 %collective-permute-start.2 = (bf16[4,64,128]{2,1,0:T(8,128)(2,1)S(1)}, bf16[4,64,128]{2,1,0:T(8,128)(2,1)S(1)}, u32[]{:S(2)}, u32[]{:S(2)}) collective-permute-start(bf16[4,64,128]{2,1,0:T(8,128)(2,1)S(1)} %get-tuple-element.24), channel_id=1, source_target_pairs={{0,2},{1,3},{2,0},{3,1},{4,6},{5,7},{6,4},{7,5},{8,10},{9,11},{10,... | collective-permute-start | bytes 196616 | tf_op jit(solution)/shard_map/ppermute | solution.py:258
  7.6 2.4 %collective-permute-done.2.received = bf16[4,64,128]{2,1,0:T(8,128)(2,1)S(1)} collective-permute-done((bf16[4,64,128]{2,1,0:T(8,128)(2,1)S(1)}, bf16[4,64,128]{2,1,0:T(8,128)(2,1)S(1)}, u32[]{:S(2)}, u32[]{:S(2)}) %collective-permute-start.2) | collective-permute-done | bytes 65568 | tf_op jit(solution)/shard_map/ppermute | solution.py:258
  10.0 0.0 copy-start
  10.0 4.0 %collective-permute-start.3 = (bf16[336,128]{1,0:T(8,128)(2,1)S(1)}, bf16[336,128]{1,0:T(8,128)(2,1)S(1)}, u32[]{:S(2)}, u32[]{:S(2)}) collective-permute-start(bf16[336,128]{1,0:T(8,128)(2,1)S(1)} %sum_plane.1.refs_0_), channel_id=1, source_target_pairs={{0,12},{1,13},{2,14},{3,15},{4,8},{5,9},{6,10},{7,11},{8,4},{9,5},... | collective-permute-start | bytes 258056 | tf_op jit(solution)/shard_map/ppermute | solution.py:258
  14.0 0.0 collective-permute-start.4
  14.0 0.6 %collective-permute-start.5 = (bf16[336,128]{1,0:T(8,128)(2,1)S(1)}, bf16[336,128]{1,0:T(8,128)(2,1)S(1)}, u32[]{:S(2)}, u32[]{:S(2)}) collective-permute-start(bf16[336,128]{1,0:T(8,128)(2,1)S(1)} %sum_plane.1.refs_0_), channel_id=1, source_target_pairs={{0,4},{1,5},{2,6},{3,7},{4,0},{5,1},{6,2},{7,3},{8,12},{9,13},{10,... | collective-permute-start | bytes 258056 | tf_op jit(solution)/shard_map/ppermute | solution.py:258
  14.6 1.6 %collective-permute-start = (bf16[4,64,128]{2,1,0:T(8,128)(2,1)S(1)}, bf16[4,64,128]{2,1,0:T(8,128)(2,1)S(1)}, u32[]{:S(2)}, u32[]{:S(2)}) collective-permute-start(bf16[4,64,128]{2,1,0:T(8,128)(2,1)S(1)} %get-tuple-element.19.x_mine), channel_id=1, source_target_pairs={{0,16},{1,17},{2,18},{3,19},{4,20},{5,21},{6,22},{7,23},{8,24},{9,... | collective-permute-start | bytes 196616 | tf_op jit(solution)/shard_map/ppermute | solution.py:258
  16.3 2.6 %collective-permute-done.after.x_peer = bf16[4,64,128]{2,1,0:T(8,128)(2,1)S(1)} collective-permute-done((bf16[4,64,128]{2,1,0:T(8,128)(2,1)S(1)}, bf16[4,64,128]{2,1,0:T(8,128)(2,1)S(1)}, u32[]{:S(2)}, u32[]{:S(2)}) %collective-permute-start) | collective-permute-done | bytes 65568 | tf_op jit(solution)/shard_map/ppermute | solution.py:258
  18.9 0.0 collective-permute-done.3.refs_1_
  18.9 1.6 %collective-permute-done.4.refs_2_ = bf16[336,128]{1,0:T(8,128)(2,1)S(1)} collective-permute-done((bf16[336,128]{1,0:T(8,128)(2,1)S(1)}, bf16[336,128]{1,0:T(8,128)(2,1)S(1)}, u32[]{:S(2)}, u32[]{:S(2)}) %collective-permute-start.4) | collective-permute-done | bytes 86048 | tf_op jit(solution)/shard_map/ppermute | solution.py:258
  20.5 0.0 collective-permute-done.5.refs_3_
  20.6 1.5 %collective-permute-start.6 = (bf16[528,128]{1,0:T(8,128)(2,1)S(1)}, bf16[528,128]{1,0:T(8,128)(2,1)S(1)}, u32[]{:S(2)}, u32[]{:S(2)}) collective-permute-start(bf16[528,128]{1,0:T(8,128)(2,1)S(1)} %get-tuple-element.25.plane_0.mine), channel_id=1, source_target_pairs={{0,16},{1,17},{2,18},{3,19},{4,20},{5,21},{6,22},{7,23},{8,24},{9,... | collective-permute-start | bytes 405512 | tf_op jit(solution)/shard_map/ppermute | solution.py:258
  22.1 1.5 %collective-permute-start.7 = (bf16[528,128]{1,0:T(8,128)(2,1)S(1)}, bf16[528,128]{1,0:T(8,128)(2,1)S(1)}, u32[]{:S(2)}, u32[]{:S(2)}) collective-permute-start(bf16[528,128]{1,0:T(8,128)(2,1)S(1)} %get-tuple-element.25.plane_0.mine), channel_id=1, source_target_pairs={{0,2},{1,3},{2,0},{3,1},{4,6},{5,7},{6,4},{7,5},{8,10},{9,11},{10,... | collective-permute-start | bytes 405512 | tf_op jit(solution)/shard_map/ppermute | solution.py:258
  23.6 0.5 %collective-permute-start.8 = (bf16[528,128]{1,0:T(8,128)(2,1)S(1)}, bf16[528,128]{1,0:T(8,128)(2,1)S(1)}, u32[]{:S(2)}, u32[]{:S(2)}) collective-permute-start(bf16[528,128]{1,0:T(8,128)(2,1)S(1)} %get-tuple-element.25.plane_0.mine), channel_id=1, source_target_pairs={{0,18},{1,19},{2,16},{3,17},{4,22},{5,23},{6,20},{7,21},{8,26},{9,... | collective-permute-start | bytes 405512 | tf_op jit(solution)/shard_map/ppermute | solution.py:258
  24.1 0.0 collective-permute-start.9
  24.1 2.1 %collective-permute-done.6.plane_1.peer = bf16[528,128]{1,0:T(8,128)(2,1)S(1)} collective-permute-done((bf16[528,128]{1,0:T(8,128)(2,1)S(1)}, bf16[528,128]{1,0:T(8,128)(2,1)S(1)}, u32[]{:S(2)}, u32[]{:S(2)}) %collective-permute-start.6) | collective-permute-done | bytes 135200 | tf_op jit(solution)/shard_map/ppermute | solution.py:258
  26.2 3.8 %collective-permute-done.7.plane_2 = bf16[528,128]{1,0:T(8,128)(2,1)S(1)} collective-permute-done((bf16[528,128]{1,0:T(8,128)(2,1)S(1)}, bf16[528,128]{1,0:T(8,128)(2,1)S(1)}, u32[]{:S(2)}, u32[]{:S(2)}) %collective-permute-start.7) | collective-permute-done | bytes 135200 | tf_op jit(solution)/shard_map/ppermute | solution.py:258
  30.0 0.0 collective-permute-done.8.plane_3
  30.0 0.0 copy-done
  30.0 0.9 %back.1 = (bf16[512,256]{1,0:T(8,128)(2,1)S(1)}, bf16[512,256]{1,0:T(8,128)(2,1)S(1)}, f32[512,256]{1,0:T(8,128)S(1)}, f32[32,64]{1,0:T(8,128)S(1)}) custom-call(bf16[528,128]{1,0:T(8,128)(2,1)S(1)} %get-tuple-element.25.plane_0.mine, bf16[528,128]{1,0:T(8,128)(2,1)S(1)} %collective-permute-done.6.plane_1.peer, ...), custom_call_target="tpu_custom_call" | custom-call | tf_op jit(solution)/shard_map/back/pallas_call | solution.py:296
  30.9 0.0 collective-permute-done.9.x_last
  30.9 0.7 %last.1 = (bf16[576,256]{1,0:T(8,128)(2,1)S(1)}, f32[64,256]{1,0:T(8,128)S(1)}) custom-call(bf16[528,128]{1,0:T(8,128)(2,1)S(1)} %get-tuple-element.25.plane_0.mine, bf16[528,128]{1,0:T(8,128)(2,1)S(1)} %collective-permute-done.6.plane_1.peer, bf16[528,128]{1,0:T(8,128)(2,1)S(1)} %collective-permute-done.7.plane_2, ...), custom_call_target="tpu_custom_call" | custom-call | tf_op jit(solution)/shard_map/last/pallas_call | solution.py:308
  31.6 0.1 collective-permute-start.10
  31.7 0.9 %out.1 = bf16[32,256]{1,0:T(8,128)(2,1)} custom-call(bf16[528,128]{1,0:T(8,128)(2,1)S(1)} %get-tuple-element.25.plane_0.mine, bf16[528,128]{1,0:T(8,128)(2,1)S(1)} %collective-permute-done.6.plane_1.peer, f32[4,64,128]{2,1,0:T(8,128)S(1)} %get-tuple-element.26.exact, f32[32,64]{1,0:T(8,128)S(1)} %get-tuple-element.27.own_counts, bf16[2,256,256]{2,1,0:T(8,128)(2,1)S(1)} %copy-done), custom_call_target="tpu_custom_call" | custom-call | tf_op jit(solution)/shard_map/out/pallas_call | solution.py:319
  32.6 0.7 %collective-permute-done.10.theirs = bf16[576,256]{1,0:T(8,128)(2,1)S(1)} collective-permute-done((bf16[576,256]{1,0:T(8,128)(2,1)S(1)}, bf16[576,256]{1,0:T(8,128)(2,1)S(1)}, u32[]{:S(2)}, u32[]{:S(2)}) %collective-permute-start.10) | collective-permute-done | bytes 294944 | tf_op jit(solution)/shard_map/ppermute | solution.py:258
  33.3 0.9 %add.1 = (f32[2,256,256]{2,1,0:T(8,128)}, f32[64,256]{1,0:T(8,128)}) custom-call(bf16[576,256]{1,0:T(8,128)(2,1)S(1)} %get-tuple-element.31.mine, bf16[576,256]{1,0:T(8,128)(2,1)S(1)} %collective-permute-done.10.theirs, f32[64,256]{1,0:T(8,128)S(1)} %get-tuple-element.32.kept), custom_call_target="tpu_custom_call" | custom-call | tf_op jit(solution)/shard_map/add/pallas_call | solution.py:326
  (3 shorter events, 0.1 us)
Async XLA Ops:
  3.0 1.6 %collective-permute-start.1 = (bf16[12,64,128]{2,1,0:T(8,128)(2,1)S(1)}, bf16[12,64,128]{2,1,0:T(8,128)(2,1)S(1)}, u32[]{:S(2)}, u32[]{:S(2)}) collective-permute-start(bf16[12,64,128]{2,1,0:T(8,128)(2,1)S(1)} %get-tuple-element.22), channel_id=1, source_target_pairs={{0,1},{1,0},{2,3},{3,2},{4,5},{5,4},{6,7},{7,6},{8,9},{9,8},{10,11... | collective-permute-start | bytes 589832 | tf_op jit(solution)/shard_map/ppermute | solution.py:258
  4.6 5.3 %collective-permute-start.2 = (bf16[4,64,128]{2,1,0:T(8,128)(2,1)S(1)}, bf16[4,64,128]{2,1,0:T(8,128)(2,1)S(1)}, u32[]{:S(2)}, u32[]{:S(2)}) collective-permute-start(bf16[4,64,128]{2,1,0:T(8,128)(2,1)S(1)} %get-tuple-element.24), channel_id=1, source_target_pairs={{0,2},{1,3},{2,0},{3,1},{4,6},{5,7},{6,4},{7,5},{8,10},{9,11},{10,... | collective-permute-start | bytes 196616 | tf_op jit(solution)/shard_map/ppermute | solution.py:258
  10.0 20.1 %copy-start = (bf16[2,256,256]{2,1,0:T(8,128)(2,1)S(1)}, bf16[2,256,256]{2,1,0:T(8,128)(2,1)}, u32[]{:S(2)}) copy-start(bf16[2,256,256]{2,1,0:T(8,128)(2,1)} %w_second.3) | copy-start | bytes 786436
  10.0 8.9 %collective-permute-start.3 = (bf16[336,128]{1,0:T(8,128)(2,1)S(1)}, bf16[336,128]{1,0:T(8,128)(2,1)S(1)}, u32[]{:S(2)}, u32[]{:S(2)}) collective-permute-start(bf16[336,128]{1,0:T(8,128)(2,1)S(1)} %sum_plane.1.refs_0_), channel_id=1, source_target_pairs={{0,12},{1,13},{2,14},{3,15},{4,8},{5,9},{6,10},{7,11},{8,4},{9,5},... | collective-permute-start | bytes 258056 | tf_op jit(solution)/shard_map/ppermute | solution.py:258
  14.0 6.5 %collective-permute-start.4 = (bf16[336,128]{1,0:T(8,128)(2,1)S(1)}, bf16[336,128]{1,0:T(8,128)(2,1)S(1)}, u32[]{:S(2)}, u32[]{:S(2)}) collective-permute-start(bf16[336,128]{1,0:T(8,128)(2,1)S(1)} %sum_plane.1.refs_0_), channel_id=1, source_target_pairs={{0,8},{1,9},{2,10},{3,11},{4,12},{5,13},{6,14},{7,15},{8,0},{9,1},... | collective-permute-start | bytes 258056 | tf_op jit(solution)/shard_map/ppermute | solution.py:258
  14.0 6.5 %collective-permute-start.5 = (bf16[336,128]{1,0:T(8,128)(2,1)S(1)}, bf16[336,128]{1,0:T(8,128)(2,1)S(1)}, u32[]{:S(2)}, u32[]{:S(2)}) collective-permute-start(bf16[336,128]{1,0:T(8,128)(2,1)S(1)} %sum_plane.1.refs_0_), channel_id=1, source_target_pairs={{0,4},{1,5},{2,6},{3,7},{4,0},{5,1},{6,2},{7,3},{8,12},{9,13},{10,... | collective-permute-start | bytes 258056 | tf_op jit(solution)/shard_map/ppermute | solution.py:258
  14.6 4.3 %collective-permute-start = (bf16[4,64,128]{2,1,0:T(8,128)(2,1)S(1)}, bf16[4,64,128]{2,1,0:T(8,128)(2,1)S(1)}, u32[]{:S(2)}, u32[]{:S(2)}) collective-permute-start(bf16[4,64,128]{2,1,0:T(8,128)(2,1)S(1)} %get-tuple-element.19.x_mine), channel_id=1, source_target_pairs={{0,16},{1,17},{2,18},{3,19},{4,20},{5,21},{6,22},{7,23},{8,24},{9,... | collective-permute-start | bytes 196616 | tf_op jit(solution)/shard_map/ppermute | solution.py:258
  20.6 5.7 %collective-permute-start.6 = (bf16[528,128]{1,0:T(8,128)(2,1)S(1)}, bf16[528,128]{1,0:T(8,128)(2,1)S(1)}, u32[]{:S(2)}, u32[]{:S(2)}) collective-permute-start(bf16[528,128]{1,0:T(8,128)(2,1)S(1)} %get-tuple-element.25.plane_0.mine), channel_id=1, source_target_pairs={{0,16},{1,17},{2,18},{3,19},{4,20},{5,21},{6,22},{7,23},{8,24},{9,... | collective-permute-start | bytes 405512 | tf_op jit(solution)/shard_map/ppermute | solution.py:258
  22.1 7.9 %collective-permute-start.7 = (bf16[528,128]{1,0:T(8,128)(2,1)S(1)}, bf16[528,128]{1,0:T(8,128)(2,1)S(1)}, u32[]{:S(2)}, u32[]{:S(2)}) collective-permute-start(bf16[528,128]{1,0:T(8,128)(2,1)S(1)} %get-tuple-element.25.plane_0.mine), channel_id=1, source_target_pairs={{0,2},{1,3},{2,0},{3,1},{4,6},{5,7},{6,4},{7,5},{8,10},{9,11},{10,... | collective-permute-start | bytes 405512 | tf_op jit(solution)/shard_map/ppermute | solution.py:258
  23.6 6.4 %collective-permute-start.8 = (bf16[528,128]{1,0:T(8,128)(2,1)S(1)}, bf16[528,128]{1,0:T(8,128)(2,1)S(1)}, u32[]{:S(2)}, u32[]{:S(2)}) collective-permute-start(bf16[528,128]{1,0:T(8,128)(2,1)S(1)} %get-tuple-element.25.plane_0.mine), channel_id=1, source_target_pairs={{0,18},{1,19},{2,16},{3,17},{4,22},{5,23},{6,20},{7,21},{8,26},{9,... | collective-permute-start | bytes 405512 | tf_op jit(solution)/shard_map/ppermute | solution.py:258
  24.1 6.8 %collective-permute-start.9 = (bf16[4,64,128]{2,1,0:T(8,128)(2,1)S(1)}, bf16[4,64,128]{2,1,0:T(8,128)(2,1)S(1)}, u32[]{:S(2)}, u32[]{:S(2)}) collective-permute-start(bf16[4,64,128]{2,1,0:T(8,128)(2,1)S(1)} %collective-permute-done.after.x_peer), channel_id=1, source_target_pairs={{0,1},{1,0},{2,3},{3,2},{4,5},{5,4},{6,7},{7,6},{8,9},{9,8},{10,11... | collective-permute-start | bytes 196616 | tf_op jit(solution)/shard_map/ppermute | solution.py:258
  31.6 1.6 %collective-permute-start.10 = (bf16[576,256]{1,0:T(8,128)(2,1)S(1)}, bf16[576,256]{1,0:T(8,128)(2,1)S(1)}, u32[]{:S(2)}, u32[]{:S(2)}) collective-permute-start(bf16[576,256]{1,0:T(8,128)(2,1)S(1)} %get-tuple-element.31.mine), channel_id=1, source_target_pairs={{0,1},{1,0},{2,3},{3,2},{4,5},{5,4},{6,7},{7,6},{8,9},{9,8},{10,11... | collective-permute-start | bytes 884744 | tf_op jit(solution)/shard_map/ppermute | solution.py:258

commit v5 on v3

--- a/solution.py
+++ b/solution.py
@@ -119,7 +119,7 @@
     message[2 * rows :, :] = functools.reduce(lambda a, b: a + b, lists).astype(BF16)
 
 
-def back_kernel(n_feat, plane_0, plane_1, plane_2, plane_3, w_second, cot_all, near_cot, d_hidden, own_counts, lists, spread, turn):
+def write_back(n_feat, plane_0, plane_1, plane_2, plane_3, w_second, cot_all, near_cot, d_hidden, own_counts, lists, spread, turn):
     line = n_feat // 4
     width = 2 * OWN
     my_graph = lax.axis_index("graph")
@@ -172,13 +172,13 @@
     d_hidden[...] = part + dot(near_cot[...], w_second[1], ((1,), (1,)))
 
 
-def out_kernel(n_feat, mine, peer, exact, own_counts, w_second, layer_out, ext):
+def out_kernel(n_feat, peer, exact, own_counts, w_second, layer_out, ext):
     my_graph = lax.axis_index("graph")
     my_z = lax.axis_index("feat") // 4
     own = exact[pl.ds(my_z, 1)][0]
-    other = peer[pl.ds(pl.multiple_of(my_z * 4 * OWN, 4 * OWN), 2 * OWN), :].astype(F32)
+    far = peer[pl.ds(pl.multiple_of(my_z * 4 * OWN, 4 * OWN), 2 * OWN), :].astype(F32)
     hiddens = []
-    for value in (own, other):
+    for value in (own, far):
         value = jnp.concatenate([value[0:OWN, :], value[OWN : 2 * OWN, :]], axis=1)
         hiddens.append((value * (0.5 + 0.5 * jnp.tanh(0.5 * value))).astype(BF16))
     ext[pl.ds(pl.multiple_of(my_graph * OWN, OWN), OWN), :] = hiddens[0]
@@ -189,9 +189,10 @@
 
 
 def last_kernel(
-    n_feat, plane_0, plane_1, plane_2, plane_3, cot, near_cot, d_hidden, x_mine, x_core, x_peer, x_last,
-    swapped, kept, hidden, d_pre, slices,
+    n_feat, plane_0, plane_1, plane_2, plane_3, w_second, x_mine, x_core, x_peer, x_last,
+    own_counts, swapped, kept, cot, near_cot, d_hidden, lists, spread, turn, hidden, d_pre, slices,
 ):
+    write_back(n_feat, plane_0, plane_1, plane_2, plane_3, w_second, cot, near_cot, d_hidden, own_counts, lists, spread, turn)
     my_graph = lax.axis_index("graph")
     my_feat = lax.axis_index("feat")
     rows = n_feat * OWN
@@ -292,36 +293,30 @@
     plane = [message, *plane[::-1]]
 
     half = (devices // 2) * OWN
-    cot, near_cot, d_hidden, own_counts = call(
-        functools.partial(back_kernel, n_feat),
-        [((half, HID), BF16), ((half, HID), BF16), ((half, HID), F32), ((OWN, width), F32)],
-        [VMEM] * 5,
+    own_counts, swapped, kept = call(
+        functools.partial(last_kernel, n_feat),
+        [((OWN, width), F32), ((2 * HID + width, HID), BF16), ((width, HID), F32)],
+        [VMEM] * 9,
         [
+            pltpu.VMEM((half, HID), BF16),
+            pltpu.VMEM((half, HID), BF16),
+            pltpu.VMEM((half, HID), F32),
             pltpu.VMEM((4, INTS, LANES), BF16),
             pltpu.VMEM((4, width, LANES), F32),
             pltpu.VMEM((LANES, width), F32),
-        ],
-        name="back",
-    )(*plane, w_second)
-
-    swapped, kept = call(
-        functools.partial(last_kernel, n_feat),
-        [((2 * HID + width, HID), BF16), ((width, HID), F32)],
-        [VMEM] * 11,
-        [
             pltpu.VMEM((half, HID), BF16),
             pltpu.VMEM((2 * half, HID), BF16),
             pltpu.VMEM((2, 2 * width, rows), BF16),
         ],
         name="last",
-    )(*plane, cot, near_cot, d_hidden, x_mine, x_core, x_peer, x_last)
+    )(*plane, w_second, x_mine, x_core, x_peer, x_last)
     (layer_out,) = call(
         functools.partial(out_kernel, n_feat),
         [((OWN, HID), BF16)],
-        [VMEM] * 5,
+        [VMEM] * 4,
         [pltpu.VMEM((width, HID), BF16)],
         name="out",
-    )(message, plane[1], exact, own_counts, w_second)
+    )(plane[1], exact, own_counts, w_second)
     grad_second, grad_first = call(
         add_kernel,
         [((2, HID, HID), F32), ((width, HID), F32)],

time: 34.3 us -> 33.6 us (0.980)
  waiting for transfers between devices: 14.2 us -> 13.7 us
    ppermute x11, waiting for transfers between devices: 14.2 us -> 13.7 us  [swap(): lax.ppermute(value, AXES, [(d, d ^ relative) for d in range(2 * n_feat)])]
    pallas_call x2 -> x1, Pallas kernels: 1.57 us -> 1.54 us  [pair_body(): call(functools.partial(last_kernel, n_feat), [((OWN, width), F32), ((2 *...]
  transfers between devices with their start and end apart: 11 -> 11, of which waited for: 9 -> 9; matrix products, arithmetic and copies ran while one was open for 0% -> 0% of each run, Pallas kernels for 5% -> 3%
where the time goes in v5:
time: 33.6 us; the launch traced here: 33.5 us
  waiting for transfers between devices  13.7 us (41%)
  starting transfers between devices  13.4 us (40%)
  Pallas kernels  5.74 us (17%)
  between operations  0.68 us (2%)
    ppermute x11, waiting for transfers between devices, swap(): lax.ppermute(value, AXES, [(d, d ^ relative) for d in range(2 * n_feat)])  13.7 us
    ppermute x11, starting transfers between devices, swap(): lax.ppermute(value, AXES, [(d, d ^ relative) for d in range(2 * n_feat)])  13.4 us
    pallas_call x1, Pallas kernels, pair_body(): call(first_kernel, [((width + INTS, LANES), BF16), (block, BF16), ((2 * l...  2.34 us
    pallas_call x1, Pallas kernels, pair_body(): call(functools.partial(last_kernel, n_feat), [((OWN, width), F32), ((2 *...  1.54 us
    pallas_call x1, Pallas kernels, pair_body(): call(functools.partial(out_kernel, n_feat), [((OWN, HID), BF16)], [VMEM]...  0.9 us
    pallas_call x1, Pallas kernels, pair_body(): call(add_kernel, [((2, HID, HID), F32), ((width, HID), F32)], [VMEM] * 3,...  0.87 us
  transfers between devices with their start and end apart: 11, of which 9 were waited for; matrix products, arithmetic and copies ran while one was open for 0% of the time, Pallas kernels for 3%

profile of v5, /device:TPU:0, one launch (start us, length us, event | category | flops | bytes accessed | tf_op | source)
XLA Modules:
  0.0 33.5 jit_solution(10425594605967346792)
XLA Ops:
  0.6 2.3 %first.1 = (bf16[80,128]{1,0:T(8,128)(2,1)S(1)}, bf16[4,64,128]{2,1,0:T(8,128)(2,1)S(1)}, f32[8,64,128]{2,1,0:T(8,128)S(1)}, bf16[12,64,128]{2,1,0:T(8,128)(2,1)S(1)}) custom-call(bf16[32,1024]{1,0:T(8,128)(2,1)} %bitcast.5, s32[15,512]{1,0:T(8,128)} %bitcast.6, bf16[64,256]{1,0:T(8,128)(2,1)} %bitcast.7, bf16[32,256]{1,0:T(8,128)(2,1)} %cot_hbm.1, ...), custom_call_target="tpu_custom_call" | custom-call | tf_op jit(solution)/shard_map/first/pallas_call | solution.py:268
  3.0 0.5 %collective-permute-start.1 = (bf16[12,64,128]{2,1,0:T(8,128)(2,1)S(1)}, bf16[12,64,128]{2,1,0:T(8,128)(2,1)S(1)}, u32[]{:S(2)}, u32[]{:S(2)}) collective-permute-start(bf16[12,64,128]{2,1,0:T(8,128)(2,1)S(1)} %get-tuple-element.19), channel_id=1, source_target_pairs={{0,1},{1,0},{2,3},{3,2},{4,5},{5,4},{6,7},{7,6},{8,9},{9,8},{10,11... | collective-permute-start | bytes 589832 | tf_op jit(solution)/shard_map/ppermute | solution.py:258
  3.5 1.1 %collective-permute-done.1.received.x_core = bf16[12,64,128]{2,1,0:T(8,128)(2,1)S(1)} collective-permute-done((bf16[12,64,128]{2,1,0:T(8,128)(2,1)S(1)}, bf16[12,64,128]{2,1,0:T(8,128)(2,1)S(1)}, u32[]{:S(2)}, u32[]{:S(2)}) %collective-permute-start.1) | collective-permute-done | bytes 196640 | tf_op jit(solution)/shard_map/ppermute | solution.py:258
  4.6 3.0 %collective-permute-start.2 = (bf16[4,64,128]{2,1,0:T(8,128)(2,1)S(1)}, bf16[4,64,128]{2,1,0:T(8,128)(2,1)S(1)}, u32[]{:S(2)}, u32[]{:S(2)}) collective-permute-start(bf16[4,64,128]{2,1,0:T(8,128)(2,1)S(1)} %get-tuple-element.21), channel_id=1, source_target_pairs={{0,2},{1,3},{2,0},{3,1},{4,6},{5,7},{6,4},{7,5},{8,10},{9,11},{10,... | collective-permute-start | bytes 196616 | tf_op jit(solution)/shard_map/ppermute | solution.py:258
  7.6 2.4 %collective-permute-done.2.received = bf16[4,64,128]{2,1,0:T(8,128)(2,1)S(1)} collective-permute-done((bf16[4,64,128]{2,1,0:T(8,128)(2,1)S(1)}, bf16[4,64,128]{2,1,0:T(8,128)(2,1)S(1)}, u32[]{:S(2)}, u32[]{:S(2)}) %collective-permute-start.2) | collective-permute-done | bytes 65568 | tf_op jit(solution)/shard_map/ppermute | solution.py:258
  10.0 0.0 copy-start
  10.0 4.0 %collective-permute-start.5 = (bf16[336,128]{1,0:T(8,128)(2,1)S(1)}, bf16[336,128]{1,0:T(8,128)(2,1)S(1)}, u32[]{:S(2)}, u32[]{:S(2)}) collective-permute-start(bf16[336,128]{1,0:T(8,128)(2,1)S(1)} %sum_plane.1.refs_0_), channel_id=1, source_target_pairs={{0,12},{1,13},{2,14},{3,15},{4,8},{5,9},{6,10},{7,11},{8,4},{9,5},... | collective-permute-start | bytes 258056 | tf_op jit(solution)/shard_map/ppermute | solution.py:258
  14.0 0.0 collective-permute-start.4
  14.0 0.6 %collective-permute-start.3 = (bf16[336,128]{1,0:T(8,128)(2,1)S(1)}, bf16[336,128]{1,0:T(8,128)(2,1)S(1)}, u32[]{:S(2)}, u32[]{:S(2)}) collective-permute-start(bf16[336,128]{1,0:T(8,128)(2,1)S(1)} %sum_plane.1.refs_0_), channel_id=1, source_target_pairs={{0,4},{1,5},{2,6},{3,7},{4,0},{5,1},{6,2},{7,3},{8,12},{9,13},{10,... | collective-permute-start | bytes 258056 | tf_op jit(solution)/shard_map/ppermute | solution.py:258
  14.6 1.6 %collective-permute-start = (bf16[4,64,128]{2,1,0:T(8,128)(2,1)S(1)}, bf16[4,64,128]{2,1,0:T(8,128)(2,1)S(1)}, u32[]{:S(2)}, u32[]{:S(2)}) collective-permute-start(bf16[4,64,128]{2,1,0:T(8,128)(2,1)S(1)} %get-tuple-element.16.x_mine), channel_id=1, source_target_pairs={{0,16},{1,17},{2,18},{3,19},{4,20},{5,21},{6,22},{7,23},{8,24},{9,... | collective-permute-start | bytes 196616 | tf_op jit(solution)/shard_map/ppermute | solution.py:258
  16.3 2.6 %collective-permute-done.after.x_peer = bf16[4,64,128]{2,1,0:T(8,128)(2,1)S(1)} collective-permute-done((bf16[4,64,128]{2,1,0:T(8,128)(2,1)S(1)}, bf16[4,64,128]{2,1,0:T(8,128)(2,1)S(1)}, u32[]{:S(2)}, u32[]{:S(2)}) %collective-permute-start) | collective-permute-done | bytes 65568 | tf_op jit(solution)/shard_map/ppermute | solution.py:258
  18.9 0.0 collective-permute-done.5.refs_3_
  18.9 1.6 %collective-permute-done.4.refs_2_ = bf16[336,128]{1,0:T(8,128)(2,1)S(1)} collective-permute-done((bf16[336,128]{1,0:T(8,128)(2,1)S(1)}, bf16[336,128]{1,0:T(8,128)(2,1)S(1)}, u32[]{:S(2)}, u32[]{:S(2)}) %collective-permute-start.4) | collective-permute-done | bytes 86048 | tf_op jit(solution)/shard_map/ppermute | solution.py:258
  20.5 0.0 collective-permute-done.3.refs_1_
  20.6 2.5 %collective-permute-start.8 = (bf16[528,128]{1,0:T(8,128)(2,1)S(1)}, bf16[528,128]{1,0:T(8,128)(2,1)S(1)}, u32[]{:S(2)}, u32[]{:S(2)}) collective-permute-start(bf16[528,128]{1,0:T(8,128)(2,1)S(1)} %get-tuple-element.22.plane_0), channel_id=1, source_target_pairs={{0,18},{1,19},{2,16},{3,17},{4,22},{5,23},{6,20},{7,21},{8,26},{9,... | collective-permute-start | bytes 405512 | tf_op jit(solution)/shard_map/ppermute | solution.py:258
  23.1 0.5 %collective-permute-start.7 = (bf16[528,128]{1,0:T(8,128)(2,1)S(1)}, bf16[528,128]{1,0:T(8,128)(2,1)S(1)}, u32[]{:S(2)}, u32[]{:S(2)}) collective-permute-start(bf16[528,128]{1,0:T(8,128)(2,1)S(1)} %get-tuple-element.22.plane_0), channel_id=1, source_target_pairs={{0,2},{1,3},{2,0},{3,1},{4,6},{5,7},{6,4},{7,5},{8,10},{9,11},{10,... | collective-permute-start | bytes 405512 | tf_op jit(solution)/shard_map/ppermute | solution.py:258
  23.6 0.5 %collective-permute-start.6 = (bf16[528,128]{1,0:T(8,128)(2,1)S(1)}, bf16[528,128]{1,0:T(8,128)(2,1)S(1)}, u32[]{:S(2)}, u32[]{:S(2)}) collective-permute-start(bf16[528,128]{1,0:T(8,128)(2,1)S(1)} %get-tuple-element.22.plane_0), channel_id=1, source_target_pairs={{0,16},{1,17},{2,18},{3,19},{4,20},{5,21},{6,22},{7,23},{8,24},{9,... | collective-permute-start | bytes 405512 | tf_op jit(solution)/shard_map/ppermute | solution.py:258
  24.1 0.0 collective-permute-start.9
  24.1 1.3 %collective-permute-done.9.x_last = bf16[4,64,128]{2,1,0:T(8,128)(2,1)S(1)} collective-permute-done((bf16[4,64,128]{2,1,0:T(8,128)(2,1)S(1)}, bf16[4,64,128]{2,1,0:T(8,128)(2,1)S(1)}, u32[]{:S(2)}, u32[]{:S(2)}) %collective-permute-start.9) | collective-permute-done | bytes 65568 | tf_op jit(solution)/shard_map/ppermute | solution.py:258
  25.4 1.7 %collective-permute-done.8.plane_3 = bf16[528,128]{1,0:T(8,128)(2,1)S(1)} collective-permute-done((bf16[528,128]{1,0:T(8,128)(2,1)S(1)}, bf16[528,128]{1,0:T(8,128)(2,1)S(1)}, u32[]{:S(2)}, u32[]{:S(2)}) %collective-permute-start.8) | collective-permute-done | bytes 135200 | tf_op jit(solution)/shard_map/ppermute | solution.py:258
  27.1 2.3 %collective-permute-done.7.plane_2 = bf16[528,128]{1,0:T(8,128)(2,1)S(1)} collective-permute-done((bf16[528,128]{1,0:T(8,128)(2,1)S(1)}, bf16[528,128]{1,0:T(8,128)(2,1)S(1)}, u32[]{:S(2)}, u32[]{:S(2)}) %collective-permute-start.7) | collective-permute-done | bytes 135200 | tf_op jit(solution)/shard_map/ppermute | solution.py:258
  29.4 0.1 collective-permute-done.6.plane_1.peer
  29.4 0.0 copy-done
  29.4 1.5 %last.1 = (f32[32,64]{1,0:T(8,128)S(1)}, bf16[576,256]{1,0:T(8,128)(2,1)S(1)}, f32[64,256]{1,0:T(8,128)S(1)}) custom-call(bf16[528,128]{1,0:T(8,128)(2,1)S(1)} %get-tuple-element.22.plane_0, bf16[528,128]{1,0:T(8,128)(2,1)S(1)} %collective-permute-done.6.plane_1.peer, bf16[528,128]{1,0:T(8,128)(2,1)S(1)} %collective-permute-done.7.plane_2, ...), custom_call_target="tpu_custom_call" | custom-call | tf_op jit(solution)/shard_map/last/pallas_call | solution.py:296
  31.0 0.1 collective-permute-start.10
  31.0 0.9 %out.1 = bf16[32,256]{1,0:T(8,128)(2,1)} custom-call(bf16[528,128]{1,0:T(8,128)(2,1)S(1)} %collective-permute-done.6.plane_1.peer, f32[4,64,128]{2,1,0:T(8,128)S(1)} %get-tuple-element.23.exact, f32[32,64]{1,0:T(8,128)S(1)} %get-tuple-element.24.own_counts, bf16[2,256,256]{2,1,0:T(8,128)(2,1)S(1)} %copy-done), custom_call_target="tpu_custom_call" | custom-call | tf_op jit(solution)/shard_map/out/pallas_call | solution.py:313
  31.9 0.7 %collective-permute-done.10.theirs = bf16[576,256]{1,0:T(8,128)(2,1)S(1)} collective-permute-done((bf16[576,256]{1,0:T(8,128)(2,1)S(1)}, bf16[576,256]{1,0:T(8,128)(2,1)S(1)}, u32[]{:S(2)}, u32[]{:S(2)}) %collective-permute-start.10) | collective-permute-done | bytes 294944 | tf_op jit(solution)/shard_map/ppermute | solution.py:258
  32.6 0.9 %add.1 = (f32[2,256,256]{2,1,0:T(8,128)}, f32[64,256]{1,0:T(8,128)}) custom-call(bf16[576,256]{1,0:T(8,128)(2,1)S(1)} %get-tuple-element.25.mine, bf16[576,256]{1,0:T(8,128)(2,1)S(1)} %collective-permute-done.10.theirs, f32[64,256]{1,0:T(8,128)S(1)} %get-tuple-element.26.kept), custom_call_target="tpu_custom_call" | custom-call | tf_op jit(solution)/shard_map/add/pallas_call | solution.py:320
  (3 shorter events, 0.1 us)
Async XLA Ops:
  3.0 1.6 %collective-permute-start.1 = (bf16[12,64,128]{2,1,0:T(8,128)(2,1)S(1)}, bf16[12,64,128]{2,1,0:T(8,128)(2,1)S(1)}, u32[]{:S(2)}, u32[]{:S(2)}) collective-permute-start(bf16[12,64,128]{2,1,0:T(8,128)(2,1)S(1)} %get-tuple-element.19), channel_id=1, source_target_pairs={{0,1},{1,0},{2,3},{3,2},{4,5},{5,4},{6,7},{7,6},{8,9},{9,8},{10,11... | collective-permute-start | bytes 589832 | tf_op jit(solution)/shard_map/ppermute | solution.py:258
  4.6 5.3 %collective-permute-start.2 = (bf16[4,64,128]{2,1,0:T(8,128)(2,1)S(1)}, bf16[4,64,128]{2,1,0:T(8,128)(2,1)S(1)}, u32[]{:S(2)}, u32[]{:S(2)}) collective-permute-start(bf16[4,64,128]{2,1,0:T(8,128)(2,1)S(1)} %get-tuple-element.21), channel_id=1, source_target_pairs={{0,2},{1,3},{2,0},{3,1},{4,6},{5,7},{6,4},{7,5},{8,10},{9,11},{10,... | collective-permute-start | bytes 196616 | tf_op jit(solution)/shard_map/ppermute | solution.py:258
  10.0 19.4 %copy-start = (bf16[2,256,256]{2,1,0:T(8,128)(2,1)S(1)}, bf16[2,256,256]{2,1,0:T(8,128)(2,1)}, u32[]{:S(2)}) copy-start(bf16[2,256,256]{2,1,0:T(8,128)(2,1)} %w_second.3) | copy-start | bytes 786436
  10.0 8.9 %collective-permute-start.5 = (bf16[336,128]{1,0:T(8,128)(2,1)S(1)}, bf16[336,128]{1,0:T(8,128)(2,1)S(1)}, u32[]{:S(2)}, u32[]{:S(2)}) collective-permute-start(bf16[336,128]{1,0:T(8,128)(2,1)S(1)} %sum_plane.1.refs_0_), channel_id=1, source_target_pairs={{0,12},{1,13},{2,14},{3,15},{4,8},{5,9},{6,10},{7,11},{8,4},{9,5},... | collective-permute-start | bytes 258056 | tf_op jit(solution)/shard_map/ppermute | solution.py:258
  14.0 6.5 %collective-permute-start.4 = (bf16[336,128]{1,0:T(8,128)(2,1)S(1)}, bf16[336,128]{1,0:T(8,128)(2,1)S(1)}, u32[]{:S(2)}, u32[]{:S(2)}) collective-permute-start(bf16[336,128]{1,0:T(8,128)(2,1)S(1)} %sum_plane.1.refs_0_), channel_id=1, source_target_pairs={{0,8},{1,9},{2,10},{3,11},{4,12},{5,13},{6,14},{7,15},{8,0},{9,1},... | collective-permute-start | bytes 258056 | tf_op jit(solution)/shard_map/ppermute | solution.py:258
  14.0 6.5 %collective-permute-start.3 = (bf16[336,128]{1,0:T(8,128)(2,1)S(1)}, bf16[336,128]{1,0:T(8,128)(2,1)S(1)}, u32[]{:S(2)}, u32[]{:S(2)}) collective-permute-start(bf16[336,128]{1,0:T(8,128)(2,1)S(1)} %sum_plane.1.refs_0_), channel_id=1, source_target_pairs={{0,4},{1,5},{2,6},{3,7},{4,0},{5,1},{6,2},{7,3},{8,12},{9,13},{10,... | collective-permute-start | bytes 258056 | tf_op jit(solution)/shard_map/ppermute | solution.py:258
  14.6 4.3 %collective-permute-start = (bf16[4,64,128]{2,1,0:T(8,128)(2,1)S(1)}, bf16[4,64,128]{2,1,0:T(8,128)(2,1)S(1)}, u32[]{:S(2)}, u32[]{:S(2)}) collective-permute-start(bf16[4,64,128]{2,1,0:T(8,128)(2,1)S(1)} %get-tuple-element.16.x_mine), channel_id=1, source_target_pairs={{0,16},{1,17},{2,18},{3,19},{4,20},{5,21},{6,22},{7,23},{8,24},{9,... | collective-permute-start | bytes 196616 | tf_op jit(solution)/shard_map/ppermute | solution.py:258
  20.6 6.5 %collective-permute-start.8 = (bf16[528,128]{1,0:T(8,128)(2,1)S(1)}, bf16[528,128]{1,0:T(8,128)(2,1)S(1)}, u32[]{:S(2)}, u32[]{:S(2)}) collective-permute-start(bf16[528,128]{1,0:T(8,128)(2,1)S(1)} %get-tuple-element.22.plane_0), channel_id=1, source_target_pairs={{0,18},{1,19},{2,16},{3,17},{4,22},{5,23},{6,20},{7,21},{8,26},{9,... | collective-permute-start | bytes 405512 | tf_op jit(solution)/shard_map/ppermute | solution.py:258
  23.1 6.3 %collective-permute-start.7 = (bf16[528,128]{1,0:T(8,128)(2,1)S(1)}, bf16[528,128]{1,0:T(8,128)(2,1)S(1)}, u32[]{:S(2)}, u32[]{:S(2)}) collective-permute-start(bf16[528,128]{1,0:T(8,128)(2,1)S(1)} %get-tuple-element.22.plane_0), channel_id=1, source_target_pairs={{0,2},{1,3},{2,0},{3,1},{4,6},{5,7},{6,4},{7,5},{8,10},{9,11},{10,... | collective-permute-start | bytes 405512 | tf_op jit(solution)/shard_map/ppermute | solution.py:258
  23.6 5.8 %collective-permute-start.6 = (bf16[528,128]{1,0:T(8,128)(2,1)S(1)}, bf16[528,128]{1,0:T(8,128)(2,1)S(1)}, u32[]{:S(2)}, u32[]{:S(2)}) collective-permute-start(bf16[528,128]{1,0:T(8,128)(2,1)S(1)} %get-tuple-element.22.plane_0), channel_id=1, source_target_pairs={{0,16},{1,17},{2,18},{3,19},{4,20},{5,21},{6,22},{7,23},{8,24},{9,... | collective-permute-start | bytes 405512 | tf_op jit(solution)/shard_map/ppermute | solution.py:258
  24.1 1.3 %collective-permute-start.9 = (bf16[4,64,128]{2,1,0:T(8,128)(2,1)S(1)}, bf16[4,64,128]{2,1,0:T(8,128)(2,1)S(1)}, u32[]{:S(2)}, u32[]{:S(2)}) collective-permute-start(bf16[4,64,128]{2,1,0:T(8,128)(2,1)S(1)} %collective-permute-done.after.x_peer), channel_id=1, source_target_pairs={{0,1},{1,0},{2,3},{3,2},{4,5},{5,4},{6,7},{7,6},{8,9},{9,8},{10,11... | collective-permute-start | bytes 196616 | tf_op jit(solution)/shard_map/ppermute | solution.py:258
  31.0 1.6 %collective-permute-start.10 = (bf16[576,256]{1,0:T(8,128)(2,1)S(1)}, bf16[576,256]{1,0:T(8,128)(2,1)S(1)}, u32[]{:S(2)}, u32[]{:S(2)}) collective-permute-start(bf16[576,256]{1,0:T(8,128)(2,1)S(1)} %get-tuple-element.25.mine), channel_id=1, source_target_pairs={{0,1},{1,0},{2,3},{3,2},{4,5},{5,4},{6,7},{7,6},{8,9},{9,8},{10,11... | collective-permute-start | bytes 884744 | tf_op jit(solution)/shard_map/ppermute | solution.py:258

commit v6 on v5

--- a/solution.py
+++ b/solution.py
@@ -44,53 +44,46 @@
     pack[2 * OWN : 2 * OWN + INTS, :] = ints.astype(F32).astype(BF16)
 
 
-def first_kernel(
-    feat_hbm, nbr_hbm, w_hbm, cot_hbm, near_hbm, sends_hbm, pack, x_t, kept, sent,
-    feat_t, nbr_t, w_first, cot, near, sends, share, sems,
+def count_kernel(
+    feat_hbm, nbr_hbm, w_hbm, cot_hbm, near_hbm, sends_hbm, counts, feat_t, w_first, pack, nbr_t, cot, near, sends, sems,
 ):
     pairs = ((nbr_hbm, nbr_t), (feat_hbm, feat_t), (w_hbm, w_first), (cot_hbm, cot), (near_hbm, near), (sends_hbm, sends))
     copies = [pltpu.make_async_copy(src, dst, sems.at[i]) for i, (src, dst) in enumerate(pairs)]
     for copy in copies:
         copy.start()
     copies[0].wait()
-    sources = feat_t.shape[1]
     row = lax.broadcasted_iota(jnp.int32, (LANES, LANES), 0)
-    for t in range(x_t.shape[0]):
+    for t in range(nbr_t.shape[1] // LANES):
         cols = slice(t * LANES, (t + 1) * LANES)
         low = nbr_t[:, cols] & (LANES - 1)
         unit = jnp.left_shift(1, 4 * jnp.right_shift(nbr_t[:, cols], 7))
         packed = jnp.zeros((LANES, LANES), jnp.int32)
         for k in range(FAN1):
             packed = packed + jnp.where(row == low[k : k + 1, :], unit[k : k + 1, :], 0)
-        parts = [jnp.right_shift(packed, 4 * b) & 15 for b in range(sources // LANES)]
-        counts = jnp.concatenate([part.astype(F32).astype(BF16) for part in parts], axis=0)
-        if t == 0:
-            copies[1].wait()
-        mean = (dot(feat_t[...], counts, ((1,), (0,))) / FAN1).astype(BF16)
-        chunk = jnp.concatenate([feat_t[:, cols], mean], axis=0)
-        x_t[t] = chunk
-        sent[2 * x_t.shape[0] + t] = chunk
-        if t == 0:
-            copies[2].wait()
-        share[cols, :] = dot(chunk, w_first[...], ((0,), (0,)))
-    line = x_t.shape[0]
-    my_feat = lax.axis_index("feat")
-    for c, out in enumerate((kept, sent)):
-        for y in range(2):
-            for z in range(line):
-                owner = z * 4 + ((my_feat % 4) ^ (2 * y + c))
-                block = share[pl.ds(pl.multiple_of(owner * OWN, OWN), OWN), :].astype(out.dtype)
-                for side in range(2):
-                    out[y * line + z, side * OWN : (side + 1) * OWN, :] = block[:, side * LANES : (side + 1) * LANES]
-    for copy in copies[3:]:
+        for b in range(counts.shape[0] // LANES):
+            part = jnp.right_shift(packed, 4 * b) & 15
+            counts[b * LANES : (b + 1) * LANES, cols] = part.astype(F32).astype(BF16)
+    for copy in copies[1:]:
         copy.wait()
     write_pack(sends, cot, near, pack)
 
 
-def sum_core_kernel(mine, received, kept, sent):
-    line = kept.shape[0]
-    kept[...] = mine[0:line] + received[0:line].astype(F32)
-    sent[...] = (mine[line : 2 * line] + received[line : 2 * line].astype(F32)).astype(BF16)
+def first_kernel(counts, feat_mine, w_mine, feat_core, w_core, x_t, kept, sent, share):
+    line = x_t.shape[0]
+    mean = [(dot(feat[...], counts[...], ((1,), (0,))) / FAN1).astype(BF16) for feat in (feat_mine, feat_core)]
+    w_first = jnp.concatenate([w_mine[...], w_core[...]], axis=0)
+    for t in range(line):
+        cols = slice(t * LANES, (t + 1) * LANES)
+        chunk = jnp.concatenate([feat_mine[:, cols], mean[0][:, cols], feat_core[:, cols], mean[1][:, cols]], axis=0)
+        x_t[t] = chunk
+        share[cols, :] = dot(chunk, w_first, ((0,), (0,)))
+    my_feat = lax.axis_index("feat")
+    for y, out in enumerate((kept, sent)):
+        for z in range(line):
+            owner = z * 4 + ((my_feat % 4) ^ (2 * y))
+            block = share[pl.ds(pl.multiple_of(owner * OWN, OWN), OWN), :].astype(out.dtype)
+            for side in range(2):
+                out[z, side * OWN : (side + 1) * OWN, :] = block[:, side * LANES : (side + 1) * LANES]
 
 
 def sum_plane_kernel(pack, mine, received, message):
@@ -189,7 +182,7 @@
 
 
 def last_kernel(
-    n_feat, plane_0, plane_1, plane_2, plane_3, w_second, x_mine, x_core, x_peer, x_last,
+    n_feat, plane_0, plane_1, plane_2, plane_3, w_second, x_mine, x_peer,
     own_counts, swapped, kept, cot, near_cot, d_hidden, lists, spread, turn, hidden, d_pre, slices,
 ):
     write_back(n_feat, plane_0, plane_1, plane_2, plane_3, w_second, cot, near_cot, d_hidden, own_counts, lists, spread, turn)
@@ -217,10 +210,8 @@
 
     for z in range(line):
         cols = slice(z * LANES, (z + 1) * LANES)
-        slices[0, 0 : 2 * OWN, cols] = x_mine[z]
-        slices[0, 2 * OWN : 4 * OWN, cols] = x_core[2 * line + z]
-        slices[1, 0 : 2 * OWN, cols] = x_peer[z]
-        slices[1, 2 * OWN : 4 * OWN, cols] = x_last[z]
+        slices[0, :, cols] = x_mine[z]
+        slices[1, :, cols] = x_peer[z]
     mine = d_pre[pl.ds(pl.multiple_of(my_graph * rows, rows), rows), :]
     peer = d_pre[pl.ds(pl.multiple_of((1 - my_graph) * rows, rows), rows), :]
     first = dot(slices[0], mine, ((1,), (0,))) + dot(slices[1], peer, ((1,), (0,)))
@@ -265,16 +256,22 @@
     line = n_feat // 4
     from_hbm = [features.T, nbr_first.T, w_first.reshape(width, HID), cotangent, nbr_second.T, send_rows]
     block = (line, width, LANES)
-    pack, x_mine, kept, sent = call(
+    sources = features.shape[0]
+    counts, feat_mine, w_mine, pack = call(
+        count_kernel,
+        [((sources, rows), BF16), ((OWN, sources), BF16), ((width, HID), BF16), ((width + INTS, LANES), BF16)],
+        [ANY] * 6,
+        [pltpu.VMEM(x.shape, x.dtype) for x in (nbr_first.T, cotangent, nbr_second.T)]
+        + [pltpu.SMEM(send_rows.shape, jnp.int32), pltpu.SemaphoreType.DMA((6,))],
+        name="count",
+    )(*[pltpu.with_memory_space_constraint(x, pltpu.HBM) for x in from_hbm])
+    x_mine, kept, sent = call(
         first_kernel,
-        [((width + INTS, LANES), BF16), (block, BF16), ((2 * line, width, LANES), F32), ((3 * line, width, LANES), BF16)],
-        [ANY] * 6,
-        [pltpu.VMEM(x.shape, x.dtype) for x in from_hbm[:-1]]
-        + [pltpu.SMEM(send_rows.shape, jnp.int32), pltpu.VMEM((rows, HID), F32), pltpu.SemaphoreType.DMA((6,))],
+        [((line, 2 * width, LANES), BF16), (block, F32), (block, BF16)],
+        [VMEM] * 5,
+        [pltpu.VMEM((rows, HID), F32)],
         name="first",
-    )(*[pltpu.with_memory_space_constraint(x, pltpu.HBM) for x in from_hbm])
-    x_core = swap(n_feat, sent, 1)
-    kept, sent = call(sum_core_kernel, [(block, F32), (block, BF16)], [VMEM] * 2, name="sum_core")(kept, x_core)
+    )(counts, feat_mine, w_mine, swap(n_feat, from_hbm[0], 1), swap(n_feat, from_hbm[2], 1))
     x_peer = swap(n_feat, x_mine, n_feat)
     (message,) = call(
         sum_plane_kernel,
@@ -282,7 +279,6 @@
         [VMEM] * 3,
         name="sum_plane",
     )(pack, kept, swap(n_feat, sent, 2))
-    x_last = swap(n_feat, x_peer, 1)
     exact, message = call(
         sum_line_kernel,
         [(block, F32), ((2 * line * width + INTS, LANES), BF16)],
@@ -296,7 +292,7 @@
     own_counts, swapped, kept = call(
         functools.partial(last_kernel, n_feat),
         [((OWN, width), F32), ((2 * HID + width, HID), BF16), ((width, HID), F32)],
-        [VMEM] * 9,
+        [VMEM] * 7,
         [
             pltpu.VMEM((half, HID), BF16),
             pltpu.VMEM((half, HID), BF16),
@@ -309,7 +305,7 @@
             pltpu.VMEM((2, 2 * width, rows), BF16),
         ],
         name="last",
-    )(*plane, w_second, x_mine, x_core, x_peer, x_last)
+    )(*plane, w_second, x_mine, x_peer)
     (layer_out,) = call(
         functools.partial(out_kernel, n_feat),
         [((OWN, HID), BF16)],

time: 33.6 us -> 32.7 us (0.973)
  waiting for transfers between devices: 13.7 us -> 12.6 us
    ppermute x11, waiting for transfers between devices: 13.7 us -> 12.6 us  [swap(): lax.ppermute(value, AXES, [(d, d ^ relative) for d in range(2 * n_feat)])]
  transfers between devices with their start and end apart: 11 -> 11, of which waited for: 9 -> 6; matrix products, arithmetic and copies ran while one was open for 0% -> 0% of each run, Pallas kernels for 3% -> 8%
where the time goes in v6:
time: 32.7 us; the launch traced here: 32.6 us
  starting transfers between devices  13.4 us (41%)
  waiting for transfers between devices  12.6 us (39%)
  Pallas kernels  5.78 us (18%)
  between operations  0.71 us (2%)
    ppermute x11, starting transfers between devices, swap(): lax.ppermute(value, AXES, [(d, d ^ relative) for d in range(2 * n_feat)])  13.4 us
    ppermute x11, waiting for transfers between devices, swap(): lax.ppermute(value, AXES, [(d, d ^ relative) for d in range(2 * n_feat)])  12.6 us
    pallas_call x1, Pallas kernels, pair_body(): call(count_kernel, [((sources, rows), BF16), ((OWN, sources), BF16), ((wi...  1.69 us
    pallas_call x1, Pallas kernels, pair_body(): call(functools.partial(last_kernel, n_feat), [((OWN, width), F32), ((2 *...  1.55 us
    pallas_call x1, Pallas kernels, pair_body(): call(functools.partial(out_kernel, n_feat), [((OWN, HID), BF16)], [VMEM]...  0.9 us
    pallas_call x1, Pallas kernels, pair_body(): call(add_kernel, [((2, HID, HID), F32), ((width, HID), F32)], [VMEM] * 3,...  0.87 us
    pallas_call x1, Pallas kernels, pair_body(): call(first_kernel, [((line, 2 * width, LANES), BF16), (block, F32), (bloc...  0.72 us
  transfers between devices with their start and end apart: 11, of which 6 were waited for; matrix products, arithmetic and copies ran while one was open for 0% of the time, Pallas kernels for 8%

profile of v6, /device:TPU:0, one launch (start us, length us, event | category | flops | bytes accessed | tf_op | source)
XLA Modules:
  0.0 32.6 jit_solution(2968287408534611754)
XLA Ops:
  0.6 0.5 %collective-permute-start = (bf16[32,1024]{1,0:T(8,128)(2,1)}, bf16[32,1024]{1,0:T(8,128)(2,1)S(1)}, u32[]{:S(2)}, u32[]{:S(2)}) collective-permute-start(bf16[32,1024]{1,0:T(8,128)(2,1)} %bitcast.5), channel_id=1, source_target_pairs={{0,1},{1,0},{2,3},{3,2},{4,5},{5,4},{6,7},{7,6},{8,9},{9,8},{10,11... | collective-permute-start | bytes 196616 | tf_op jit(solution)/shard_map/ppermute | solution.py:249
  1.1 0.1 collective-permute-start.1
  1.2 1.7 %count.1 = (bf16[1024,512]{1,0:T(8,128)(2,1)S(1)}, bf16[32,1024]{1,0:T(8,128)(2,1)S(1)}, bf16[64,256]{1,0:T(8,128)(2,1)S(1)}, bf16[80,128]{1,0:T(8,128)(2,1)S(1)}) custom-call(bf16[32,1024]{1,0:T(8,128)(2,1)} %bitcast.6, s32[15,512]{1,0:T(8,128)} %bitcast.7, bf16[64,256]{1,0:T(8,128)(2,1)} %bitcast.9, bf16[32,256]{1,0:T(8,128)(2,1)} %cot_hbm.1, ...), custom_call_target="tpu_custom_call" | custom-call | tf_op jit(solution)/shard_map/count/pallas_call | solution.py:260
  2.9 0.0 collective-permute-done.1.w_core
  2.9 0.0 collective-permute-done.feat_core
  2.9 0.7 %first.1 = (bf16[4,128,128]{2,1,0:T(8,128)(2,1)S(1)}, f32[4,64,128]{2,1,0:T(8,128)S(1)}, bf16[4,64,128]{2,1,0:T(8,128)(2,1)S(1)}) custom-call(bf16[1024,512]{1,0:T(8,128)(2,1)S(1)} %get-tuple-element.17.counts, bf16[32,1024]{1,0:T(8,128)(2,1)S(1)} %get-tuple-element.18.feat_mine, bf16[64,256]{1,0:T(8,128)(2,1)S(1)} %get-tuple-element.19.w_mine, ...), custom_call_target="tpu_custom_call" | custom-call | tf_op jit(solution)/shard_map/first/pallas_call | solution.py:268
  3.7 3.0 %collective-permute-start.3 = (bf16[4,64,128]{2,1,0:T(8,128)(2,1)S(1)}, bf16[4,64,128]{2,1,0:T(8,128)(2,1)S(1)}, u32[]{:S(2)}, u32[]{:S(2)}) collective-permute-start(bf16[4,64,128]{2,1,0:T(8,128)(2,1)S(1)} %get-tuple-element.23), channel_id=1, source_target_pairs={{0,2},{1,3},{2,0},{3,1},{4,6},{5,7},{6,4},{7,5},{8,10},{9,11},{10,... | collective-permute-start | bytes 196616 | tf_op jit(solution)/shard_map/ppermute | solution.py:249
  6.7 1.5 %collective-permute-start.2 = (bf16[4,128,128]{2,1,0:T(8,128)(2,1)S(1)}, bf16[4,128,128]{2,1,0:T(8,128)(2,1)S(1)}, u32[]{:S(2)}, u32[]{:S(2)}) collective-permute-start(bf16[4,128,128]{2,1,0:T(8,128)(2,1)S(1)} %get-tuple-element.20.x_mine), channel_id=1, source_target_pairs={{0,16},{1,17},{2,18},{3,19},{4,20},{5,21},{6,22},{7,23},{8,24},{9,... | collective-permute-start | bytes 393224 | tf_op jit(solution)/shard_map/ppermute | solution.py:249
  8.2 0.8 %collective-permute-done.3.received = bf16[4,64,128]{2,1,0:T(8,128)(2,1)S(1)} collective-permute-done((bf16[4,64,128]{2,1,0:T(8,128)(2,1)S(1)}, bf16[4,64,128]{2,1,0:T(8,128)(2,1)S(1)}, u32[]{:S(2)}, u32[]{:S(2)}) %collective-permute-start.3) | collective-permute-done | bytes 65568 | tf_op jit(solution)/shard_map/ppermute | solution.py:249
  9.0 0.0 copy-start
  9.1 4.1 %collective-permute-start.6 = (bf16[336,128]{1,0:T(8,128)(2,1)S(1)}, bf16[336,128]{1,0:T(8,128)(2,1)S(1)}, u32[]{:S(2)}, u32[]{:S(2)}) collective-permute-start(bf16[336,128]{1,0:T(8,128)(2,1)S(1)} %sum_plane.1.refs_0_), channel_id=1, source_target_pairs={{0,12},{1,13},{2,14},{3,15},{4,8},{5,9},{6,10},{7,11},{8,4},{9,5},... | collective-permute-start | bytes 258056 | tf_op jit(solution)/shard_map/ppermute | solution.py:249
  13.1 0.0 collective-permute-start.5
  13.1 0.6 %collective-permute-start.4 = (bf16[336,128]{1,0:T(8,128)(2,1)S(1)}, bf16[336,128]{1,0:T(8,128)(2,1)S(1)}, u32[]{:S(2)}, u32[]{:S(2)}) collective-permute-start(bf16[336,128]{1,0:T(8,128)(2,1)S(1)} %sum_plane.1.refs_0_), channel_id=1, source_target_pairs={{0,4},{1,5},{2,6},{3,7},{4,0},{5,1},{6,2},{7,3},{8,12},{9,13},{10,... | collective-permute-start | bytes 258056 | tf_op jit(solution)/shard_map/ppermute | solution.py:249
  13.8 0.0 collective-permute-done.2.after.x_peer
  13.8 2.4 %collective-permute-done.6.refs_3_ = bf16[336,128]{1,0:T(8,128)(2,1)S(1)} collective-permute-done((bf16[336,128]{1,0:T(8,128)(2,1)S(1)}, bf16[336,128]{1,0:T(8,128)(2,1)S(1)}, u32[]{:S(2)}, u32[]{:S(2)}) %collective-permute-start.6) | collective-permute-done | bytes 86048 | tf_op jit(solution)/shard_map/ppermute | solution.py:249
  16.2 3.4 %collective-permute-done.5.refs_2_ = bf16[336,128]{1,0:T(8,128)(2,1)S(1)} collective-permute-done((bf16[336,128]{1,0:T(8,128)(2,1)S(1)}, bf16[336,128]{1,0:T(8,128)(2,1)S(1)}, u32[]{:S(2)}, u32[]{:S(2)}) %collective-permute-start.5) | collective-permute-done | bytes 86048 | tf_op jit(solution)/shard_map/ppermute | solution.py:249
  19.6 0.0 collective-permute-done.4.refs_1_
  19.7 2.5 %collective-permute-start.9 = (bf16[528,128]{1,0:T(8,128)(2,1)S(1)}, bf16[528,128]{1,0:T(8,128)(2,1)S(1)}, u32[]{:S(2)}, u32[]{:S(2)}) collective-permute-start(bf16[528,128]{1,0:T(8,128)(2,1)S(1)} %get-tuple-element.24.plane_0), channel_id=1, source_target_pairs={{0,18},{1,19},{2,16},{3,17},{4,22},{5,23},{6,20},{7,21},{8,26},{9,... | collective-permute-start | bytes 405512 | tf_op jit(solution)/shard_map/ppermute | solution.py:249
  22.2 0.5 %collective-permute-start.8 = (bf16[528,128]{1,0:T(8,128)(2,1)S(1)}, bf16[528,128]{1,0:T(8,128)(2,1)S(1)}, u32[]{:S(2)}, u32[]{:S(2)}) collective-permute-start(bf16[528,128]{1,0:T(8,128)(2,1)S(1)} %get-tuple-element.24.plane_0), channel_id=1, source_target_pairs={{0,2},{1,3},{2,0},{3,1},{4,6},{5,7},{6,4},{7,5},{8,10},{9,11},{10,... | collective-permute-start | bytes 405512 | tf_op jit(solution)/shard_map/ppermute | solution.py:249
  22.7 0.5 %collective-permute-start.7 = (bf16[528,128]{1,0:T(8,128)(2,1)S(1)}, bf16[528,128]{1,0:T(8,128)(2,1)S(1)}, u32[]{:S(2)}, u32[]{:S(2)}) collective-permute-start(bf16[528,128]{1,0:T(8,128)(2,1)S(1)} %get-tuple-element.24.plane_0), channel_id=1, source_target_pairs={{0,16},{1,17},{2,18},{3,19},{4,20},{5,21},{6,22},{7,23},{8,24},{9,... | collective-permute-start | bytes 405512 | tf_op jit(solution)/shard_map/ppermute | solution.py:249
  23.2 3.0 %collective-permute-done.9.plane_3 = bf16[528,128]{1,0:T(8,128)(2,1)S(1)} collective-permute-done((bf16[528,128]{1,0:T(8,128)(2,1)S(1)}, bf16[528,128]{1,0:T(8,128)(2,1)S(1)}, u32[]{:S(2)}, u32[]{:S(2)}) %collective-permute-start.9) | collective-permute-done | bytes 135200 | tf_op jit(solution)/shard_map/ppermute | solution.py:249
  26.3 2.2 %collective-permute-done.8.plane_2 = bf16[528,128]{1,0:T(8,128)(2,1)S(1)} collective-permute-done((bf16[528,128]{1,0:T(8,128)(2,1)S(1)}, bf16[528,128]{1,0:T(8,128)(2,1)S(1)}, u32[]{:S(2)}, u32[]{:S(2)}) %collective-permute-start.8) | collective-permute-done | bytes 135200 | tf_op jit(solution)/shard_map/ppermute | solution.py:249
  28.5 0.0 collective-permute-done.7.plane_1.peer
  28.5 0.0 copy-done
  28.5 1.5 %last.1 = (f32[32,64]{1,0:T(8,128)S(1)}, bf16[576,256]{1,0:T(8,128)(2,1)S(1)}, f32[64,256]{1,0:T(8,128)S(1)}) custom-call(bf16[528,128]{1,0:T(8,128)(2,1)S(1)} %get-tuple-element.24.plane_0, bf16[528,128]{1,0:T(8,128)(2,1)S(1)} %collective-permute-done.7.plane_1.peer, bf16[528,128]{1,0:T(8,128)(2,1)S(1)} %collective-permute-done.8.plane_2, ...), custom_call_target="tpu_custom_call" | custom-call | tf_op jit(solution)/shard_map/last/pallas_call | solution.py:292
  30.0 0.1 collective-permute-start.10
  30.1 0.9 %out.1 = bf16[32,256]{1,0:T(8,128)(2,1)} custom-call(bf16[528,128]{1,0:T(8,128)(2,1)S(1)} %collective-permute-done.7.plane_1.peer, f32[4,64,128]{2,1,0:T(8,128)S(1)} %get-tuple-element.25.exact, f32[32,64]{1,0:T(8,128)S(1)} %get-tuple-element.26.own_counts, bf16[2,256,256]{2,1,0:T(8,128)(2,1)S(1)} %copy-done), custom_call_target="tpu_custom_call" | custom-call | tf_op jit(solution)/shard_map/out/pallas_call | solution.py:309
  31.0 0.7 %collective-permute-done.10.theirs = bf16[576,256]{1,0:T(8,128)(2,1)S(1)} collective-permute-done((bf16[576,256]{1,0:T(8,128)(2,1)S(1)}, bf16[576,256]{1,0:T(8,128)(2,1)S(1)}, u32[]{:S(2)}, u32[]{:S(2)}) %collective-permute-start.10) | collective-permute-done | bytes 294944 | tf_op jit(solution)/shard_map/ppermute | solution.py:249
  31.7 0.9 %add.1 = (f32[2,256,256]{2,1,0:T(8,128)}, f32[64,256]{1,0:T(8,128)}) custom-call(bf16[576,256]{1,0:T(8,128)(2,1)S(1)} %get-tuple-element.27.mine, bf16[576,256]{1,0:T(8,128)(2,1)S(1)} %collective-permute-done.10.theirs, f32[64,256]{1,0:T(8,128)S(1)} %get-tuple-element.28.kept), custom_call_target="tpu_custom_call" | custom-call | tf_op jit(solution)/shard_map/add/pallas_call | solution.py:316
  (2 shorter events, 0.1 us)
Async XLA Ops:
  0.6 2.3 %collective-permute-start = (bf16[32,1024]{1,0:T(8,128)(2,1)}, bf16[32,1024]{1,0:T(8,128)(2,1)S(1)}, u32[]{:S(2)}, u32[]{:S(2)}) collective-permute-start(bf16[32,1024]{1,0:T(8,128)(2,1)} %bitcast.5), channel_id=1, source_target_pairs={{0,1},{1,0},{2,3},{3,2},{4,5},{5,4},{6,7},{7,6},{8,9},{9,8},{10,11... | collective-permute-start | bytes 196616 | tf_op jit(solution)/shard_map/ppermute | solution.py:249
  1.1 1.8 %collective-permute-start.1 = (bf16[64,256]{1,0:T(8,128)(2,1)}, bf16[64,256]{1,0:T(8,128)(2,1)S(1)}, u32[]{:S(2)}, u32[]{:S(2)}) collective-permute-start(bf16[64,256]{1,0:T(8,128)(2,1)} %bitcast.8), channel_id=1, source_target_pairs={{0,1},{1,0},{2,3},{3,2},{4,5},{5,4},{6,7},{7,6},{8,9},{9,8},{10,11... | collective-permute-start | bytes 98312 | tf_op jit(solution)/shard_map/ppermute | solution.py:249
  3.7 5.3 %collective-permute-start.3 = (bf16[4,64,128]{2,1,0:T(8,128)(2,1)S(1)}, bf16[4,64,128]{2,1,0:T(8,128)(2,1)S(1)}, u32[]{:S(2)}, u32[]{:S(2)}) collective-permute-start(bf16[4,64,128]{2,1,0:T(8,128)(2,1)S(1)} %get-tuple-element.23), channel_id=1, source_target_pairs={{0,2},{1,3},{2,0},{3,1},{4,6},{5,7},{6,4},{7,5},{8,10},{9,11},{10,... | collective-permute-start | bytes 196616 | tf_op jit(solution)/shard_map/ppermute | solution.py:249
  6.7 7.1 %collective-permute-start.2 = (bf16[4,128,128]{2,1,0:T(8,128)(2,1)S(1)}, bf16[4,128,128]{2,1,0:T(8,128)(2,1)S(1)}, u32[]{:S(2)}, u32[]{:S(2)}) collective-permute-start(bf16[4,128,128]{2,1,0:T(8,128)(2,1)S(1)} %get-tuple-element.20.x_mine), channel_id=1, source_target_pairs={{0,16},{1,17},{2,18},{3,19},{4,20},{5,21},{6,22},{7,23},{8,24},{9,... | collective-permute-start | bytes 393224 | tf_op jit(solution)/shard_map/ppermute | solution.py:249
  9.0 19.4 %copy-start = (bf16[2,256,256]{2,1,0:T(8,128)(2,1)S(1)}, bf16[2,256,256]{2,1,0:T(8,128)(2,1)}, u32[]{:S(2)}) copy-start(bf16[2,256,256]{2,1,0:T(8,128)(2,1)} %w_second.3) | copy-start | bytes 786436
  9.1 7.2 %collective-permute-start.6 = (bf16[336,128]{1,0:T(8,128)(2,1)S(1)}, bf16[336,128]{1,0:T(8,128)(2,1)S(1)}, u32[]{:S(2)}, u32[]{:S(2)}) collective-permute-start(bf16[336,128]{1,0:T(8,128)(2,1)S(1)} %sum_plane.1.refs_0_), channel_id=1, source_target_pairs={{0,12},{1,13},{2,14},{3,15},{4,8},{5,9},{6,10},{7,11},{8,4},{9,5},... | collective-permute-start | bytes 258056 | tf_op jit(solution)/shard_map/ppermute | solution.py:249
  13.1 6.5 %collective-permute-start.5 = (bf16[336,128]{1,0:T(8,128)(2,1)S(1)}, bf16[336,128]{1,0:T(8,128)(2,1)S(1)}, u32[]{:S(2)}, u32[]{:S(2)}) collective-permute-start(bf16[336,128]{1,0:T(8,128)(2,1)S(1)} %sum_plane.1.refs_0_), channel_id=1, source_target_pairs={{0,8},{1,9},{2,10},{3,11},{4,12},{5,13},{6,14},{7,15},{8,0},{9,1},... | collective-permute-start | bytes 258056 | tf_op jit(solution)/shard_map/ppermute | solution.py:249
  13.1 6.5 %collective-permute-start.4 = (bf16[336,128]{1,0:T(8,128)(2,1)S(1)}, bf16[336,128]{1,0:T(8,128)(2,1)S(1)}, u32[]{:S(2)}, u32[]{:S(2)}) collective-permute-start(bf16[336,128]{1,0:T(8,128)(2,1)S(1)} %sum_plane.1.refs_0_), channel_id=1, source_target_pairs={{0,4},{1,5},{2,6},{3,7},{4,0},{5,1},{6,2},{7,3},{8,12},{9,13},{10,... | collective-permute-start | bytes 258056 | tf_op jit(solution)/shard_map/ppermute | solution.py:249
  19.7 6.6 %collective-permute-start.9 = (bf16[528,128]{1,0:T(8,128)(2,1)S(1)}, bf16[528,128]{1,0:T(8,128)(2,1)S(1)}, u32[]{:S(2)}, u32[]{:S(2)}) collective-permute-start(bf16[528,128]{1,0:T(8,128)(2,1)S(1)} %get-tuple-element.24.plane_0), channel_id=1, source_target_pairs={{0,18},{1,19},{2,16},{3,17},{4,22},{5,23},{6,20},{7,21},{8,26},{9,... | collective-permute-start | bytes 405512 | tf_op jit(solution)/shard_map/ppermute | solution.py:249
  22.2 6.3 %collective-permute-start.8 = (bf16[528,128]{1,0:T(8,128)(2,1)S(1)}, bf16[528,128]{1,0:T(8,128)(2,1)S(1)}, u32[]{:S(2)}, u32[]{:S(2)}) collective-permute-start(bf16[528,128]{1,0:T(8,128)(2,1)S(1)} %get-tuple-element.24.plane_0), channel_id=1, source_target_pairs={{0,2},{1,3},{2,0},{3,1},{4,6},{5,7},{6,4},{7,5},{8,10},{9,11},{10,... | collective-permute-start | bytes 405512 | tf_op jit(solution)/shard_map/ppermute | solution.py:249
  22.7 5.8 %collective-permute-start.7 = (bf16[528,128]{1,0:T(8,128)(2,1)S(1)}, bf16[528,128]{1,0:T(8,128)(2,1)S(1)}, u32[]{:S(2)}, u32[]{:S(2)}) collective-permute-start(bf16[528,128]{1,0:T(8,128)(2,1)S(1)} %get-tuple-element.24.plane_0), channel_id=1, source_target_pairs={{0,16},{1,17},{2,18},{3,19},{4,20},{5,21},{6,22},{7,23},{8,24},{9,... | collective-permute-start | bytes 405512 | tf_op jit(solution)/shard_map/ppermute | solution.py:249
  30.0 1.6 %collective-permute-start.10 = (bf16[576,256]{1,0:T(8,128)(2,1)S(1)}, bf16[576,256]{1,0:T(8,128)(2,1)S(1)}, u32[]{:S(2)}, u32[]{:S(2)}) collective-permute-start(bf16[576,256]{1,0:T(8,128)(2,1)S(1)} %get-tuple-element.27.mine), channel_id=1, source_target_pairs={{0,1},{1,0},{2,3},{3,2},{4,5},{5,4},{6,7},{7,6},{8,9},{9,8},{10,11... | collective-permute-start | bytes 884744 | tf_op jit(solution)/shard_map/ppermute | solution.py:249

commit v7 on v6

--- a/solution.py
+++ b/solution.py
@@ -70,11 +70,12 @@
 
 def first_kernel(counts, feat_mine, w_mine, feat_core, w_core, x_t, kept, sent, share):
     line = x_t.shape[0]
-    mean = [(dot(feat[...], counts[...], ((1,), (0,))) / FAN1).astype(BF16) for feat in (feat_mine, feat_core)]
+    both = jnp.concatenate([feat_mine[...], feat_core[...]], axis=0)
+    mean = (dot(both, counts[...], ((1,), (0,))) / FAN1).astype(BF16)
     w_first = jnp.concatenate([w_mine[...], w_core[...]], axis=0)
     for t in range(line):
         cols = slice(t * LANES, (t + 1) * LANES)
-        chunk = jnp.concatenate([feat_mine[:, cols], mean[0][:, cols], feat_core[:, cols], mean[1][:, cols]], axis=0)
+        chunk = jnp.concatenate([both[0:OWN, cols], mean[0:OWN, cols], both[OWN:, cols], mean[OWN:, cols]], axis=0)
         x_t[t] = chunk
         share[cols, :] = dot(chunk, w_first, ((0,), (0,)))
     my_feat = lax.axis_index("feat")
@@ -112,7 +113,7 @@
     message[2 * rows :, :] = functools.reduce(lambda a, b: a + b, lists).astype(BF16)
 
 
-def write_back(n_feat, plane_0, plane_1, plane_2, plane_3, w_second, cot_all, near_cot, d_hidden, own_counts, lists, spread, turn):
+def write_back(n_feat, plane_0, plane_1, plane_2, plane_3, w_second, cots, d_hidden, own_counts, lists, spread, turn):
     line = n_feat // 4
     width = 2 * OWN
     my_graph = lax.axis_index("graph")
@@ -125,7 +126,7 @@
             span = pl.ds(pl.multiple_of(at * LANES + z * OWN, OWN), OWN)
             for side in range(2):
                 top = (2 * z + 1) * width + side * OWN
-                cot_all[span, side * LANES : (side + 1) * LANES] = message[top : top + OWN, :]
+                cots[span, side * LANES : (side + 1) * LANES] = message[top : top + OWN, :]
 
     ints = lists[...].reshape(4 * INTS, LANES)
     source = lax.broadcasted_iota(jnp.int32, (LANES, LANES), 0)
@@ -151,18 +152,18 @@
                 counts = counts + jnp.where(slot_ix == place_of[k : k + 1, :], 1.0, 0.0)
             spread[at] = counts
             block = jnp.concatenate([jnp.where(z_of == z, counts, 0.0) for z in range(line)], axis=0).astype(BF16)
-            total = total + dot(block, cot_all[at * LANES : (at + 1) * LANES, :], ((1,), (0,)))
+            total = total + dot(block, cots[at * LANES : (at + 1) * LANES, 0:HID], ((1,), (0,)))
         total = (total / FAN2).astype(BF16)
         for z in range(line):
             for p in range(2):
                 at = (p * 2 + y) * LANES + z * OWN
-                near_cot[at : at + OWN, :] = total[z * width + p * OWN : z * width + (p + 1) * OWN, :]
+                cots[at : at + OWN, HID : 2 * HID] = total[z * width + p * OWN : z * width + (p + 1) * OWN, :]
 
     turn[...] = spread[pl.ds(my_graph * 2 + my_y, 1)][0].T
     own_counts[...] = turn[pl.ds(pl.multiple_of(my_z * OWN, OWN), OWN), :]
 
-    part = dot(cot_all[...], w_second[0], ((1,), (1,)))
-    d_hidden[...] = part + dot(near_cot[...], w_second[1], ((1,), (1,)))
+    weights = jnp.concatenate([w_second[0], w_second[1]], axis=1)
+    d_hidden[...] = dot(cots[...], weights, ((1,), (1,)))
 
 
 def out_kernel(n_feat, peer, exact, own_counts, w_second, layer_out, ext):
@@ -183,9 +184,9 @@
 
 def last_kernel(
     n_feat, plane_0, plane_1, plane_2, plane_3, w_second, x_mine, x_peer,
-    own_counts, swapped, kept, cot, near_cot, d_hidden, lists, spread, turn, hidden, d_pre, slices,
+    own_counts, swapped, kept, cots, d_hidden, lists, spread, turn, hidden, d_pre, slices,
 ):
-    write_back(n_feat, plane_0, plane_1, plane_2, plane_3, w_second, cot, near_cot, d_hidden, own_counts, lists, spread, turn)
+    write_back(n_feat, plane_0, plane_1, plane_2, plane_3, w_second, cots, d_hidden, own_counts, lists, spread, turn)
     my_graph = lax.axis_index("graph")
     my_feat = lax.axis_index("feat")
     rows = n_feat * OWN
@@ -205,8 +206,9 @@
             target = pl.ds(pl.multiple_of(graph * rows + (z * 4 + (my_feat % 4 ^ 2 * y)) * OWN, OWN), OWN)
             d_pre[target, :] = (d_hidden[span, :] * slope).astype(BF16)
 
-    swapped[0:HID, :] = dot(hidden[...], cot[...], ((0,), (0,))).astype(BF16)
-    swapped[HID : 2 * HID, :] = dot(hidden[...], near_cot[...], ((0,), (0,))).astype(BF16)
+    second = dot(hidden[...], cots[...], ((0,), (0,))).astype(BF16)
+    swapped[0:HID, :] = second[:, 0:HID]
+    swapped[HID : 2 * HID, :] = second[:, HID : 2 * HID]
 
     for z in range(line):
         cols = slice(z * LANES, (z + 1) * LANES)
@@ -294,8 +296,7 @@
         [((OWN, width), F32), ((2 * HID + width, HID), BF16), ((width, HID), F32)],
         [VMEM] * 7,
         [
-            pltpu.VMEM((half, HID), BF16),
-            pltpu.VMEM((half, HID), BF16),
+            pltpu.VMEM((half, 2 * HID), BF16),
             pltpu.VMEM((half, HID), F32),
             pltpu.VMEM((4, INTS, LANES), BF16),
             pltpu.VMEM((4, width, LANES), F32),

time: 32.7 us -> 32.4 us (level)
  no operation moved by 1% of the time
where the time goes in v7:
time: 32.4 us; the launch traced here: 32.3 us
  starting transfers between devices  13.4 us (41%)
  waiting for transfers between devices  12.6 us (39%)
  Pallas kernels  5.5 us (17%)
  between operations  0.71 us (2%)
    ppermute x11, starting transfers between devices, swap(): lax.ppermute(value, AXES, [(d, d ^ relative) for d in range(2 * n_feat)])  13.4 us
    ppermute x11, waiting for transfers between devices, swap(): lax.ppermute(value, AXES, [(d, d ^ relative) for d in range(2 * n_feat)])  12.6 us
    pallas_call x1, Pallas kernels, pair_body(): call(count_kernel, [((sources, rows), BF16), ((OWN, sources), BF16), ((wi...  1.69 us
    pallas_call x1, Pallas kernels, pair_body(): call(functools.partial(last_kernel, n_feat), [((OWN, width), F32), ((2 *...  1.44 us
    pallas_call x1, Pallas kernels, pair_body(): call(functools.partial(out_kernel, n_feat), [((OWN, HID), BF16)], [VMEM]...  0.9 us
    pallas_call x1, Pallas kernels, pair_body(): call(add_kernel, [((2, HID, HID), F32), ((width, HID), F32)], [VMEM] * 3,...  0.87 us
  transfers between devices with their start and end apart: 11, of which 6 were waited for; matrix products, arithmetic and copies ran while one was open for 0% of the time, Pallas kernels for 8%

profile of v7, /device:TPU:0, one launch (start us, length us, event | category | flops | bytes accessed | tf_op | source)
XLA Modules:
  0.0 32.3 jit_solution(11746917726350400973)
XLA Ops:
  0.6 0.5 %collective-permute-start = (bf16[32,1024]{1,0:T(8,128)(2,1)}, bf16[32,1024]{1,0:T(8,128)(2,1)S(1)}, u32[]{:S(2)}, u32[]{:S(2)}) collective-permute-start(bf16[32,1024]{1,0:T(8,128)(2,1)} %bitcast.5), channel_id=1, source_target_pairs={{0,1},{1,0},{2,3},{3,2},{4,5},{5,4},{6,7},{7,6},{8,9},{9,8},{10,11... | collective-permute-start | bytes 196616 | tf_op jit(solution)/shard_map/ppermute | solution.py:251
  1.1 0.1 collective-permute-start.1
  1.2 1.7 %count.1 = (bf16[1024,512]{1,0:T(8,128)(2,1)S(1)}, bf16[32,1024]{1,0:T(8,128)(2,1)S(1)}, bf16[64,256]{1,0:T(8,128)(2,1)S(1)}, bf16[80,128]{1,0:T(8,128)(2,1)S(1)}) custom-call(bf16[32,1024]{1,0:T(8,128)(2,1)} %bitcast.6, s32[15,512]{1,0:T(8,128)} %bitcast.7, bf16[64,256]{1,0:T(8,128)(2,1)} %bitcast.9, bf16[32,256]{1,0:T(8,128)(2,1)} %cot_hbm.1, ...), custom_call_target="tpu_custom_call" | custom-call | tf_op jit(solution)/shard_map/count/pallas_call | solution.py:262
  2.9 0.0 collective-permute-done.1.w_core
  2.9 0.0 collective-permute-done.feat_core
  2.9 0.6 %first.1 = (bf16[4,128,128]{2,1,0:T(8,128)(2,1)S(1)}, f32[4,64,128]{2,1,0:T(8,128)S(1)}, bf16[4,64,128]{2,1,0:T(8,128)(2,1)S(1)}) custom-call(bf16[1024,512]{1,0:T(8,128)(2,1)S(1)} %get-tuple-element.17.counts, bf16[32,1024]{1,0:T(8,128)(2,1)S(1)} %get-tuple-element.18.feat_mine, bf16[64,256]{1,0:T(8,128)(2,1)S(1)} %get-tuple-element.19.w_mine, ...), custom_call_target="tpu_custom_call" | custom-call | tf_op jit(solution)/shard_map/first/pallas_call | solution.py:270
  3.5 3.0 %collective-permute-start.3 = (bf16[4,64,128]{2,1,0:T(8,128)(2,1)S(1)}, bf16[4,64,128]{2,1,0:T(8,128)(2,1)S(1)}, u32[]{:S(2)}, u32[]{:S(2)}) collective-permute-start(bf16[4,64,128]{2,1,0:T(8,128)(2,1)S(1)} %get-tuple-element.23), channel_id=1, source_target_pairs={{0,2},{1,3},{2,0},{3,1},{4,6},{5,7},{6,4},{7,5},{8,10},{9,11},{10,... | collective-permute-start | bytes 196616 | tf_op jit(solution)/shard_map/ppermute | solution.py:251
  6.5 1.5 %collective-permute-start.2 = (bf16[4,128,128]{2,1,0:T(8,128)(2,1)S(1)}, bf16[4,128,128]{2,1,0:T(8,128)(2,1)S(1)}, u32[]{:S(2)}, u32[]{:S(2)}) collective-permute-start(bf16[4,128,128]{2,1,0:T(8,128)(2,1)S(1)} %get-tuple-element.20.x_mine), channel_id=1, source_target_pairs={{0,16},{1,17},{2,18},{3,19},{4,20},{5,21},{6,22},{7,23},{8,24},{9,... | collective-permute-start | bytes 393224 | tf_op jit(solution)/shard_map/ppermute | solution.py:251
  8.0 0.8 %collective-permute-done.3.received = bf16[4,64,128]{2,1,0:T(8,128)(2,1)S(1)} collective-permute-done((bf16[4,64,128]{2,1,0:T(8,128)(2,1)S(1)}, bf16[4,64,128]{2,1,0:T(8,128)(2,1)S(1)}, u32[]{:S(2)}, u32[]{:S(2)}) %collective-permute-start.3) | collective-permute-done | bytes 65568 | tf_op jit(solution)/shard_map/ppermute | solution.py:251
  8.9 0.0 copy-start
  8.9 4.1 %collective-permute-start.6 = (bf16[336,128]{1,0:T(8,128)(2,1)S(1)}, bf16[336,128]{1,0:T(8,128)(2,1)S(1)}, u32[]{:S(2)}, u32[]{:S(2)}) collective-permute-start(bf16[336,128]{1,0:T(8,128)(2,1)S(1)} %sum_plane.1.refs_0_), channel_id=1, source_target_pairs={{0,12},{1,13},{2,14},{3,15},{4,8},{5,9},{6,10},{7,11},{8,4},{9,5},... | collective-permute-start | bytes 258056 | tf_op jit(solution)/shard_map/ppermute | solution.py:251
  13.0 0.0 collective-permute-start.5
  13.0 0.6 %collective-permute-start.4 = (bf16[336,128]{1,0:T(8,128)(2,1)S(1)}, bf16[336,128]{1,0:T(8,128)(2,1)S(1)}, u32[]{:S(2)}, u32[]{:S(2)}) collective-permute-start(bf16[336,128]{1,0:T(8,128)(2,1)S(1)} %sum_plane.1.refs_0_), channel_id=1, source_target_pairs={{0,4},{1,5},{2,6},{3,7},{4,0},{5,1},{6,2},{7,3},{8,12},{9,13},{10,... | collective-permute-start | bytes 258056 | tf_op jit(solution)/shard_map/ppermute | solution.py:251
  13.6 0.0 collective-permute-done.2.after.x_peer
  13.6 2.4 %collective-permute-done.6.refs_3_ = bf16[336,128]{1,0:T(8,128)(2,1)S(1)} collective-permute-done((bf16[336,128]{1,0:T(8,128)(2,1)S(1)}, bf16[336,128]{1,0:T(8,128)(2,1)S(1)}, u32[]{:S(2)}, u32[]{:S(2)}) %collective-permute-start.6) | collective-permute-done | bytes 86048 | tf_op jit(solution)/shard_map/ppermute | solution.py:251
  16.1 3.4 %collective-permute-done.5.refs_2_ = bf16[336,128]{1,0:T(8,128)(2,1)S(1)} collective-permute-done((bf16[336,128]{1,0:T(8,128)(2,1)S(1)}, bf16[336,128]{1,0:T(8,128)(2,1)S(1)}, u32[]{:S(2)}, u32[]{:S(2)}) %collective-permute-start.5) | collective-permute-done | bytes 86048 | tf_op jit(solution)/shard_map/ppermute | solution.py:251
  19.5 0.0 collective-permute-done.4.refs_1_
  19.5 2.5 %collective-permute-start.9 = (bf16[528,128]{1,0:T(8,128)(2,1)S(1)}, bf16[528,128]{1,0:T(8,128)(2,1)S(1)}, u32[]{:S(2)}, u32[]{:S(2)}) collective-permute-start(bf16[528,128]{1,0:T(8,128)(2,1)S(1)} %get-tuple-element.24.plane_0), channel_id=1, source_target_pairs={{0,18},{1,19},{2,16},{3,17},{4,22},{5,23},{6,20},{7,21},{8,26},{9,... | collective-permute-start | bytes 405512 | tf_op jit(solution)/shard_map/ppermute | solution.py:251
  22.0 0.5 %collective-permute-start.8 = (bf16[528,128]{1,0:T(8,128)(2,1)S(1)}, bf16[528,128]{1,0:T(8,128)(2,1)S(1)}, u32[]{:S(2)}, u32[]{:S(2)}) collective-permute-start(bf16[528,128]{1,0:T(8,128)(2,1)S(1)} %get-tuple-element.24.plane_0), channel_id=1, source_target_pairs={{0,2},{1,3},{2,0},{3,1},{4,6},{5,7},{6,4},{7,5},{8,10},{9,11},{10,... | collective-permute-start | bytes 405512 | tf_op jit(solution)/shard_map/ppermute | solution.py:251
  22.5 0.5 %collective-permute-start.7 = (bf16[528,128]{1,0:T(8,128)(2,1)S(1)}, bf16[528,128]{1,0:T(8,128)(2,1)S(1)}, u32[]{:S(2)}, u32[]{:S(2)}) collective-permute-start(bf16[528,128]{1,0:T(8,128)(2,1)S(1)} %get-tuple-element.24.plane_0), channel_id=1, source_target_pairs={{0,16},{1,17},{2,18},{3,19},{4,20},{5,21},{6,22},{7,23},{8,24},{9,... | collective-permute-start | bytes 405512 | tf_op jit(solution)/shard_map/ppermute | solution.py:251
  23.1 3.0 %collective-permute-done.9.plane_3 = bf16[528,128]{1,0:T(8,128)(2,1)S(1)} collective-permute-done((bf16[528,128]{1,0:T(8,128)(2,1)S(1)}, bf16[528,128]{1,0:T(8,128)(2,1)S(1)}, u32[]{:S(2)}, u32[]{:S(2)}) %collective-permute-start.9) | collective-permute-done | bytes 135200 | tf_op jit(solution)/shard_map/ppermute | solution.py:251
  26.1 2.2 %collective-permute-done.8.plane_2 = bf16[528,128]{1,0:T(8,128)(2,1)S(1)} collective-permute-done((bf16[528,128]{1,0:T(8,128)(2,1)S(1)}, bf16[528,128]{1,0:T(8,128)(2,1)S(1)}, u32[]{:S(2)}, u32[]{:S(2)}) %collective-permute-start.8) | collective-permute-done | bytes 135200 | tf_op jit(solution)/shard_map/ppermute | solution.py:251
  28.3 0.0 collective-permute-done.7.plane_1.peer
  28.3 0.0 copy-done
  28.3 1.4 %last.1 = (f32[32,64]{1,0:T(8,128)S(1)}, bf16[576,256]{1,0:T(8,128)(2,1)S(1)}, f32[64,256]{1,0:T(8,128)S(1)}) custom-call(bf16[528,128]{1,0:T(8,128)(2,1)S(1)} %get-tuple-element.24.plane_0, bf16[528,128]{1,0:T(8,128)(2,1)S(1)} %collective-permute-done.7.plane_1.peer, bf16[528,128]{1,0:T(8,128)(2,1)S(1)} %collective-permute-done.8.plane_2, ...), custom_call_target="tpu_custom_call" | custom-call | tf_op jit(solution)/shard_map/last/pallas_call | solution.py:294
  29.8 0.1 collective-permute-start.10
  29.8 0.9 %out.1 = bf16[32,256]{1,0:T(8,128)(2,1)} custom-call(bf16[528,128]{1,0:T(8,128)(2,1)S(1)} %collective-permute-done.7.plane_1.peer, f32[4,64,128]{2,1,0:T(8,128)S(1)} %get-tuple-element.25.exact, f32[32,64]{1,0:T(8,128)S(1)} %get-tuple-element.26.own_counts, bf16[2,256,256]{2,1,0:T(8,128)(2,1)S(1)} %copy-done), custom_call_target="tpu_custom_call" | custom-call | tf_op jit(solution)/shard_map/out/pallas_call | solution.py:310
  30.7 0.7 %collective-permute-done.10.theirs = bf16[576,256]{1,0:T(8,128)(2,1)S(1)} collective-permute-done((bf16[576,256]{1,0:T(8,128)(2,1)S(1)}, bf16[576,256]{1,0:T(8,128)(2,1)S(1)}, u32[]{:S(2)}, u32[]{:S(2)}) %collective-permute-start.10) | collective-permute-done | bytes 294944 | tf_op jit(solution)/shard_map/ppermute | solution.py:251
  31.4 0.9 %add.1 = (f32[2,256,256]{2,1,0:T(8,128)}, f32[64,256]{1,0:T(8,128)}) custom-call(bf16[576,256]{1,0:T(8,128)(2,1)S(1)} %get-tuple-element.27.mine, bf16[576,256]{1,0:T(8,128)(2,1)S(1)} %collective-permute-done.10.theirs, f32[64,256]{1,0:T(8,128)S(1)} %get-tuple-element.28.kept), custom_call_target="tpu_custom_call" | custom-call | tf_op jit(solution)/shard_map/add/pallas_call | solution.py:317
  (2 shorter events, 0.1 us)
Async XLA Ops:
  0.6 2.3 %collective-permute-start = (bf16[32,1024]{1,0:T(8,128)(2,1)}, bf16[32,1024]{1,0:T(8,128)(2,1)S(1)}, u32[]{:S(2)}, u32[]{:S(2)}) collective-permute-start(bf16[32,1024]{1,0:T(8,128)(2,1)} %bitcast.5), channel_id=1, source_target_pairs={{0,1},{1,0},{2,3},{3,2},{4,5},{5,4},{6,7},{7,6},{8,9},{9,8},{10,11... | collective-permute-start | bytes 196616 | tf_op jit(solution)/shard_map/ppermute | solution.py:251
  1.1 1.8 %collective-permute-start.1 = (bf16[64,256]{1,0:T(8,128)(2,1)}, bf16[64,256]{1,0:T(8,128)(2,1)S(1)}, u32[]{:S(2)}, u32[]{:S(2)}) collective-permute-start(bf16[64,256]{1,0:T(8,128)(2,1)} %bitcast.8), channel_id=1, source_target_pairs={{0,1},{1,0},{2,3},{3,2},{4,5},{5,4},{6,7},{7,6},{8,9},{9,8},{10,11... | collective-permute-start | bytes 98312 | tf_op jit(solution)/shard_map/ppermute | solution.py:251
  3.5 5.3 %collective-permute-start.3 = (bf16[4,64,128]{2,1,0:T(8,128)(2,1)S(1)}, bf16[4,64,128]{2,1,0:T(8,128)(2,1)S(1)}, u32[]{:S(2)}, u32[]{:S(2)}) collective-permute-start(bf16[4,64,128]{2,1,0:T(8,128)(2,1)S(1)} %get-tuple-element.23), channel_id=1, source_target_pairs={{0,2},{1,3},{2,0},{3,1},{4,6},{5,7},{6,4},{7,5},{8,10},{9,11},{10,... | collective-permute-start | bytes 196616 | tf_op jit(solution)/shard_map/ppermute | solution.py:251
  6.5 7.1 %collective-permute-start.2 = (bf16[4,128,128]{2,1,0:T(8,128)(2,1)S(1)}, bf16[4,128,128]{2,1,0:T(8,128)(2,1)S(1)}, u32[]{:S(2)}, u32[]{:S(2)}) collective-permute-start(bf16[4,128,128]{2,1,0:T(8,128)(2,1)S(1)} %get-tuple-element.20.x_mine), channel_id=1, source_target_pairs={{0,16},{1,17},{2,18},{3,19},{4,20},{5,21},{6,22},{7,23},{8,24},{9,... | collective-permute-start | bytes 393224 | tf_op jit(solution)/shard_map/ppermute | solution.py:251
  8.9 19.4 %copy-start = (bf16[2,256,256]{2,1,0:T(8,128)(2,1)S(1)}, bf16[2,256,256]{2,1,0:T(8,128)(2,1)}, u32[]{:S(2)}) copy-start(bf16[2,256,256]{2,1,0:T(8,128)(2,1)} %w_second.3) | copy-start | bytes 786436
  8.9 7.2 %collective-permute-start.6 = (bf16[336,128]{1,0:T(8,128)(2,1)S(1)}, bf16[336,128]{1,0:T(8,128)(2,1)S(1)}, u32[]{:S(2)}, u32[]{:S(2)}) collective-permute-start(bf16[336,128]{1,0:T(8,128)(2,1)S(1)} %sum_plane.1.refs_0_), channel_id=1, source_target_pairs={{0,12},{1,13},{2,14},{3,15},{4,8},{5,9},{6,10},{7,11},{8,4},{9,5},... | collective-permute-start | bytes 258056 | tf_op jit(solution)/shard_map/ppermute | solution.py:251
  13.0 6.5 %collective-permute-start.5 = (bf16[336,128]{1,0:T(8,128)(2,1)S(1)}, bf16[336,128]{1,0:T(8,128)(2,1)S(1)}, u32[]{:S(2)}, u32[]{:S(2)}) collective-permute-start(bf16[336,128]{1,0:T(8,128)(2,1)S(1)} %sum_plane.1.refs_0_), channel_id=1, source_target_pairs={{0,8},{1,9},{2,10},{3,11},{4,12},{5,13},{6,14},{7,15},{8,0},{9,1},... | collective-permute-start | bytes 258056 | tf_op jit(solution)/shard_map/ppermute | solution.py:251
  13.0 6.5 %collective-permute-start.4 = (bf16[336,128]{1,0:T(8,128)(2,1)S(1)}, bf16[336,128]{1,0:T(8,128)(2,1)S(1)}, u32[]{:S(2)}, u32[]{:S(2)}) collective-permute-start(bf16[336,128]{1,0:T(8,128)(2,1)S(1)} %sum_plane.1.refs_0_), channel_id=1, source_target_pairs={{0,4},{1,5},{2,6},{3,7},{4,0},{5,1},{6,2},{7,3},{8,12},{9,13},{10,... | collective-permute-start | bytes 258056 | tf_op jit(solution)/shard_map/ppermute | solution.py:251
  19.5 6.6 %collective-permute-start.9 = (bf16[528,128]{1,0:T(8,128)(2,1)S(1)}, bf16[528,128]{1,0:T(8,128)(2,1)S(1)}, u32[]{:S(2)}, u32[]{:S(2)}) collective-permute-start(bf16[528,128]{1,0:T(8,128)(2,1)S(1)} %get-tuple-element.24.plane_0), channel_id=1, source_target_pairs={{0,18},{1,19},{2,16},{3,17},{4,22},{5,23},{6,20},{7,21},{8,26},{9,... | collective-permute-start | bytes 405512 | tf_op jit(solution)/shard_map/ppermute | solution.py:251
  22.0 6.3 %collective-permute-start.8 = (bf16[528,128]{1,0:T(8,128)(2,1)S(1)}, bf16[528,128]{1,0:T(8,128)(2,1)S(1)}, u32[]{:S(2)}, u32[]{:S(2)}) collective-permute-start(bf16[528,128]{1,0:T(8,128)(2,1)S(1)} %get-tuple-element.24.plane_0), channel_id=1, source_target_pairs={{0,2},{1,3},{2,0},{3,1},{4,6},{5,7},{6,4},{7,5},{8,10},{9,11},{10,... | collective-permute-start | bytes 405512 | tf_op jit(solution)/shard_map/ppermute | solution.py:251
  22.5 5.8 %collective-permute-start.7 = (bf16[528,128]{1,0:T(8,128)(2,1)S(1)}, bf16[528,128]{1,0:T(8,128)(2,1)S(1)}, u32[]{:S(2)}, u32[]{:S(2)}) collective-permute-start(bf16[528,128]{1,0:T(8,128)(2,1)S(1)} %get-tuple-element.24.plane_0), channel_id=1, source_target_pairs={{0,16},{1,17},{2,18},{3,19},{4,20},{5,21},{6,22},{7,23},{8,24},{9,... | collective-permute-start | bytes 405512 | tf_op jit(solution)/shard_map/ppermute | solution.py:251
  29.8 1.6 %collective-permute-start.10 = (bf16[576,256]{1,0:T(8,128)(2,1)S(1)}, bf16[576,256]{1,0:T(8,128)(2,1)S(1)}, u32[]{:S(2)}, u32[]{:S(2)}) collective-permute-start(bf16[576,256]{1,0:T(8,128)(2,1)S(1)} %get-tuple-element.27.mine), channel_id=1, source_target_pairs={{0,1},{1,0},{2,3},{3,2},{4,5},{5,4},{6,7},{7,6},{8,9},{9,8},{10,11... | collective-permute-start | bytes 884744 | tf_op jit(solution)/shard_map/ppermute | solution.py:251

commit v8 on v7

--- a/solution.py
+++ b/solution.py
@@ -95,7 +95,7 @@
 
 
 def sum_line_kernel(after, *refs):
-    parts, (exact, message) = refs[:-2], refs[-2:]
+    parts, (exact, message) = (refs[0], refs[1], refs[3], refs[2]), refs[-2:]
     my_z = lax.axis_index("feat") // 4
     line, width = exact.shape[0], exact.shape[1]
     rows = line * width
@@ -286,7 +286,7 @@
         [(block, F32), ((2 * line * width + INTS, LANES), BF16)],
         [ANY] + [VMEM] * line,
         name="sum_line",
-    )(x_peer, message, *[swap(n_feat, message, 4 * z) for z in range(1, line)])
+    )(x_peer, message, *[swap(n_feat, message, 4 * z) for z in (1, 3, 2)])
     plane = [swap(n_feat, message, r) for r in (n_feat + 2, 2, n_feat)]
     plane = [message, *plane[::-1]]
 

time: 32.4 us -> 31.5 us (0.972); the launches traced: 32.3 us -> 31 us
  waiting for transfers between devices: 12.6 us -> 11.4 us
    ppermute x11, waiting for transfers between devices: 12.6 us -> 11.4 us  [swap(): lax.ppermute(value, AXES, [(d, d ^ relative) for d in range(2 * n_feat)])]
  transfers between devices with their start and end apart: 11 -> 11, of which waited for: 6 -> 7; matrix products, arithmetic and copies ran while one was open for 0% -> 0% of each run, Pallas kernels for 8% -> 8%
where the time goes in v8:
time: 31.5 us; the launch traced here: 31 us
  starting transfers between devices  13.4 us (43%)
  waiting for transfers between devices  11.4 us (36%)
  Pallas kernels  5.51 us (17%)
  between operations  0.7 us (2%)
    ppermute x11, starting transfers between devices, swap(): lax.ppermute(value, AXES, [(d, d ^ relative) for d in range(2 * n_feat)])  13.4 us
    ppermute x11, waiting for transfers between devices, swap(): lax.ppermute(value, AXES, [(d, d ^ relative) for d in range(2 * n_feat)])  11.4 us
    pallas_call x1, Pallas kernels, pair_body(): call(count_kernel, [((sources, rows), BF16), ((OWN, sources), BF16), ((wi...  1.69 us
    pallas_call x1, Pallas kernels, pair_body(): call(functools.partial(last_kernel, n_feat), [((OWN, width), F32), ((2 *...  1.44 us
    pallas_call x1, Pallas kernels, pair_body(): call(functools.partial(out_kernel, n_feat), [((OWN, HID), BF16)], [VMEM]...  0.9 us
    pallas_call x1, Pallas kernels, pair_body(): call(add_kernel, [((2, HID, HID), F32), ((width, HID), F32)], [VMEM] * 3,...  0.87 us
  transfers between devices with their start and end apart: 11, of which 7 were waited for; matrix products, arithmetic and copies ran while one was open for 0% of the time, Pallas kernels for 8%

profile of v8, /device:TPU:0, one launch (start us, length us, event | category | flops | bytes accessed | tf_op | source)
XLA Modules:
  0.0 31.0 jit_solution(1088603550385993215)
XLA Ops:
  0.6 0.5 %collective-permute-start = (bf16[32,1024]{1,0:T(8,128)(2,1)}, bf16[32,1024]{1,0:T(8,128)(2,1)S(1)}, u32[]{:S(2)}, u32[]{:S(2)}) collective-permute-start(bf16[32,1024]{1,0:T(8,128)(2,1)} %bitcast.5), channel_id=1, source_target_pairs={{0,1},{1,0},{2,3},{3,2},{4,5},{5,4},{6,7},{7,6},{8,9},{9,8},{10,11... | collective-permute-start | bytes 196616 | tf_op jit(solution)/shard_map/ppermute | solution.py:251
  1.1 0.1 collective-permute-start.1
  1.2 1.7 %count.1 = (bf16[1024,512]{1,0:T(8,128)(2,1)S(1)}, bf16[32,1024]{1,0:T(8,128)(2,1)S(1)}, bf16[64,256]{1,0:T(8,128)(2,1)S(1)}, bf16[80,128]{1,0:T(8,128)(2,1)S(1)}) custom-call(bf16[32,1024]{1,0:T(8,128)(2,1)} %bitcast.6, s32[15,512]{1,0:T(8,128)} %bitcast.7, bf16[64,256]{1,0:T(8,128)(2,1)} %bitcast.9, bf16[32,256]{1,0:T(8,128)(2,1)} %cot_hbm.1, ...), custom_call_target="tpu_custom_call" | custom-call | tf_op jit(solution)/shard_map/count/pallas_call | solution.py:262
  2.9 0.0 collective-permute-done.1.w_core
  2.9 0.0 collective-permute-done.feat_core
  2.9 0.6 %first.1 = (bf16[4,128,128]{2,1,0:T(8,128)(2,1)S(1)}, f32[4,64,128]{2,1,0:T(8,128)S(1)}, bf16[4,64,128]{2,1,0:T(8,128)(2,1)S(1)}) custom-call(bf16[1024,512]{1,0:T(8,128)(2,1)S(1)} %get-tuple-element.17.counts, bf16[32,1024]{1,0:T(8,128)(2,1)S(1)} %get-tuple-element.18.feat_mine, bf16[64,256]{1,0:T(8,128)(2,1)S(1)} %get-tuple-element.19.w_mine, ...), custom_call_target="tpu_custom_call" | custom-call | tf_op jit(solution)/shard_map/first/pallas_call | solution.py:270
  3.5 3.0 %collective-permute-start.3 = (bf16[4,64,128]{2,1,0:T(8,128)(2,1)S(1)}, bf16[4,64,128]{2,1,0:T(8,128)(2,1)S(1)}, u32[]{:S(2)}, u32[]{:S(2)}) collective-permute-start(bf16[4,64,128]{2,1,0:T(8,128)(2,1)S(1)} %get-tuple-element.23), channel_id=1, source_target_pairs={{0,2},{1,3},{2,0},{3,1},{4,6},{5,7},{6,4},{7,5},{8,10},{9,11},{10,... | collective-permute-start | bytes 196616 | tf_op jit(solution)/shard_map/ppermute | solution.py:251
  6.5 1.5 %collective-permute-start.2 = (bf16[4,128,128]{2,1,0:T(8,128)(2,1)S(1)}, bf16[4,128,128]{2,1,0:T(8,128)(2,1)S(1)}, u32[]{:S(2)}, u32[]{:S(2)}) collective-permute-start(bf16[4,128,128]{2,1,0:T(8,128)(2,1)S(1)} %get-tuple-element.20.x_mine), channel_id=1, source_target_pairs={{0,16},{1,17},{2,18},{3,19},{4,20},{5,21},{6,22},{7,23},{8,24},{9,... | collective-permute-start | bytes 393224 | tf_op jit(solution)/shard_map/ppermute | solution.py:251
  8.0 0.8 %collective-permute-done.3.received = bf16[4,64,128]{2,1,0:T(8,128)(2,1)S(1)} collective-permute-done((bf16[4,64,128]{2,1,0:T(8,128)(2,1)S(1)}, bf16[4,64,128]{2,1,0:T(8,128)(2,1)S(1)}, u32[]{:S(2)}, u32[]{:S(2)}) %collective-permute-start.3) | collective-permute-done | bytes 65568 | tf_op jit(solution)/shard_map/ppermute | solution.py:251
  8.9 0.0 copy-start
  8.9 3.1 %collective-permute-start.6 = (bf16[336,128]{1,0:T(8,128)(2,1)S(1)}, bf16[336,128]{1,0:T(8,128)(2,1)S(1)}, u32[]{:S(2)}, u32[]{:S(2)}) collective-permute-start(bf16[336,128]{1,0:T(8,128)(2,1)S(1)} %sum_plane.1.refs_0_), channel_id=1, source_target_pairs={{0,8},{1,9},{2,10},{3,11},{4,12},{5,13},{6,14},{7,15},{8,0},{9,1},... | collective-permute-start | bytes 258056 | tf_op jit(solution)/shard_map/ppermute | solution.py:251
  11.9 1.3 %collective-permute-start.5 = (bf16[336,128]{1,0:T(8,128)(2,1)S(1)}, bf16[336,128]{1,0:T(8,128)(2,1)S(1)}, u32[]{:S(2)}, u32[]{:S(2)}) collective-permute-start(bf16[336,128]{1,0:T(8,128)(2,1)S(1)} %sum_plane.1.refs_0_), channel_id=1, source_target_pairs={{0,12},{1,13},{2,14},{3,15},{4,8},{5,9},{6,10},{7,11},{8,4},{9,5},... | collective-permute-start | bytes 258056 | tf_op jit(solution)/shard_map/ppermute | solution.py:251
  13.3 0.2 collective-permute-start.4
  13.5 0.0 collective-permute-done.2.after.x_peer
  13.5 3.7 %collective-permute-done.6.refs_3_ = bf16[336,128]{1,0:T(8,128)(2,1)S(1)} collective-permute-done((bf16[336,128]{1,0:T(8,128)(2,1)S(1)}, bf16[336,128]{1,0:T(8,128)(2,1)S(1)}, u32[]{:S(2)}, u32[]{:S(2)}) %collective-permute-start.6) | collective-permute-done | bytes 86048 | tf_op jit(solution)/shard_map/ppermute | solution.py:251
  17.2 1.5 %collective-permute-done.5.refs_2_ = bf16[336,128]{1,0:T(8,128)(2,1)S(1)} collective-permute-done((bf16[336,128]{1,0:T(8,128)(2,1)S(1)}, bf16[336,128]{1,0:T(8,128)(2,1)S(1)}, u32[]{:S(2)}, u32[]{:S(2)}) %collective-permute-start.5) | collective-permute-done | bytes 86048 | tf_op jit(solution)/shard_map/ppermute | solution.py:251
  18.7 0.1 collective-permute-done.4.refs_1_
  18.9 2.5 %collective-permute-start.9 = (bf16[528,128]{1,0:T(8,128)(2,1)S(1)}, bf16[528,128]{1,0:T(8,128)(2,1)S(1)}, u32[]{:S(2)}, u32[]{:S(2)}) collective-permute-start(bf16[528,128]{1,0:T(8,128)(2,1)S(1)} %get-tuple-element.24.plane_0), channel_id=1, source_target_pairs={{0,18},{1,19},{2,16},{3,17},{4,22},{5,23},{6,20},{7,21},{8,26},{9,... | collective-permute-start | bytes 405512 | tf_op jit(solution)/shard_map/ppermute | solution.py:251
  21.4 0.5 %collective-permute-start.8 = (bf16[528,128]{1,0:T(8,128)(2,1)S(1)}, bf16[528,128]{1,0:T(8,128)(2,1)S(1)}, u32[]{:S(2)}, u32[]{:S(2)}) collective-permute-start(bf16[528,128]{1,0:T(8,128)(2,1)S(1)} %get-tuple-element.24.plane_0), channel_id=1, source_target_pairs={{0,2},{1,3},{2,0},{3,1},{4,6},{5,7},{6,4},{7,5},{8,10},{9,11},{10,... | collective-permute-start | bytes 405512 | tf_op jit(solution)/shard_map/ppermute | solution.py:251
  22.0 0.5 %collective-permute-start.7 = (bf16[528,128]{1,0:T(8,128)(2,1)S(1)}, bf16[528,128]{1,0:T(8,128)(2,1)S(1)}, u32[]{:S(2)}, u32[]{:S(2)}) collective-permute-start(bf16[528,128]{1,0:T(8,128)(2,1)S(1)} %get-tuple-element.24.plane_0), channel_id=1, source_target_pairs={{0,16},{1,17},{2,18},{3,19},{4,20},{5,21},{6,22},{7,23},{8,24},{9,... | collective-permute-start | bytes 405512 | tf_op jit(solution)/shard_map/ppermute | solution.py:251
  22.5 3.1 %collective-permute-done.9.plane_3 = bf16[528,128]{1,0:T(8,128)(2,1)S(1)} collective-permute-done((bf16[528,128]{1,0:T(8,128)(2,1)S(1)}, bf16[528,128]{1,0:T(8,128)(2,1)S(1)}, u32[]{:S(2)}, u32[]{:S(2)}) %collective-permute-start.9) | collective-permute-done | bytes 135200 | tf_op jit(solution)/shard_map/ppermute | solution.py:251
  25.6 1.4 %collective-permute-done.8.plane_2 = bf16[528,128]{1,0:T(8,128)(2,1)S(1)} collective-permute-done((bf16[528,128]{1,0:T(8,128)(2,1)S(1)}, bf16[528,128]{1,0:T(8,128)(2,1)S(1)}, u32[]{:S(2)}, u32[]{:S(2)}) %collective-permute-start.8) | collective-permute-done | bytes 135200 | tf_op jit(solution)/shard_map/ppermute | solution.py:251
  27.0 0.0 collective-permute-done.7.plane_1.peer
  27.0 0.0 copy-done
  27.0 1.4 %last.1 = (f32[32,64]{1,0:T(8,128)S(1)}, bf16[576,256]{1,0:T(8,128)(2,1)S(1)}, f32[64,256]{1,0:T(8,128)S(1)}) custom-call(bf16[528,128]{1,0:T(8,128)(2,1)S(1)} %get-tuple-element.24.plane_0, bf16[528,128]{1,0:T(8,128)(2,1)S(1)} %collective-permute-done.7.plane_1.peer, bf16[528,128]{1,0:T(8,128)(2,1)S(1)} %collective-permute-done.8.plane_2, ...), custom_call_target="tpu_custom_call" | custom-call | tf_op jit(solution)/shard_map/last/pallas_call | solution.py:294
  28.5 0.1 collective-permute-start.10
  28.5 0.9 %out.1 = bf16[32,256]{1,0:T(8,128)(2,1)} custom-call(bf16[528,128]{1,0:T(8,128)(2,1)S(1)} %collective-permute-done.7.plane_1.peer, f32[4,64,128]{2,1,0:T(8,128)S(1)} %get-tuple-element.25.exact, f32[32,64]{1,0:T(8,128)S(1)} %get-tuple-element.26.own_counts, bf16[2,256,256]{2,1,0:T(8,128)(2,1)S(1)} %copy-done), custom_call_target="tpu_custom_call" | custom-call | tf_op jit(solution)/shard_map/out/pallas_call | solution.py:310
  29.4 0.7 %collective-permute-done.10.theirs = bf16[576,256]{1,0:T(8,128)(2,1)S(1)} collective-permute-done((bf16[576,256]{1,0:T(8,128)(2,1)S(1)}, bf16[576,256]{1,0:T(8,128)(2,1)S(1)}, u32[]{:S(2)}, u32[]{:S(2)}) %collective-permute-start.10) | collective-permute-done | bytes 294944 | tf_op jit(solution)/shard_map/ppermute | solution.py:251
  30.1 0.9 %add.1 = (f32[2,256,256]{2,1,0:T(8,128)}, f32[64,256]{1,0:T(8,128)}) custom-call(bf16[576,256]{1,0:T(8,128)(2,1)S(1)} %get-tuple-element.27.mine, bf16[576,256]{1,0:T(8,128)(2,1)S(1)} %collective-permute-done.10.theirs, f32[64,256]{1,0:T(8,128)S(1)} %get-tuple-element.28.kept), custom_call_target="tpu_custom_call" | custom-call | tf_op jit(solution)/shard_map/add/pallas_call | solution.py:317
  (2 shorter events, 0.1 us)
Async XLA Ops:
  0.6 2.3 %collective-permute-start = (bf16[32,1024]{1,0:T(8,128)(2,1)}, bf16[32,1024]{1,0:T(8,128)(2,1)S(1)}, u32[]{:S(2)}, u32[]{:S(2)}) collective-permute-start(bf16[32,1024]{1,0:T(8,128)(2,1)} %bitcast.5), channel_id=1, source_target_pairs={{0,1},{1,0},{2,3},{3,2},{4,5},{5,4},{6,7},{7,6},{8,9},{9,8},{10,11... | collective-permute-start | bytes 196616 | tf_op jit(solution)/shard_map/ppermute | solution.py:251
  1.1 1.8 %collective-permute-start.1 = (bf16[64,256]{1,0:T(8,128)(2,1)}, bf16[64,256]{1,0:T(8,128)(2,1)S(1)}, u32[]{:S(2)}, u32[]{:S(2)}) collective-permute-start(bf16[64,256]{1,0:T(8,128)(2,1)} %bitcast.8), channel_id=1, source_target_pairs={{0,1},{1,0},{2,3},{3,2},{4,5},{5,4},{6,7},{7,6},{8,9},{9,8},{10,11... | collective-permute-start | bytes 98312 | tf_op jit(solution)/shard_map/ppermute | solution.py:251
  3.5 5.3 %collective-permute-start.3 = (bf16[4,64,128]{2,1,0:T(8,128)(2,1)S(1)}, bf16[4,64,128]{2,1,0:T(8,128)(2,1)S(1)}, u32[]{:S(2)}, u32[]{:S(2)}) collective-permute-start(bf16[4,64,128]{2,1,0:T(8,128)(2,1)S(1)} %get-tuple-element.23), channel_id=1, source_target_pairs={{0,2},{1,3},{2,0},{3,1},{4,6},{5,7},{6,4},{7,5},{8,10},{9,11},{10,... | collective-permute-start | bytes 196616 | tf_op jit(solution)/shard_map/ppermute | solution.py:251
  6.5 7.0 %collective-permute-start.2 = (bf16[4,128,128]{2,1,0:T(8,128)(2,1)S(1)}, bf16[4,128,128]{2,1,0:T(8,128)(2,1)S(1)}, u32[]{:S(2)}, u32[]{:S(2)}) collective-permute-start(bf16[4,128,128]{2,1,0:T(8,128)(2,1)S(1)} %get-tuple-element.20.x_mine), channel_id=1, source_target_pairs={{0,16},{1,17},{2,18},{3,19},{4,20},{5,21},{6,22},{7,23},{8,24},{9,... | collective-permute-start | bytes 393224 | tf_op jit(solution)/shard_map/ppermute | solution.py:251
  8.9 18.1 %copy-start = (bf16[2,256,256]{2,1,0:T(8,128)(2,1)S(1)}, bf16[2,256,256]{2,1,0:T(8,128)(2,1)}, u32[]{:S(2)}) copy-start(bf16[2,256,256]{2,1,0:T(8,128)(2,1)} %w_second.3) | copy-start | bytes 786436
  8.9 8.3 %collective-permute-start.6 = (bf16[336,128]{1,0:T(8,128)(2,1)S(1)}, bf16[336,128]{1,0:T(8,128)(2,1)S(1)}, u32[]{:S(2)}, u32[]{:S(2)}) collective-permute-start(bf16[336,128]{1,0:T(8,128)(2,1)S(1)} %sum_plane.1.refs_0_), channel_id=1, source_target_pairs={{0,8},{1,9},{2,10},{3,11},{4,12},{5,13},{6,14},{7,15},{8,0},{9,1},... | collective-permute-start | bytes 258056 | tf_op jit(solution)/shard_map/ppermute | solution.py:251
  11.9 6.8 %collective-permute-start.5 = (bf16[336,128]{1,0:T(8,128)(2,1)S(1)}, bf16[336,128]{1,0:T(8,128)(2,1)S(1)}, u32[]{:S(2)}, u32[]{:S(2)}) collective-permute-start(bf16[336,128]{1,0:T(8,128)(2,1)S(1)} %sum_plane.1.refs_0_), channel_id=1, source_target_pairs={{0,12},{1,13},{2,14},{3,15},{4,8},{5,9},{6,10},{7,11},{8,4},{9,5},... | collective-permute-start | bytes 258056 | tf_op jit(solution)/shard_map/ppermute | solution.py:251
  13.3 5.6 %collective-permute-start.4 = (bf16[336,128]{1,0:T(8,128)(2,1)S(1)}, bf16[336,128]{1,0:T(8,128)(2,1)S(1)}, u32[]{:S(2)}, u32[]{:S(2)}) collective-permute-start(bf16[336,128]{1,0:T(8,128)(2,1)S(1)} %sum_plane.1.refs_0_), channel_id=1, source_target_pairs={{0,4},{1,5},{2,6},{3,7},{4,0},{5,1},{6,2},{7,3},{8,12},{9,13},{10,... | collective-permute-start | bytes 258056 | tf_op jit(solution)/shard_map/ppermute | solution.py:251
  18.9 6.7 %collective-permute-start.9 = (bf16[528,128]{1,0:T(8,128)(2,1)S(1)}, bf16[528,128]{1,0:T(8,128)(2,1)S(1)}, u32[]{:S(2)}, u32[]{:S(2)}) collective-permute-start(bf16[528,128]{1,0:T(8,128)(2,1)S(1)} %get-tuple-element.24.plane_0), channel_id=1, source_target_pairs={{0,18},{1,19},{2,16},{3,17},{4,22},{5,23},{6,20},{7,21},{8,26},{9,... | collective-permute-start | bytes 405512 | tf_op jit(solution)/shard_map/ppermute | solution.py:251
  21.4 5.6 %collective-permute-start.8 = (bf16[528,128]{1,0:T(8,128)(2,1)S(1)}, bf16[528,128]{1,0:T(8,128)(2,1)S(1)}, u32[]{:S(2)}, u32[]{:S(2)}) collective-permute-start(bf16[528,128]{1,0:T(8,128)(2,1)S(1)} %get-tuple-element.24.plane_0), channel_id=1, source_target_pairs={{0,2},{1,3},{2,0},{3,1},{4,6},{5,7},{6,4},{7,5},{8,10},{9,11},{10,... | collective-permute-start | bytes 405512 | tf_op jit(solution)/shard_map/ppermute | solution.py:251
  22.0 5.1 %collective-permute-start.7 = (bf16[528,128]{1,0:T(8,128)(2,1)S(1)}, bf16[528,128]{1,0:T(8,128)(2,1)S(1)}, u32[]{:S(2)}, u32[]{:S(2)}) collective-permute-start(bf16[528,128]{1,0:T(8,128)(2,1)S(1)} %get-tuple-element.24.plane_0), channel_id=1, source_target_pairs={{0,16},{1,17},{2,18},{3,19},{4,20},{5,21},{6,22},{7,23},{8,24},{9,... | collective-permute-start | bytes 405512 | tf_op jit(solution)/shard_map/ppermute | solution.py:251
  28.5 1.6 %collective-permute-start.10 = (bf16[576,256]{1,0:T(8,128)(2,1)S(1)}, bf16[576,256]{1,0:T(8,128)(2,1)S(1)}, u32[]{:S(2)}, u32[]{:S(2)}) collective-permute-start(bf16[576,256]{1,0:T(8,128)(2,1)S(1)} %get-tuple-element.27.mine), channel_id=1, source_target_pairs={{0,1},{1,0},{2,3},{3,2},{4,5},{5,4},{6,7},{7,6},{8,9},{9,8},{10,11... | collective-permute-start | bytes 884744 | tf_op jit(solution)/shard_map/ppermute | solution.py:251
